TPU v7x, 32 devices: a whole 2x2x4 slice. The times are simulated.
32 devices in a mesh: grp: 4 (over x, core), tile: 8 (over z, y).
Axes of the slice: x: 2, y: 2, z: 4, core: 2. Of those that a mesh axis runs over, the one named last changes fastest.
Arguments:
- air_state: float32 [256, 128, 768], P('tile', 'grp'), may hold values from -400 to 400
- cotangent: float32 [256, 128, 768], P('tile', 'grp'), may hold values from -0.0625 to 0.0625
- cost_count: int32 [256, 128], P('tile', 'grp'), may hold values from 1 to 2, as said below
- assignment: int32 [256, 128], P('tile', 'grp'), may hold values from 0 to 1023, as said below
- orientation: int32 [8, 4], P('tile', 'grp'), may hold values from 0 to 3
- weight_in: bfloat16 [768, 512], replicated, may hold values from -0.21875 to 0.21875
- weight_out: bfloat16 [512, 768], replicated, may hold values from -0.25 to 0.25
Outputs:
- tendency: float32 [32768, 768], P(('grp', 'tile'))
- weight_in_grad: float32 [393216], P(('grp', 'tile'))
- weight_out_grad: float32 [393216], P(('grp', 'tile'))
Inputs may be any that keep to these rules, and one draw needn't show every extreme that they name: `cost_count`: every batch receives exactly 256 columns of cost 2; one device holds at most 512 of them, and some device exactly that many. `assignment`: on every device the values form a permutation of 0 to 1023.
All inputs are finite; a program needn't handle non-finite values.
Results may differ from a plain program's by a relative error of at most 0.0035.
Values sent between devices are 32-bit elements; how exact they have to be, the bound alone decides.
No kernel may reach another device: no remote copies, remote signals or barrier semaphores. Data moves between devices by JAX's collectives and lax.ppermute only.
A program may use at most 128 MiB of HBM per device.

v0:
```python
import jax
import jax.numpy as jnp
from jax import lax
from jax.sharding import PartitionSpec as P

V = 8
L = 96
DSTEPS = 2
F = 768
COLS = 1024
K2 = 256


tau_rate = 0.5
courant = 0.1
eps_norm = 1e-06


def extended(block, sides, width):
    for axis, dim in sides:
        count = lax.axis_size(axis)
        forward = [(i, i + 1) for i in range(count - 1)]
        forward.append((count - 1, 0))
        backward = [(target, source) for source, target in forward]
        low = lax.ppermute(
            lax.slice_in_dim(block, block.shape[dim] - width, None, axis=dim), axis, forward
        )
        high = lax.ppermute(lax.slice_in_dim(block, 0, width, axis=dim), axis, backward)
        block = jnp.concatenate([low, block, high], axis=dim)
    return block


def turn_frame(field_in, quarter_turns):

    def make_turn(turn_count):

        def apply_turn(block_in):
            rotated = jnp.rot90(block_in, turn_count, axes=(0, 1))
            east_wind = rotated[:, :, 0:L]
            north_wind = rotated[:, :, L : 2 * L]
            for repeat in range(turn_count):
                east_wind, north_wind = (-north_wind, east_wind)
            return jnp.concatenate([east_wind, north_wind, rotated[:, :, 2 * L :]], axis=2)

        return apply_turn

    return lax.switch(
        quarter_turns, [make_turn(0), make_turn(1), make_turn(2), make_turn(3)], field_in
    )


def advance(padded):
    east_wind = padded[:, :, 0:L]
    north_wind = padded[:, :, L : 2 * L]
    face_x = jnp.tile(0.5 * (east_wind[:-1, 1:-1] + east_wind[1:, 1:-1]), (1, 1, V))
    flux_x = (
        jnp.maximum(face_x, 0.0) * padded[:-1, 1:-1] + jnp.minimum(face_x, 0.0) * padded[1:, 1:-1]
    )
    face_y = jnp.tile(0.5 * (north_wind[1:-1, :-1] + north_wind[1:-1, 1:]), (1, 1, V))
    flux_y = (
        jnp.maximum(face_y, 0.0) * padded[1:-1, :-1] + jnp.minimum(face_y, 0.0) * padded[1:-1, 1:]
    )
    return padded[1:-1, 1:-1] - courant * (
        flux_x[1:] - flux_x[:-1] + (flux_y[:, 1:] - flux_y[:, :-1])
    )


def forward_rows(rows, weight_in, weight_out):
    inv_rms = lax.rsqrt(jnp.mean(rows * rows, axis=1, keepdims=True) + eps_norm)
    unit_rows = rows * inv_rms
    normed = unit_rows.astype(jnp.bfloat16)
    preact = jnp.dot(normed, weight_in, preferred_element_type=jnp.float32)
    hidden = jax.nn.silu(preact).astype(jnp.bfloat16)
    output = tau_rate * jnp.dot(hidden, weight_out, preferred_element_type=jnp.float32)
    return (output, normed, preact, hidden, inv_rms, unit_rows)


def backward_rows(grad_rows, saved, weight_in, weight_out):
    normed, preact, hidden, inv_rms, unit_rows = saved
    err_out = (tau_rate * grad_rows).astype(jnp.bfloat16)
    back_prop = jnp.dot(err_out, weight_out.T, preferred_element_type=jnp.float32)
    logistic = jax.nn.sigmoid(preact)
    err_in = (back_prop * logistic * (1.0 + preact * (1.0 - logistic))).astype(jnp.bfloat16)
    grad_out = jnp.dot(hidden.T, err_out, preferred_element_type=jnp.float32)
    grad_in = jnp.dot(normed.T, err_in, preferred_element_type=jnp.float32)
    d_normed = jnp.dot(err_in, weight_in.T, preferred_element_type=jnp.float32)
    input_grad = inv_rms * (
        d_normed - unit_rows * jnp.mean(d_normed * unit_rows, axis=1, keepdims=True)
    )
    return (grad_out, grad_in, input_grad)


def finish_physics(start_rows, cot_rows, picked, keep_mask, first, weight_in, weight_out):
    h_one, normed, preact, hidden = first
    x_one = start_rows + h_one
    level_two = forward_rows(x_one, weight_in, weight_out)
    x_two = x_one + level_two[0]
    level_three = forward_rows(x_two[picked], weight_in, weight_out)
    weight_col = keep_mask[:, None]
    tendency = (
        h_one + level_two[0] + jnp.zeros_like(h_one).at[picked].add(level_three[0] * weight_col)
    )
    out_three, in_three, back_three = backward_rows(
        cot_rows[picked] * weight_col, level_three[1:], weight_in, weight_out
    )
    carried = jnp.zeros_like(start_rows).at[picked].add(back_three * weight_col)
    g_two = cot_rows + carried
    out_two, in_two, back_two = backward_rows(g_two, level_two[1:], weight_in, weight_out)
    g_one = g_two + back_two
    err_out = (tau_rate * g_one).astype(jnp.bfloat16)
    grad_out = out_three + out_two + jnp.dot(hidden.T, err_out, preferred_element_type=jnp.float32)
    summed_out = lax.psum_scatter(
        grad_out.reshape(-1), ("grp", "tile"), scatter_dimension=0, tiled=True
    )
    back_prop = jnp.dot(err_out, weight_out.T, preferred_element_type=jnp.float32)
    logistic = jax.nn.sigmoid(preact)
    err_in = (back_prop * logistic * (1.0 + preact * (1.0 - logistic))).astype(jnp.bfloat16)
    grad_in = in_three + in_two + jnp.dot(normed.T, err_in, preferred_element_type=jnp.float32)
    summed_in = lax.psum_scatter(
        grad_in.reshape(-1), ("grp", "tile"), scatter_dimension=0, tiled=True
    )
    return (tendency, summed_in, summed_out)


def per_device(air_state, cotangent, cost_count, assignment, orientation, weight_in, weight_out):
    quarter_turns = orientation[0, 0]
    band_field = turn_frame(air_state, quarter_turns)
    for repeat in range(DSTEPS):
        padded = extended(band_field, (("grp", 1), ("tile", 0)), 1)
        band_field = advance(padded)
    columns = turn_frame(band_field, (4 - quarter_turns) % 4).reshape(COLS, F)
    cot_rows = cotangent.reshape(COLS, F)
    cost_rows = cost_count.reshape(COLS)
    destination = assignment.reshape(COLS)
    tile_count = lax.axis_size("grp") * lax.axis_size("tile")
    pair_size = COLS // tile_count
    picked = jnp.nonzero(cost_rows == 2, size=2 * K2, fill_value=0)[0].astype(jnp.int32)
    keep_mask = (jnp.arange(2 * K2) < jnp.sum(cost_rows == 2)).astype(jnp.float32)
    first = forward_rows(columns, weight_in, weight_out)[:4]
    local_tend, summed_in, summed_out = finish_physics(
        columns, cot_rows, picked, keep_mask, first, weight_in, weight_out
    )
    outgoing = (
        jnp.zeros_like(local_tend).at[destination].set(local_tend).reshape(tile_count, pair_size, F)
    )
    tendency = lax.all_to_all(
        outgoing, ("grp", "tile"), split_axis=0, concat_axis=0, tiled=True
    ).reshape(COLS, F)
    return (tendency, summed_in, summed_out)


def solution(mesh):
    in_specs = (
        P("tile", "grp", None),
        P("tile", "grp", None),
        P("tile", "grp"),
        P("tile", "grp"),
        P("tile", "grp"),
        P(),
        P(),
    )
    out_specs = (P(("grp", "tile"), None), P(("grp", "tile")), P(("grp", "tile")))
    return jax.shard_map(
        per_device, mesh=mesh, in_specs=in_specs, out_specs=out_specs, check_vma=False
    )
```

profile of v0, /device:TPU:0, one launch (start us, length us, event | category | flops | bytes accessed | tf_op | source)
XLA Modules:
  0.0 493.3 jit_solution(4810372516702799939)
XLA Ops:
  7.2 4.0 copy.202
  11.2 1.6 copy.203
  13.6 7.8 %conditional.2 = (f32[32,32,768]{2,1,0:T(8,128)}) conditional(s32[]{:T(128)} %bitcast.10, f32[32,32,768]{2,1,0:T(8,128)} %copy.202, f32[32,32,768]{2,1,0:T(8,128)} %copy.202, f32[32,32,768]{2,1,0:T(8,128)} %copy.202, f32[32,32,768]{2,1,0:T(8,128)} %copy.202), branch_computations={%region_0.1_spmd, %region_1.2_spmd, %region_2.3_spmd, %region_3.4_... | conditional | flops 1769472 | bytes 38535204 | solution.py:47
  13.6 3.7 copy.116
  18.6 2.7 pad_maximum_fusion
  22.8 11.4 %collective-permute-start = (f32[32,1,768]{2,0,1:T(8,128)S(1)}, f32[32,1,768]{2,0,1:T(8,128)S(1)}, u32[]{:S(2)}, u32[]{:S(2)}) collective-permute-start(f32[32,1,768]{2,0,1:T(8,128)S(1)} %copy.174), channel_id=1, source_target_pairs={{0,8},{8,16},{16,24},{24,0},{1,9},{9,17},{17,25},{25,1},{2,10},{10... | collective-permute-start | bytes 294920 | tf_op jit(solution)/shard_map/ppermute | solution.py:25
  34.2 12.3 %collective-permute-start.1 = (f32[32,1,768]{2,0,1:T(8,128)S(1)}, f32[32,1,768]{2,0,1:T(8,128)S(1)}, u32[]{:S(2)}, u32[]{:S(2)}) collective-permute-start(f32[32,1,768]{2,0,1:T(8,128)S(1)} %copy.173), channel_id=1, source_target_pairs={{8,0},{16,8},{24,16},{0,24},{9,1},{17,9},{25,17},{1,25},{10,2},{18... | collective-permute-start | bytes 294920 | tf_op jit(solution)/shard_map/ppermute | solution.py:28
  48.0 7.6 %scatter_custom_fusion = s32[512]{0:T(512)S(1)} fusion(s32[1024]{0:T(1024)S(1)} %bitcast.89, s32[1024]{0:T(1024)S(1)} %broadcast.278, s32[]{:T(128)} %constant.84.clone.1), kind=kCustom, calls=%fused_computation.166 | custom fusion | flops 1024 | bytes 2052 | tf_op jit(solution)/shard_map/scatter-add | solution.py:137
  58.2 5.1 %gather_fusion.1 = f32[512,768]{1,0:T(8,128)} fusion(f32[1024,768]{1,0:T(8,128)} %bitcast.68, s32[1024]{0:T(1024)S(1)} %pad_clamp_fusion), kind=kCustom, calls=%fused_computation.1 | custom fusion | bytes 3147776 | tf_op jit(solution)/shard_map/gather | solution.py:104
  63.9 3.9 constant_dynamic-update-slice_fusion.1
  68.1 5.4 %collective-permute-start.3 = (f32[1,34,768]{2,0,1:T(1,128)S(1)}, f32[1,34,768]{2,0,1:T(1,128)S(1)}, u32[]{:S(2)}, u32[]{:S(2)}) collective-permute-start(f32[1,34,768]{2,0,1:T(1,128)S(1)} %get-tuple-element.211), channel_id=1, source_target_pairs={{1,0},{2,1},{3,2},{4,3},{5,4},{6,5},{7,6},{0,7},{9,8},{10,9},{11,1... | collective-permute-start | bytes 313352 | tf_op jit(solution)/shard_map/ppermute | solution.py:28
  73.9 2.4 tile.18
  76.3 5.1 %max.31 = f32[32,33,768]{2,0,1:T(8,128)} reshape(f32[32,33,8,96]{3,2,0,1:T(8,128)} %tile.18) | data formatting | bytes 6488064 | tf_op jit(solution)/shard_map/max | solution.py:61
  81.5 2.4 tile.19
  83.8 5.1 %min.31 = f32[32,33,768]{2,0,1:T(8,128)} reshape(f32[32,33,8,96]{3,2,0,1:T(8,128)} %tile.19) | data formatting | bytes 6488064 | tf_op jit(solution)/shard_map/min | solution.py:61
  89.0 8.1 %multiply_add_fusion = f32[32,33,768]{2,0,1:T(8,128)} fusion(f32[32,33,768]{2,0,1:T(8,128)} %min.31, f32[32,33,768]{2,0,1:T(8,128)} %copy-done.12, f32[32,33,768]{2,0,1:T(8,128)} %max.31, f32[32,33,768]{2,0,1:T(8,128)} %copy-done.22), kind=kLoop, calls=%fused_computation.63 | loop fusion | flops 2433024 | bytes 16220160 | tf_op jit(solution)/shard_map/add | solution.py:61
  97.4 2.3 tile.17
  99.7 5.1 %min.29 = f32[33,32,768]{2,1,0:T(8,128)} reshape(f32[33,32,8,96]{3,2,1,0:T(8,128)} %tile.17) | data formatting | bytes 6488064 | tf_op jit(solution)/shard_map/min | solution.py:57
  105.0 2.4 tile.16
  107.3 5.2 %max.29 = f32[33,32,768]{2,1,0:T(8,128)} reshape(f32[33,32,8,96]{3,2,1,0:T(8,128)} %tile.16) | data formatting | bytes 6488064 | tf_op jit(solution)/shard_map/max | solution.py:57
  112.5 9.4 %fusion.17 = f32[33,32,768]{2,0,1:T(8,128)S(1)} fusion(f32[1,34,768]{2,0,1:T(1,128)S(1)} %collective-permute-done.3, f32[32,34,768]{2,0,1:T(8,128)} %copy-done.16, f32[1,34,768]{2,0,1:T(1,128)S(1)} %collective-permute-done.2, f32[33,32,768]{2,1,0:T(8,128)} %min.29, f32[33,32,768]{2,1,0:T(8,128)} %max.29), kind=kLoop, calls=%fused_computation.57 | loop fusion | flops 4055040 | bytes 13283328 | tf_op jit(solution)/shard_map/add | solution.py:57
  121.9 2.6 fusion.24
  129.7 2.3 tile.43
  132.0 5.1 %min.35 = f32[32,33,768]{2,0,1:T(8,128)} reshape(f32[32,33,8,96]{3,2,0,1:T(8,128)} %tile.43) | data formatting | bytes 6488064 | tf_op jit(solution)/shard_map/min | solution.py:61
  137.2 2.4 tile.42
  139.6 5.1 %max.35 = f32[32,33,768]{2,0,1:T(8,128)} reshape(f32[32,33,8,96]{3,2,0,1:T(8,128)} %tile.42) | data formatting | bytes 6488064 | tf_op jit(solution)/shard_map/max | solution.py:61
  144.7 1.7 pad_maximum_fusion.18
  146.4 4.7 collective-permute-start.7
  151.1 5.5 %fusion.20 = f32[32,33,768]{2,0,1:T(8,128)} fusion(f32[32,33,768]{2,0,1:T(8,128)} %min.35, f32[32,1,768]{2,0,1:T(8,128)S(1)} %collective-permute-done.5, f32[32,33,768]{2,0,1:T(8,128)} %max.35, f32[32,1,768]{2,0,1:T(8,128)S(1)} %collective-permute-done.4, f32[32,32,768]{2,0,1:T(8,128)S(1)} %copy-done.2), kind=kLoop, calls=%fused_computation.61 | loop fusion | flops 4055040 | bytes 13074432 | tf_op jit(solution)/shard_map/add | solution.py:61
  156.9 2.4 tile.41
  159.3 5.1 %min.33 = f32[33,32,768]{2,1,0:T(8,128)} reshape(f32[33,32,8,96]{3,2,1,0:T(8,128)} %tile.41) | data formatting | bytes 6488064 | tf_op jit(solution)/shard_map/min | solution.py:57
  164.6 2.3 tile.40
  166.9 5.1 %max.33 = f32[33,32,768]{2,1,0:T(8,128)} reshape(f32[33,32,8,96]{3,2,1,0:T(8,128)} %tile.40) | data formatting | bytes 6488064 | tf_op jit(solution)/shard_map/max | solution.py:57
  172.0 8.1 %fusion.14 = f32[33,32,768]{2,0,1:T(8,128)S(1)} fusion(f32[1,34,768]{2,0,1:T(1,128)S(1)} %collective-permute-done.7, f32[32,1,768]{2,0,1:T(8,128)S(1)} %collective-permute-done.5, f32[32,32,768]{2,0,1:T(8,128)} %copy-done.1, f32[32,1,768]{2,0,1:T(8,128)S(1)} %collective-permute-done.4, f32[1,34,768]{2,0,1:T(1,128)S(1)} %collective-permute-done.6, ...), kind=kLoop, calls=%fused_computation.48 | loop fusion | flops 7299072 | bytes 13283328 | tf_op jit(solution)/shard_map/add | solution.py:57
  182.0 41.8 %conditional.3 = (f32[1024,768]{1,0:T(8,128)}, f32[1024,1]{0,1:T(1,128)S(1)}) conditional(s32[]{:T(128)} %clamp.9, (f32[33,32,768]{2,0,1:T(8,128)S(1)}, f32[32,33,768]{2,0,1:T(8,128)S(1)}, f32[32,32,768]{2,0,1:T(8,128)S(1)}, f32[32,32,768]{2,0,1:T(8,128)S(1)}) %tuple.105, (f32[33,32,768]{2,0,1:T(8,128)S(1)}, ...), branch_computations={%region_4.6_spmd, %region_6.8_spmd, %region_8.10_spmd, %region_10.... | conditional | flops 7273472 | bytes 72765488 | solution.py:47
  197.3 1.9 copy.145
  200.2 7.8 %fusion.12 = f32[32,32,768]{2,0,1:T(8,128)S(1)} fusion(f32[32,33,768]{2,1,0:T(8,128)S(1)} %copy.145, f32[33,32,768]{2,1,0:T(8,128)S(1)} %copy.144, f32[32,32,768]{2,0,1:T(8,128)S(1)} %get-tuple-element.175, f32[32,32,768]{2,0,1:T(8,128)S(1)} %get-tuple-element.174), kind=kLoop, calls=%fused_computation.37 | loop fusion | flops 3932160 | bytes 22020096 | tf_op jit(solution)/shard_map/cond/branch_3_fun/jit(rot90)/transpose | solution.py:38
  208.1 1.7 copy-done.15
  211.6 4.0 slice.359
  215.7 1.9 slice.268
  217.6 2.4 multiply_reduce_fusion.3
  220.0 3.5 copy.114
  223.9 3.7 copy.148
  227.6 2.9 fusion.63
  236.6 4.0 multiply_add_fusion.1
  240.6 3.6 copy.150
  244.2 4.4 gather_fusion
  249.4 1.9 fusion.64
  253.2 1.8 multiply_reduce_fusion.6
  255.0 9.2 %scatter_custom_fusion.3 = f32[1024,768]{1,0:T(8,128)} fusion(f32[1024,768]{1,0:T(8,128)} %bitcast.69, s32[512]{0:T(512)} %bitcast.84, f32[512,768]{1,0:T(8,128)} %get-tuple-element.226, f32[512,768]{1,0:T(8,128)S(1)} %gather_fusion, f32[512]{0:T(512)S(1)} %broadcast_multiply_fusion.1, f32[512]{0:T(512)S(1)} %fusion.54, f32[512]{0:T(512)S(1)} %add_rsqrt_fusion.2), kind=kCustom, calls=%fused_computation.88 | custom fusion | flops 2359296 | bytes 6297600 | tf_op jit(solution)/shard_map/scatter-add | solution.py:106
  264.2 3.5 copy.152
  267.7 3.5 copy.151
  271.2 8.6 %scatter_custom_fusion.1 = f32[1024,768]{1,0:T(8,128)} fusion(f32[1024,768]{1,0:T(8,128)} %copy.151, s32[512]{0:T(512)} %bitcast.85, f32[512,768]{1,0:T(8,128)} %fusion.64, f32[512]{0:T(512)S(1)} %fusion.55), kind=kCustom, calls=%fused_computation.95 | custom fusion | flops 786432 | bytes 4720640 | tf_op jit(solution)/shard_map/scatter-add | solution.py:101
  279.8 7.4 %scatter_custom_fusion.2 = f32[1024,768]{1,0:T(8,128)} fusion(s32[1024]{0:T(1024)} %bitcast.88, f32[1024,768]{1,0:T(8,128)} %scatter_custom_fusion.1, f32[]{:T(128)} %constant.83.clone.1), kind=kCustom, calls=%fused_computation.98 | custom fusion | bytes 3146240 | tf_op jit(solution)/shard_map/scatter | solution.py:144
  287.3 4.6 all-to-all-start
  292.1 4.2 multiply_convert_fusion.5
  304.1 1.9 add_add_fusion
  306.0 2.6 reshape.286
  308.6 4.0 fusion.46
  312.6 6.5 %fusion.37 = f32[768,512]{1,0:T(8,128)} fusion(f32[1024,512]{1,0:T(8,128)} %copy-done.26, bf16[1024,768]{0,1:T(8,128)(2,1)} %copy-done.28, bf16[512,768]{1,0:T(8,128)(2,1)S(1)} %copy-done, f32[1024,768]{1,0:T(8,128)} %get-tuple-element.142, f32[1024]{0:T(1024)S(1)} %bitcast.81), kind=kOutput, calls=%fused_computation.105 | convolution fusion | flops 1616904192 | bytes 9179136 | tf_op jit(solution)/shard_map/dot_general | solution.py:118
  319.1 2.6 add_bitcast_fusion
  321.6 1.5 copy.155
  323.2 156.5 %all-reduce.5.cloned.1.call-done = (f32[393216]{0:T(1024)}, f32[393216]{0:T(1024)}) async-done(((f32[393216]{0:T(1024)}, f32[393216]{0:T(1024)}), (f32[393216]{0:T(1024)}, f32[393216]{0:T(1024)})) %all-reduce.5.cloned.1.call-update) | async-done | bytes 3145744
  482.5 3.8 copy.204
  (148 shorter events, 38.5 us)
Async XLA Ops:
  7.2 224.7 %copy-start = (bf16[512,768]{1,0:T(8,128)(2,1)S(1)}, bf16[512,768]{1,0:T(8,128)(2,1)}, u32[]{:S(2)}) copy-start(bf16[512,768]{1,0:T(8,128)(2,1)} %param.21) | copy-start | bytes 2359300
  7.2 4.1 copy-start.23
  13.5 33.1 %copy-start.33 = (s32[32,32]{1,0:T(8,128)S(1)}, s32[32,32]{1,0:T(8,128)}, u32[]{:S(2)}) copy-start(s32[32,32]{1,0:T(8,128)} %param.17) | copy-start | bytes 12292
  13.5 43.9 %copy-start.34 = (s32[32,32]{1,0:T(8,128)S(1)}, s32[32,32]{1,0:T(8,128)}, u32[]{:S(2)}) copy-start(s32[32,32]{1,0:T(8,128)} %param.18) | copy-start | bytes 12292
  22.8 41.0 %collective-permute-start = (f32[32,1,768]{2,0,1:T(8,128)S(1)}, f32[32,1,768]{2,0,1:T(8,128)S(1)}, u32[]{:S(2)}, u32[]{:S(2)}) collective-permute-start(f32[32,1,768]{2,0,1:T(8,128)S(1)} %copy.174), channel_id=1, source_target_pairs={{0,8},{8,16},{16,24},{24,0},{1,9},{9,17},{17,25},{25,1},{2,10},{10... | collective-permute-start | bytes 294920 | tf_op jit(solution)/shard_map/ppermute | solution.py:25
  34.2 33.6 %collective-permute-start.1 = (f32[32,1,768]{2,0,1:T(8,128)S(1)}, f32[32,1,768]{2,0,1:T(8,128)S(1)}, u32[]{:S(2)}, u32[]{:S(2)}) collective-permute-start(f32[32,1,768]{2,0,1:T(8,128)S(1)} %copy.173), channel_id=1, source_target_pairs={{8,0},{16,8},{24,16},{0,24},{9,1},{17,9},{25,17},{1,25},{10,2},{18... | collective-permute-start | bytes 294920 | tf_op jit(solution)/shard_map/ppermute | solution.py:28
  56.9 0.6 copy-start.35
  67.8 6.1 %copy-start.22 = (f32[32,33,768]{2,0,1:T(8,128)}, f32[32,33,768]{2,0,1:T(8,128)S(1)}, u32[]{:S(2)}) copy-start(f32[32,33,768]{2,0,1:T(8,128)S(1)} %get-tuple-element.217) | copy-start | bytes 9732100
  67.9 5.7 %copy-start.12 = (f32[32,33,768]{2,0,1:T(8,128)}, f32[32,33,768]{2,0,1:T(8,128)S(1)}, u32[]{:S(2)}) copy-start(f32[32,33,768]{2,0,1:T(8,128)S(1)} %get-tuple-element.222) | copy-start | bytes 9732100
  67.9 6.0 %copy-start.16 = (f32[32,34,768]{2,0,1:T(8,128)}, f32[32,34,768]{2,0,1:T(8,128)S(1)}, u32[]{:S(2)}) copy-start(f32[32,34,768]{2,0,1:T(8,128)S(1)} %get-tuple-element.221) | copy-start | bytes 10027012
  68.1 29.0 %collective-permute-start.2 = (f32[1,34,768]{2,0,1:T(1,128)S(1)}, f32[1,34,768]{2,0,1:T(1,128)S(1)}, u32[]{:S(2)}, u32[]{:S(2)}) collective-permute-start(f32[1,34,768]{2,0,1:T(1,128)S(1)} %get-tuple-element.210), channel_id=1, source_target_pairs={{0,1},{1,2},{2,3},{3,4},{4,5},{5,6},{6,7},{7,0},{8,9},{9,10},{10,1... | collective-permute-start | bytes 313352 | tf_op jit(solution)/shard_map/ppermute | solution.py:25
  68.1 29.0 %collective-permute-start.3 = (f32[1,34,768]{2,0,1:T(1,128)S(1)}, f32[1,34,768]{2,0,1:T(1,128)S(1)}, u32[]{:S(2)}, u32[]{:S(2)}) collective-permute-start(f32[1,34,768]{2,0,1:T(1,128)S(1)} %get-tuple-element.211), channel_id=1, source_target_pairs={{1,0},{2,1},{3,2},{4,3},{5,4},{6,5},{7,6},{0,7},{9,8},{10,9},{11,1... | collective-permute-start | bytes 313352 | tf_op jit(solution)/shard_map/ppermute | solution.py:28
  89.0 8.1 %copy-start.17 = (f32[32,34,768]{2,0,1:T(8,128)S(1)}, f32[32,34,768]{2,0,1:T(8,128)}, u32[]{:S(2)}) copy-start(f32[32,34,768]{2,0,1:T(8,128)} %copy-done.16) | copy-start | bytes 10027012
  112.5 9.5 %copy-start.6 = (f32[32,32,768]{2,1,0:T(8,128)S(1)}, f32[32,32,768]{2,1,0:T(8,128)}, u32[]{:S(2)}) copy-start(f32[32,32,768]{2,1,0:T(8,128)} %get-tuple-element.245) | copy-start | bytes 9437188
  112.5 9.5 %copy-start.8 = (f32[32,33,768]{2,0,1:T(8,128)S(1)}, f32[32,33,768]{2,0,1:T(8,128)}, u32[]{:S(2)}) copy-start(f32[32,33,768]{2,0,1:T(8,128)} %multiply_add_fusion) | copy-start | bytes 9732100
  124.5 4.8 copy-start.1
  124.5 4.1 collective-permute-start.4
  126.1 3.2 collective-permute-start.5
  144.7 6.5 %copy-start.2 = (f32[32,32,768]{2,0,1:T(8,128)S(1)}, f32[32,32,768]{2,0,1:T(8,128)}, u32[]{:S(2)}) copy-start(f32[32,32,768]{2,0,1:T(8,128)} %copy-done.1) | copy-start | bytes 9437188
  146.4 10.3 %collective-permute-start.6 = (f32[1,34,768]{2,0,1:T(1,128)S(1)}, f32[1,34,768]{2,0,1:T(1,128)S(1)}, u32[]{:S(2)}, u32[]{:S(2)}) collective-permute-start(f32[1,34,768]{2,0,1:T(1,128)S(1)} %get-tuple-element.208), channel_id=1, source_target_pairs={{0,1},{1,2},{2,3},{3,4},{4,5},{5,6},{6,7},{7,0},{8,9},{9,10},{10,1... | collective-permute-start | bytes 313352 | tf_op jit(solution)/shard_map/ppermute | solution.py:25
  146.4 10.2 %collective-permute-start.7 = (f32[1,34,768]{2,0,1:T(1,128)S(1)}, f32[1,34,768]{2,0,1:T(1,128)S(1)}, u32[]{:S(2)}, u32[]{:S(2)}) collective-permute-start(f32[1,34,768]{2,0,1:T(1,128)S(1)} %get-tuple-element.209), channel_id=1, source_target_pairs={{1,0},{2,1},{3,2},{4,3},{5,4},{6,5},{7,6},{0,7},{9,8},{10,9},{11,1... | collective-permute-start | bytes 313352 | tf_op jit(solution)/shard_map/ppermute | solution.py:28
  172.0 8.5 %copy-start.7 = (f32[32,33,768]{2,0,1:T(8,128)S(1)}, f32[32,33,768]{2,0,1:T(8,128)}, u32[]{:S(2)}) copy-start(f32[32,33,768]{2,0,1:T(8,128)} %fusion.20) | copy-start | bytes 9732100
  180.1 1.9 copy-start.3
  208.1 1.7 copy-start.15
  223.9 3.7 copy-start.9
  230.5 1.4 copy-start.26
  231.8 1.9 copy-start.19
  234.9 1.7 copy-start.4
  236.6 4.0 copy-start.10
  249.4 2.9 copy-start.31
  249.4 2.1 copy-start.29
  252.4 0.8 copy-start.24
  287.3 195.3 %all-to-all-start = ((f32[32,32,768]{2,1,0:T(8,128)}), f32[32,32,768]{2,1,0:T(8,128)}, u32[]{:S(2)}, u32[]{:S(2)}) async-start(f32[32,32,768]{2,1,0:T(8,128)} %bitcast.78), calls=%async_computation | async-start | bytes 6291456 | tf_op jit(solution)/shard_map/all_to_all | solution.py:146
  291.9 187.8 %all-reduce.5.cloned.1.call-start = ((), (), s32[]{:S(2)}) async-start(), calls=%async_computation.1 | async-start | bytes 6291456
  292.1 4.2 copy-start.5
  296.3 1.1 copy-start.20
  296.4 2.3 copy-start.18
  298.6 1.6 copy-start.27
  300.2 1.5 copy-start.28
  300.2 2.2 copy-start.11
  302.4 1.5 copy-start.30
  302.4 1.7 copy-start.32
  306.0 2.6 copy-start.21
  312.6 6.5 %copy-start.25 = (bf16[512,512]{1,0:T(8,128)(2,1)S(1)}, bf16[512,512]{1,0:T(8,128)(2,1)}, u32[]{:S(2)}) copy-start(bf16[512,512]{1,0:T(8,128)(2,1)} %copy-done.24) | copy-start | bytes 1572868
Sparse Core Ops, SparseCore 0:
  323.3 156.3 all-reduce.4
where the time goes:
time: 503 us; the launch traced here: 493 us
  waiting for transfers between devices  158 us (31%)
  local copies, waits for them, and re-layouts  143 us (28%)
  other arithmetic  82.6 us (16%)
  starting transfers between devices  41 us (8%)
  matrix products  37.3 us (7%)
  loops' own time  15.5 us (3%)
  between operations  15.5 us (3%)
    unnamed x2, waiting for transfers between devices  157 us
    unnamed x76, local copies, waits for them, and re-layouts  26.2 us
    ppermute x4, starting transfers between devices, extended(): lax.ppermute(lax.slice_in_dim(block, 0, width, axis=dim), axis, backward)  23.1 us
    add x2, other arithmetic, advance(): jnp.maximum(face_x, 0.0) * padded[:-1, 1:-1]  17.5 us
    another operation x2, loops' own time, turn_frame(): lax.switch(quarter_turns, [make_turn(0), make_turn(1), make_turn(2), make...  15.5 us
    add x2, other arithmetic, advance(): jnp.maximum(face_y, 0.0) * padded[1:-1, :-1]  13.6 us
    ppermute x4, starting transfers between devices, extended(): lax.ppermute(lax.slice_in_dim(block, block.shape[dim] - width, None, axis...  13.1 us
    max x4, local copies, waits for them, and re-layouts, advance(): jnp.maximum(face_x, 0.0) * padded[:-1, 1:-1]  10.5 us
  transfers between devices with their start and end apart: 10, of which 3 were waited for; matrix products, arithmetic and copies ran while one was open for 17% of the time, Pallas kernels for 0%

commit v1 on v0

v1 whole, which is shorter than its diff:
```python
import functools
import jax
import jax.numpy as jnp
from jax import lax
from jax.experimental import pallas as pl
from jax.experimental.pallas import tpu as pltpu
from jax.sharding import PartitionSpec as P

V = 8
TAU = 0.5
COURANT = 0.1
EPS = 1e-06
LANES = 128
COL = 256
F32 = jnp.float32
BF16 = jnp.bfloat16
SIDE_WINDS = (((0, 1.0), (1, 1.0)), ((1, 1.0), (0, -1.0)), ((0, -1.0), (1, -1.0)), ((1, -1.0), (0, 1.0)))

VMEM = pl.BlockSpec(memory_space=pltpu.VMEM)
SMEM = pl.BlockSpec(memory_space=pltpu.SMEM)


def params(mib):
    return pltpu.CompilerParams(vmem_limit_bytes=mib * 1024 * 1024)


def side_cells(k, n):
    pick = lambda a, b, c, e: jnp.where(k == 0, a, jnp.where(k == 1, b, jnp.where(k == 2, c, e)))
    base = pick(0, (n - 1) * n, n * n - 1, n - 1)
    return base, pick(1, -n, -1, n), pick(n, 1, -n, -1)


def turn_winds(ref, rows, quarter, levels):
    start, size = rows
    width = -(-2 * levels // LANES) * LANES
    w = ref[start : start + size, 0:width]
    lane = lax.broadcasted_iota(jnp.int32, w.shape, 1)
    swapped = jnp.where(lane < levels, pltpu.roll(w, width - levels, 1), pltpu.roll(w, levels, 1))
    cos = ((quarter == 0).astype(F32) - (quarter == 2).astype(F32))
    sin = ((quarter == 1).astype(F32) - (quarter == 3).astype(F32))
    turned = w * cos + swapped * jnp.where(lane < levels, -sin, sin)
    ref[start : start + size, 0:width] = jnp.where(lane < 2 * levels, turned, w)


def copy_rows(dst, dst_base, src, cell, step, count):
    def body(s, carry):
        dst[pl.ds(dst_base + s, 1), :] = src[pl.ds(cell + s * step, 1), :]
        return carry

    lax.fori_loop(0, count, body, 0, unroll=8)


def wind_row(src, a, which, levels):
    start = which * levels
    chunk, off = start // LANES, start % LANES
    first = src[a, :, chunk * LANES : (chunk + 1) * LANES]
    if off == 0:
        return first
    second = src[a, :, (chunk + 1) * LANES : (chunk + 2) * LANES]
    lane = lax.broadcasted_iota(jnp.int32, first.shape, 1)
    shift = LANES - off
    return jnp.where(lane < shift, pltpu.roll(first, shift, 1), pltpu.roll(second, shift, 1))


def repeat_levels(face, levels, chunks):
    lane = lax.broadcasted_iota(jnp.int32, face.shape, 1)
    rolls = {0: face}
    out = []
    for c in range(chunks):
        result, at = None, 0
        while at < LANES:
            index = (c * LANES + at) % levels
            shift = (at - index) % LANES
            if shift not in rolls:
                rolls[shift] = pltpu.roll(face, shift, 1)
            result = rolls[shift] if result is None else jnp.where(lane < at, result, rolls[shift])
            at += levels - index
        out.append(result)
    return out


def transport(src, dst, face_lead, face_sub, lo, hi, winds, levels):
    (lead, lead_sign), (sub, sub_sign) = winds
    size, feats = src.shape[1], src.shape[2]
    chunks = feats // LANES
    period = face_lead.shape[2] // LANES

    def faces(a, carry):
        here, there = wind_row(src, a, lead, levels), wind_row(src, a + 1, lead, levels)
        for c, part in enumerate(repeat_levels((0.5 * lead_sign) * (here + there), levels, period)):
            face_lead[a, :, c * LANES : (c + 1) * LANES] = part
        here = wind_row(src, a, sub, levels)
        ahead = pltpu.roll(here, size - 1, 0)
        for c, part in enumerate(repeat_levels((0.5 * sub_sign) * (here + ahead), levels, period)):
            face_sub[a, :, c * LANES : (c + 1) * LANES] = part
        return carry

    lax.fori_loop(lo - 1, hi, faces, 0)

    def update(a, carry):
        for c3 in range(period):
            lanes3 = slice(c3 * LANES, (c3 + 1) * LANES)
            high, low, side = face_lead[a, :, lanes3], face_lead[a - 1, :, lanes3], face_sub[a, :, lanes3]
            high_p, high_m = jnp.maximum(high, 0.0), jnp.minimum(high, 0.0)
            low_p, low_m = jnp.maximum(low, 0.0), jnp.minimum(low, 0.0)
            side_p, side_m = jnp.maximum(side, 0.0), jnp.minimum(side, 0.0)
            for c in range(c3, chunks, period):
                lanes = slice(c * LANES, (c + 1) * LANES)
                q = src[a, :, lanes]
                flux_high = high_p * q + high_m * src[a + 1, :, lanes]
                flux_low = low_p * src[a - 1, :, lanes] + low_m * q
                flux_side = side_p * q + side_m * pltpu.roll(q, size - 1, 0)
                flux_back = pltpu.roll(flux_side, 1, 0)
                dst[a, :, lanes] = q - COURANT * ((flux_high - flux_low) + (flux_side - flux_back))
        return carry

    lax.fori_loop(lo, hi, update, 0)


def network_forward(x, mask, w_in, w_out, normed, scale, slope, hidden, hsum, rows):
    total = None
    for use in range(3):
        inv = lax.rsqrt(jnp.mean(x * x, axis=1, keepdims=True) + EPS)
        unit = (x * inv).astype(BF16)
        normed[use, rows, :] = unit
        if use > 0:
            scale[use - 1, rows, :] = jnp.broadcast_to(inv, (x.shape[0], LANES))
        p = jnp.dot(unit, w_in, preferred_element_type=F32)
        s = 0.5 + 0.5 * jnp.tanh(0.5 * p)
        silu = p * s
        slope[use, rows, :] = s + silu * (1.0 - s)
        h = silu.astype(BF16)
        hidden[use, rows, :] = h
        if use < 2:
            total = h.astype(F32) if use == 0 else total + h.astype(F32)
            x = x + TAU * jnp.dot(h, w_out, preferred_element_type=F32)
        else:
            hsum[rows, :] = total + h.astype(F32) * mask


def pack_kernel(n, levels, turn, air, s0, s1, s2, s3, c0, c1, c2, c3):
    o = turn[0]
    for k, out in enumerate((s0, s1, s2, s3)):
        base, cm, cd = side_cells((k - o + 4) % 4, n)
        for d in range(2):
            copy_rows(out, d * n, air, base + cd * d + cm * (n - 1), -cm, n)
        turn_winds(out, (0, 2 * n), o, levels)
    c0[...] = s2[n - 1 : n, :]
    c1[...] = s2[0:1, :]
    c2[...] = s0[n - 1 : n, :]
    c3[...] = s0[0:1, :]


def inner_kernel(n, levels, turn, dest, air, air_rows, mask, w_in, w_out,
                 own, mask_rim, normed, scale, slope, hidden, outgoing,
                 q_one, q_two, face_lead, face_sub, hsum):
    o = turn[0]
    winds = ((0, 1.0), (1, 1.0))
    transport(air, q_one, face_lead, face_sub, 1, n - 1, winds, levels)
    transport(q_one, q_two, face_lead, face_sub, 2, n - 2, winds, levels)
    inner = n - 4
    parts = 2
    size = inner // parts * n
    feats = air.shape[2]

    def chunk(part, carry):
        rows = pl.ds(pl.multiple_of(part * size, size), size)
        x = q_two[pl.ds(2 + part * (inner // parts), inner // parts), :, :].reshape(size, feats)
        m = mask[pl.ds(pl.multiple_of(2 * n + part * size, 8), size), 0:1]
        network_forward(x, m, w_in[...], w_out[...], normed, scale, slope, hidden, hsum, rows)
        return carry

    lax.fori_loop(0, parts, chunk, 0)

    def place(i, carry):
        for j in range(2, n - 2):
            outgoing[pl.ds(dest[i * n + j], 1), :] = hsum[pl.ds((i - 2) * n + j, 1), :]
        return carry

    lax.fori_loop(2, n - 2, place, 0)
    for k in range(4):
        base, cm, cd = side_cells((k - o + 4) % 4, n)
        for d in range(4):
            copy_rows(own, (k * 4 + d) * n, air_rows, base + cd * d, cm, n)
        for d in range(2):
            copy_rows(mask_rim, (k * 2 + d) * n, mask, base + cd * d, cm, n)
        turn_winds(own, (k * 4 * n, 4 * n), o, levels)


def rim_kernel(n, levels, turn, dest, h0, h1, h2, h3, c_mm, c_mp, c_pp, c_pm, own, mask_rim, w_in, w_out, before,
               normed, scale, slope, hidden, outgoing,
               wide, wide_one, wide_two, slim, slim_one, slim_two, lead_wide, sub_wide, lead_slim, sub_slim, x_rim, hsum):
    outgoing[...] = before[...]
    o = turn[0]
    halo = (h0, h1, h2, h3)
    for k in range(4):
        ends = k % 2 == 0
        src, one, two = (wide, wide_one, wide_two) if ends else (slim, slim_one, slim_two)
        lead, sub = (lead_wide, sub_wide) if ends else (lead_slim, sub_slim)
        for depth in range(6):
            d = depth - 2
            row = halo[k][(1 - depth) * n : (2 - depth) * n, :] if d < 0 else own[(k * 4 + d) * n : (k * 4 + d + 1) * n, :]
            src[depth, 0:n, :] = row
            if ends:
                src[depth, n + 2 : n + 8, :] = row[0:6, :]
                src[depth, n + 8 : n + 14, :] = row[n - 6 : n, :]
                first, last = (c_mm, c_mp) if k == 0 else (c_pp, c_pm)
                for e in range(2):
                    if d < 0:
                        src[depth, n + 1 - e : n + 2 - e, :] = first[...]
                        src[depth, n + 14 + e : n + 15 + e, :] = last[...]
                    else:
                        at = e * n + n - 1 - d
                        src[depth, n + 1 - e : n + 2 - e, :] = halo[(k + 1) % 4][at : at + 1, :]
                        at = e * n + d
                        src[depth, n + 14 + e : n + 15 + e, :] = halo[(k + 3) % 4][at : at + 1, :]
        transport(src, one, lead, sub, 1, 5, SIDE_WINDS[k], levels)
        transport(one, two, lead, sub, 2, 4, SIDE_WINDS[k], levels)
        for d in range(2):
            at = (k * 2 + d) * n
            x_rim[at : at + n, :] = two[2 + d, 0:n, :]
            if ends:
                x_rim[at : at + 2, :] = two[2 + d, n + 2 : n + 4, :]
                x_rim[at + n - 2 : at + n, :] = two[2 + d, n + 12 : n + 14, :]
    turn_winds(x_rim, (0, 8 * n), (4 - o) % 4, levels)
    network_forward(x_rim[...], mask_rim[:, 0:1], w_in[...], w_out[...], normed, scale, slope, hidden, hsum,
                    slice(0, 8 * n))
    for k in range(4):
        base, cm, cd = side_cells((k - o + 4) % 4, n)
        skip = 2 * (k % 2)
        for d in range(2):
            for m in range(skip, n - skip):
                at = (k * 2 + d) * n + m
                outgoing[pl.ds(dest[base + cd * d + cm * m], 1), :] = hsum[at : at + 1, :]


def contract_rows(a, b):
    return lax.dot_general(a, b, (((0,), (0,)), ((), ())), preferred_element_type=F32)


def contract_last(a, b):
    return lax.dot_general(a, b, (((1,), (1,)), ((), ())), preferred_element_type=F32)


def network_backward(cot, mask, w_in, w_out, normed, scale, slope, err_out, err_in, rows):
    grad = cot * mask
    for use in (2, 1, 0):
        e = (TAU * grad).astype(BF16)
        err_out[use, rows, :] = e
        inner = (contract_last(e, w_out) * slope[use, rows, :]).astype(BF16)
        err_in[use, rows, :] = inner
        if use > 0:
            d = contract_last(inner, w_in)
            unit = normed[use, rows, :].astype(F32)
            d = scale[use - 1, rows, 0:1] * (d - unit * jnp.mean(d * unit, axis=1, keepdims=True))
            grad = (cot if use == 2 else grad) + d


def backward_kernel(n, grid_shape, place, turn, cot, mask, mask_rim, w_in, w_out, n_i, s_i, g_i, h_i, n_r, s_r, g_r, h_r,
                    keep, send, eo_i, ei_i, eo_r, ei_r, cot_rim, grad_in, grad_out):
    o = turn[0]
    inner = n - 4
    parts = 2
    size = inner // parts * n
    for k in range(4):
        base, cm, cd = side_cells((k - o + 4) % 4, n)
        for d in range(2):
            copy_rows(cot_rim, (k * 2 + d) * n, cot, base + cd * d, cm, n)

    def chunk(part, carry):
        rows = pl.ds(pl.multiple_of(part * size, size), size)
        at = pl.ds(pl.multiple_of(2 * n + part * size, 8), size)
        j = lax.broadcasted_iota(jnp.int32, (size, 1), 0) % n
        valid = ((j >= 2) & (j < n - 2)).astype(F32)
        network_backward(cot[at, :] * valid, mask[at, 0:1], w_in[...], w_out[...], n_i, s_i, g_i, eo_i, ei_i, rows)
        return carry

    lax.fori_loop(0, parts, chunk, 0)
    e = lax.broadcasted_iota(jnp.int32, (8 * n, 1), 0)
    m = e % n
    valid = (((e // (2 * n)) % 2 == 0) | ((m >= 2) & (m < n - 2))).astype(F32)
    network_backward(cot_rim[...] * valid, mask_rim[:, 0:1], w_in[...], w_out[...], n_r, s_r, g_r, eo_r, ei_r,
                     slice(0, 8 * n))
    flat = lambda ref: ref[...].reshape(ref.shape[0] * ref.shape[1], ref.shape[2])
    grad_out[...] = contract_rows(flat(h_i), flat(eo_i)) + contract_rows(flat(h_r), flat(eo_r))
    grad_in[...] = contract_rows(flat(n_i), flat(ei_i)) + contract_rows(flat(n_r), flat(ei_r))
    groups, tiles = grid_shape
    count = groups * tiles
    feats, units = grad_in.shape
    rows_in, rows_out = feats // count, units // count
    for g in range(groups):
        for t in range(tiles):
            p = g * tiles + t
            rg, rt = place[0] ^ g, place[1] ^ t
            at = ((rg // 2) * 2 + rt % 2) * (tiles // 2) + rt // 2
            pieces = []
            for c in range(units // COL):
                pieces.append(grad_in[p * rows_in : (p + 1) * rows_in, c * COL : (c + 1) * COL])
            for c in range(feats // COL):
                pieces.append(grad_out[p * rows_out : (p + 1) * rows_out, c * COL : (c + 1) * COL])

            def store(ref, pieces=pieces, at=at):
                row = 0
                for piece in pieces:
                    ref[at, row : row + piece.shape[0], :] = piece
                    row += piece.shape[0]

            pl.when(rg % 2 == 0)(functools.partial(store, keep))
            pl.when(rg % 2 == 1)(functools.partial(store, send))


def output_kernel(rows, w_out, out):
    x = rows[...]
    high = x.astype(BF16)
    low = (x - high.astype(F32)).astype(BF16)
    w = w_out[...]
    out[...] = TAU * (jnp.dot(high, w, preferred_element_type=F32) + jnp.dot(low, w, preferred_element_type=F32))


def shift_perm(count, by):
    return [(i, (i + by) % count) for i in range(count)]


def joint_perm(groups, tiles, move):
    return [(g * tiles + t, (lambda h: h[0] * tiles + h[1])(move(g, t))) for g in range(groups) for t in range(tiles)]


def per_device(air_state, cotangent, cost_count, assignment, orientation, weight_in, weight_out):
    groups, tiles = lax.axis_size("grp"), lax.axis_size("tile")
    count = groups * tiles
    n, feats = air_state.shape[0], air_state.shape[2]
    units = weight_in.shape[1]
    levels = feats // V
    cells, rim, inner = n * n, 8 * n, (n - 4) * n
    period = next(c for c in range(1, feats // LANES + 1) if c * LANES % levels == 0)
    shape = jax.ShapeDtypeStruct

    turn = orientation.reshape(1)
    dest = assignment.reshape(cells)
    air_rows = air_state.reshape(cells, feats)
    cot_rows = cotangent.reshape(cells, feats)
    mask = jnp.broadcast_to((cost_count.reshape(cells, 1) == 2).astype(F32), (cells, LANES))

    strips = pl.pallas_call(
        functools.partial(pack_kernel, n, levels),
        out_shape=[shape((2 * n, feats), F32)] * 4 + [shape((1, feats), F32)] * 4,
        in_specs=[SMEM, VMEM],
        out_specs=[VMEM] * 8,
        compiler_params=params(32),
        name="pack_strips",
    )(turn, air_rows)

    both = ("grp", "tile")
    halo = [
        lax.ppermute(strips[2], "tile", shift_perm(tiles, 1)),
        lax.ppermute(strips[3], "grp", shift_perm(groups, 1)),
        lax.ppermute(strips[0], "tile", shift_perm(tiles, -1)),
        lax.ppermute(strips[1], "grp", shift_perm(groups, -1)),
    ]
    corners = [
        lax.ppermute(strips[4 + i], both, joint_perm(groups, tiles, lambda g, t: ((g + dg) % groups, (t + dt) % tiles)))
        for i, (dt, dg) in enumerate(((1, 1), (1, -1), (-1, -1), (-1, 1)))
    ]

    def state(rows):
        return [
            shape((3, rows, feats), BF16),
            shape((2, rows, LANES), F32),
            shape((3, rows, units), F32),
            shape((3, rows, units), BF16),
        ]

    flops = 10 * inner * feats * units
    own, mask_rim, *saved_inner, outgoing = pl.pallas_call(
        functools.partial(inner_kernel, n, levels),
        out_shape=[shape((16 * n, feats), F32), shape((rim, LANES), F32), *state(inner), shape((cells, units), F32)],
        in_specs=[SMEM, SMEM] + [VMEM] * 5,
        out_specs=[VMEM] * 7,
        scratch_shapes=[
            pltpu.VMEM((n, n, feats), F32),
            pltpu.VMEM((n, n, feats), F32),
            pltpu.VMEM((n, n, period * LANES), F32),
            pltpu.VMEM((n, n, period * LANES), F32),
            pltpu.VMEM((inner, units), F32),
        ],
        compiler_params=params(56),
        cost_estimate=pl.CostEstimate(flops=flops * 2, bytes_accessed=40 << 20, transcendentals=0),
        name="inner_columns",
    )(turn, dest, air_state, air_rows, mask, weight_in, weight_out)

    wide, slim = n + 16, n
    *saved_rim, outgoing = pl.pallas_call(
        functools.partial(rim_kernel, n, levels),
        out_shape=[*state(rim), shape((cells, units), F32)],
        in_specs=[SMEM, SMEM] + [VMEM] * 13,
        out_specs=[VMEM] * 5,
        scratch_shapes=[pltpu.VMEM((6, wide, feats), F32)] * 3
        + [pltpu.VMEM((6, slim, feats), F32)] * 3
        + [pltpu.VMEM((6, wide, period * LANES), F32)] * 2
        + [pltpu.VMEM((6, slim, period * LANES), F32)] * 2
        + [pltpu.VMEM((rim, feats), F32), pltpu.VMEM((rim, units), F32)],
        compiler_params=params(48),
        cost_estimate=pl.CostEstimate(flops=10 * rim * feats * units, bytes_accessed=20 << 20, transcendentals=0),
        name="rim_columns",
    )(turn, dest, *halo, *corners, own, mask_rim, weight_in, weight_out, outgoing)

    arrived = lax.all_to_all(
        outgoing.reshape(count, cells // count, units), both, split_axis=0, concat_axis=0, tiled=True
    ).reshape(cells, units)

    place = jnp.stack([lax.axis_index("grp"), lax.axis_index("tile")]).astype(jnp.int32)
    rows_in, rows_out = feats // count, units // count
    piece = rows_in * (units // COL) + rows_out * (feats // COL)
    keep, send = pl.pallas_call(
        functools.partial(backward_kernel, n, (groups, tiles)),
        out_shape=[shape((count // 2, piece, COL), F32)] * 2,
        in_specs=[SMEM, SMEM] + [VMEM] * 13,
        out_specs=[VMEM] * 2,
        scratch_shapes=[
            pltpu.VMEM((3, inner, feats), BF16),
            pltpu.VMEM((3, inner, units), BF16),
            pltpu.VMEM((3, rim, feats), BF16),
            pltpu.VMEM((3, rim, units), BF16),
            pltpu.VMEM((rim, feats), F32),
            pltpu.VMEM((feats, units), F32),
            pltpu.VMEM((units, feats), F32),
        ],
        compiler_params=params(60),
        cost_estimate=pl.CostEstimate(flops=22 * cells * feats * units, bytes_accessed=40 << 20, transcendentals=0),
        name="columns_backward",
    )(place, turn, cot_rows, mask, mask_rim, weight_in, weight_out, *saved_inner, *saved_rim)

    sums = keep + lax.ppermute(send, "grp", [(i, i ^ 1) for i in range(groups)])
    sums = sums.reshape(groups // 2, 2, tiles // 2, piece, COL)
    total = sums[0, 0]
    for x in range(groups // 2):
        for y in range(2):
            if x or y:
                total = total + lax.ppermute(
                    sums[x, y], both, joint_perm(groups, tiles, lambda g, t: (g ^ (2 * x), t ^ y))
                )
    mine = total[0]
    for z in range(1, tiles // 2):
        mine = mine + lax.ppermute(total[z], "tile", [(t, t ^ (2 * z)) for t in range(tiles)])
    split = rows_in * (units // COL)
    flat = lambda part, rows: part.reshape(-1, rows, COL).transpose(1, 0, 2).reshape(-1)
    summed_in, summed_out = flat(mine[:split], rows_in), flat(mine[split:], rows_out)

    block = cells // 4
    tendency = pl.pallas_call(
        output_kernel,
        out_shape=shape((cells, feats), F32),
        grid=(cells // block,),
        in_specs=[pl.BlockSpec((block, units), lambda i: (i, 0)), pl.BlockSpec((units, feats), lambda i: (0, 0))],
        out_specs=pl.BlockSpec((block, feats), lambda i: (i, 0)),
        compiler_params=params(32),
        cost_estimate=pl.CostEstimate(flops=4 * cells * feats * units, bytes_accessed=6 << 20, transcendentals=0),
        name="tendency_rows",
    )(arrived, weight_out)
    return (tendency, summed_in, summed_out)


def solution(mesh):
    in_specs = (
        P("tile", "grp", None),
        P("tile", "grp", None),
        P("tile", "grp"),
        P("tile", "grp"),
        P("tile", "grp"),
        P(),
        P(),
    )
    out_specs = (P(("grp", "tile"), None), P(("grp", "tile")), P(("grp", "tile")))
    return jax.shard_map(
        per_device, mesh=mesh, in_specs=in_specs, out_specs=out_specs, check_vma=False
    )
```

time: 503 us -> 159 us (0.32); the launches traced: 493 us -> 159 us
  local copies, waits for them, and re-layouts: 143 us -> 8.59 us
  waiting for transfers between devices: 158 us -> 40 us
  other arithmetic: 82.6 us -> 2.42 us
  Pallas kernels: 0 us -> 79.9 us
  matrix products: 37.3 us -> 0 us
  loops' own time: 15.5 us -> 0 us
  starting transfers between devices: 41 us -> 26.3 us
  between operations: 15.5 us -> 1.44 us
    unnamed x2 -> x0, waiting for transfers between devices: 157 us -> none
    pallas_call x0 -> x5, Pallas kernels: none -> 79.9 us  [the longest x1 35.8 us: per_device(): pl.pallas_call(functools.partial(inner_kernel, n, levels), out_shape=[sha...]
    ppermute x8 -> x15, waiting for transfers between devices: 1.96 us -> 40 us  [the longest x3 22.2 us: per_device(): lax.ppermute(sums[x, y], both, joint_perm(groups, tiles, lambda g, t: (g...]
    dot_general x16 -> x0, matrix products: 37.3 us -> none  [the longest x3 7.01 us: forward_rows(): jnp.dot(hidden, weight_out, preferred_element_type=jnp.float32)]
    add x4 -> x3, other arithmetic: 31.2 us -> 1.75 us  [the longest x1 1.62 us: per_device(): sums = keep + lax.ppermute(send, 'grp', [(i, i ^ 1) for i in range(groups)])]
    another operation x15 -> x0, local copies, waits for them, and re-layouts: 26.2 us -> none  [the longest x4 9.48 us: advance(): jnp.tile(0.5 * (north_wind[1:-1, :-1] + north_wind[1:-1, 1:]), (1, 1, V))]
    scatter-add x3 -> x0, other arithmetic: 25.4 us -> none  [the longest x1 9.2 us: finish_physics(): carried = jnp.zeros_like(start_rows).at[picked].add(back_three * weight_col)]
    max x6 -> x0, local copies, waits for them, and re-layouts: 20.8 us -> none  [the longest x4 10.5 us: advance(): jnp.maximum(face_x, 0.0) * padded[:-1, 1:-1]]
  transfers between devices with their start and end apart: 10 -> 16, of which waited for: 3 -> 8; matrix products, arithmetic and copies ran while one was open for 17% -> 4% of each run, Pallas kernels for 0% -> 38%
where the time goes in v1:
time: 159 us
  Pallas kernels  79.9 us (50%)
  waiting for transfers between devices  40 us (25%)
  starting transfers between devices  26.3 us (17%)
  local copies, waits for them, and re-layouts  8.59 us (5%)
  other arithmetic  2.42 us (2%)
    pallas_call x1, Pallas kernels, per_device(): pl.pallas_call(functools.partial(inner_kernel, n, levels), out_shape=[sha...  35.8 us
    pallas_call x1, Pallas kernels, per_device(): pl.pallas_call(functools.partial(backward_kernel, n, (groups, tiles)), ou...  24.4 us
    ppermute x3, waiting for transfers between devices, per_device(): lax.ppermute(sums[x, y], both, joint_perm(groups, tiles, lambda g, t: (g...  22.2 us
    pallas_call x1, Pallas kernels, per_device(): pl.pallas_call(functools.partial(rim_kernel, n, levels), out_shape=[*stat...  14.6 us
    ppermute x4, waiting for transfers between devices, per_device(): lax.ppermute(strips[4 + i], both, joint_perm(groups, tiles, lambda g, t:...  7.32 us
    ppermute x3, waiting for transfers between devices, per_device(): lax.ppermute(total[z], 'tile', [(t, t ^ 2 * z) for t in range(tiles)])  6.93 us
    ppermute x4, starting transfers between devices, per_device(): lax.ppermute(strips[4 + i], both, joint_perm(groups, tiles, lambda g, t:...  6.3 us
    unnamed x23, local copies, waits for them, and re-layouts  6.03 us
  transfers between devices with their start and end apart: 16, of which 8 were waited for; matrix products, arithmetic and copies ran while one was open for 4% of the time, Pallas kernels for 38%

profile of v1, /device:TPU:0, one launch (start us, length us, event | category | flops | bytes accessed | tf_op | source)
XLA Modules:
  0.0 158.6 jit_solution(9451896149627819821)
XLA Ops:
  1.3 0.0 copy-start
  1.3 1.9 %copy-done = f32[32,32,768]{2,1,0:T(8,128)S(1)} copy-done((f32[32,32,768]{2,1,0:T(8,128)S(1)}, f32[32,32,768]{2,1,0:T(8,128)}, u32[]{:S(2)}) %copy-start) | copy-done | bytes 3145752
  3.2 0.0 copy-start.10
  3.2 0.0 copy-start.9
  3.2 1.5 pack_strips.1
  4.7 3.0 %collective-permute-start = (f32[64,768]{1,0:T(8,128)S(1)}, f32[64,768]{1,0:T(8,128)S(1)}, u32[]{:S(2)}, u32[]{:S(2)}) collective-permute-start(f32[64,768]{1,0:T(8,128)S(1)} %get-tuple-element.25), channel_id=1, source_target_pairs={{0,1},{1,2},{2,3},{3,4},{4,5},{5,6},{6,7},{7,0},{8,9},{9,10},{10,1... | collective-permute-start | bytes 589832 | tf_op jit(solution)/shard_map/ppermute | solution.py:355
  7.7 0.0 collective-permute-start.1
  7.7 3.2 %collective-permute-start.2 = (f32[64,768]{1,0:T(8,128)S(1)}, f32[64,768]{1,0:T(8,128)S(1)}, u32[]{:S(2)}, u32[]{:S(2)}) collective-permute-start(f32[64,768]{1,0:T(8,128)S(1)} %get-tuple-element.27), channel_id=1, source_target_pairs={{0,7},{1,0},{2,1},{3,2},{4,3},{5,4},{6,5},{7,6},{8,15},{9,8},{10,9... | collective-permute-start | bytes 589832 | tf_op jit(solution)/shard_map/ppermute | solution.py:357
  10.9 0.0 collective-permute-start.4
  10.9 1.9 %collective-permute-start.5 = (f32[1,768]{1,0:T(1,128)S(1)}, f32[1,768]{1,0:T(1,128)S(1)}, u32[]{:S(2)}, u32[]{:S(2)}) collective-permute-start(f32[1,768]{1,0:T(1,128)S(1)} %get-tuple-element.30), channel_id=1, source_target_pairs={{0,25},{1,26},{2,27},{3,28},{4,29},{5,30},{6,31},{7,24},{8,1},{9,2... | collective-permute-start | bytes 9224 | tf_op jit(solution)/shard_map/ppermute | solution.py:361
  12.8 0.0 copy-done.10
  12.8 0.1 reshape.64
  12.9 0.0 copy-done.9
  12.9 0.7 reshape.54.dest
  13.6 4.1 %collective-permute-done.4.c_mm = f32[1,768]{1,0:T(1,128)S(1)} collective-permute-done((f32[1,768]{1,0:T(1,128)S(1)}, f32[1,768]{1,0:T(1,128)S(1)}, u32[]{:S(2)}, u32[]{:S(2)}) %collective-permute-start.4) | collective-permute-done | bytes 3104 | tf_op jit(solution)/shard_map/ppermute | solution.py:361
  17.6 0.4 collective-permute-start.3
  18.0 0.0 collective-permute-done.5.c_mp
  18.0 4.3 %collective-permute-start.6 = (f32[1,768]{1,0:T(1,128)S(1)}, f32[1,768]{1,0:T(1,128)S(1)}, u32[]{:S(2)}, u32[]{:S(2)}) collective-permute-start(f32[1,768]{1,0:T(1,128)S(1)} %get-tuple-element.31), channel_id=1, source_target_pairs={{0,31},{1,24},{2,25},{3,26},{4,27},{5,28},{6,29},{7,30},{8,7},{9,0... | collective-permute-start | bytes 9224 | tf_op jit(solution)/shard_map/ppermute | solution.py:361
  22.4 1.0 broadcast_in_dim.2.mask
  23.4 0.0 copy-start.1
  23.4 0.0 copy-start.3
  23.4 35.8 %inner_columns.1 = (f32[512,768]{1,0:T(8,128)}, f32[256,128]{1,0:T(8,128)}, bf16[3,896,768]{2,1,0:T(8,128)(2,1)}, f32[2,896,128]{2,1,0:T(8,128)}, f32[3,896,512]...) custom-call(s32[1]{0:T(128)} %bitcast.47.turn, s32[1024]{0:T(1024)} %reshape.54.dest, ...), custom_call_target="tpu_custom_call" | custom-call | flops 7046430720 | bytes 41943040 | tf_op jit(solution)/shard_map/inner_columns/pallas_call | solution.py:374
  59.2 0.0 collective-permute-done.6.c_pp
  59.2 0.1 collective-permute-start.7
  59.3 0.7 pad_add_fusion.place
  60.0 3.2 %collective-permute-done.7.c_pm = f32[1,768]{1,0:T(1,128)S(1)} collective-permute-done((f32[1,768]{1,0:T(1,128)S(1)}, f32[1,768]{1,0:T(1,128)S(1)}, u32[]{:S(2)}, u32[]{:S(2)}) %collective-permute-start.7) | collective-permute-done | bytes 3104 | tf_op jit(solution)/shard_map/ppermute | solution.py:361
  63.2 0.0 collective-permute-done.h0
  63.2 0.0 collective-permute-done.1.h1
  63.2 0.0 collective-permute-done.2.h2
  63.2 0.0 collective-permute-done.3.h3
  63.2 0.0 copy-done.1
  63.2 0.0 copy-done.3
  63.3 0.0 copy-done.5
  63.3 0.0 copy-start.4
  63.3 0.9 copy-done.4
  64.2 14.6 %rim_columns.1 = (bf16[3,256,768]{2,1,0:T(8,128)(2,1)S(1)}, f32[2,256,128]{2,1,0:T(8,128)S(1)}, f32[3,256,512]{2,1,0:T(8,128)}, bf16[3,256,512]{2,1,0:T(8,128)(2,1)S(1)}, f32[1024,512]{1,0:T(8,128)}) custom-call(s32[1]{0:T(128)} %bitcast.48.turn, s32[1024]{0:T(1024)S(1)} %copy-done.5, f32[64,768]{1,0:T(8,128)S(1)} %collective-permute-done.h0, ...), custom_call_target="tpu_custom_call" | custom-call | flops 1006632960 | bytes 20971520 | tf_op jit(solution)/shard_map/rim_columns/pallas_call | solution.py:392
  78.7 1.0 copy-done.6
  79.7 0.9 copy-done.7
  80.6 0.7 copy-done.8
  81.3 3.8 %all-to-all-start = ((f32[32,32,512]{2,1,0:T(8,128)}), f32[32,32,512]{2,1,0:T(8,128)S(1)}, u32[]{:S(2)}, u32[]{:S(2)}) async-start(f32[32,32,512]{2,1,0:T(8,128)} %bitcast.55), calls=%async_computation | async-start | bytes 4194304 | tf_op jit(solution)/shard_map/all_to_all | solution.py:407
  85.1 24.4 %columns_backward.1 = (f32[16,96,256]{2,1,0:T(8,128)}, f32[16,96,256]{2,1,0:T(8,128)}) custom-call(s32[2]{0:T(128)} %pad_add_fusion.place, s32[1]{0:T(128)} %bitcast.49.turn, f32[1024,768]{1,0:T(8,128)} %bitcast.60, f32[1024,128]{1,0:T(8,128)} %broadcast_in_dim.2.mask, f32[256,128]{1,0:T(8,128)} %get-tuple-element.34.mask_rim, bf16[768,512]{1,0:T(8,128)(2,1)} %w_in.5, ...), custom_call_target="tpu_custom_call" | custom-call | flops 8858370048 | bytes 41943040 | tf_op jit(solution)/shard_map/columns_backward/pallas_call | solution.py:414
  109.5 0.0 collective-permute-start.8
  109.6 3.6 %collective-permute-done.8 = f32[16,96,256]{2,1,0:T(8,128)S(1)} collective-permute-done((f32[16,96,256]{2,1,0:T(8,128)}, f32[16,96,256]{2,1,0:T(8,128)S(1)}, u32[]{:S(2)}, u32[]{:S(2)}) %collective-permute-start.8) | collective-permute-done | bytes 1572896 | tf_op jit(solution)/shard_map/ppermute | solution.py:433
  113.1 1.6 %add.21 = f32[16,96,256]{2,1,0:T(8,128)S(1)} add(f32[16,96,256]{2,1,0:T(8,128)} %get-tuple-element.45, f32[16,96,256]{2,1,0:T(8,128)S(1)} %collective-permute-done.8) | non-fusion elementwise | flops 393216 | bytes 4718592 | tf_op jit(solution)/shard_map/add | solution.py:433
  114.7 0.1 slice_bitcast_fusion.2
  114.8 0.0 copy-start.2
  114.8 1.6 %collective-permute-start.10 = (f32[4,96,256]{2,1,0:T(8,128)S(1)}, f32[4,96,256]{2,1,0:T(8,128)S(1)}, u32[]{:S(2)}, u32[]{:S(2)}) collective-permute-start(f32[4,96,256]{2,1,0:T(8,128)S(1)} %get-tuple-element.49), channel_id=1, source_target_pairs={{0,16},{1,17},{2,18},{3,19},{4,20},{5,21},{6,22},{7,23},{8,24},{9,... | collective-permute-start | bytes 1179656 | tf_op jit(solution)/shard_map/ppermute | solution.py:439
  116.5 1.5 collective-permute-start.11
  118.0 0.4 collective-permute-start.9
  118.4 9.7 %collective-permute-done.10 = f32[4,96,256]{2,1,0:T(8,128)S(1)} collective-permute-done((f32[4,96,256]{2,1,0:T(8,128)S(1)}, f32[4,96,256]{2,1,0:T(8,128)S(1)}, u32[]{:S(2)}, u32[]{:S(2)}) %collective-permute-start.10) | collective-permute-done | bytes 393248 | tf_op jit(solution)/shard_map/ppermute | solution.py:439
  128.1 12.2 %collective-permute-done.11 = f32[4,96,256]{2,1,0:T(8,128)S(1)} collective-permute-done((f32[4,96,256]{2,1,0:T(8,128)S(1)}, f32[4,96,256]{2,1,0:T(8,128)S(1)}, u32[]{:S(2)}, u32[]{:S(2)}) %collective-permute-start.11) | collective-permute-done | bytes 393248 | tf_op jit(solution)/shard_map/ppermute | solution.py:439
  140.4 0.2 collective-permute-done.9
  140.6 0.1 fusion.2
  140.7 3.6 %collective-permute-start.12 = (f32[96,256]{1,0:T(8,128)S(1)}, f32[96,256]{1,0:T(8,128)S(1)}, u32[]{:S(2)}, u32[]{:S(2)}) collective-permute-start(f32[96,256]{1,0:T(8,128)S(1)} %get-tuple-element.50), channel_id=1, source_target_pairs={{0,2},{1,3},{2,0},{3,1},{4,6},{5,7},{6,4},{7,5},{8,10},{9,11},{10,... | collective-permute-start | bytes 294920 | tf_op jit(solution)/shard_map/ppermute | solution.py:444
  144.3 0.7 collective-permute-start.13
  145.0 1.7 %collective-permute-start.14 = (f32[96,256]{1,0:T(8,128)S(1)}, f32[96,256]{1,0:T(8,128)S(1)}, u32[]{:S(2)}, u32[]{:S(2)}) collective-permute-start(f32[96,256]{1,0:T(8,128)S(1)} %get-tuple-element.51), channel_id=1, source_target_pairs={{0,6},{1,7},{2,4},{3,5},{4,2},{5,3},{6,0},{7,1},{8,14},{9,15},{10,... | collective-permute-start | bytes 294920 | tf_op jit(solution)/shard_map/ppermute | solution.py:444
  146.7 0.8 collective-permute-done.12
  147.5 6.2 %collective-permute-done.13 = f32[96,256]{1,0:T(8,128)S(1)} collective-permute-done((f32[96,256]{1,0:T(8,128)S(1)}, f32[96,256]{1,0:T(8,128)S(1)}, u32[]{:S(2)}, u32[]{:S(2)}) %collective-permute-start.13) | collective-permute-done | bytes 98336 | tf_op jit(solution)/shard_map/ppermute | solution.py:444
  153.7 0.0 collective-permute-done.14
  153.8 0.6 reshape.63
  154.4 0.6 copy.12
  155.1 0.0 all-to-all-done
  155.1 0.0 copy-done.2
  155.1 3.5 %tendency_rows.1 = f32[1024,768]{1,0:T(8,128)} custom-call(f32[1024,512]{1,0:T(8,128)S(1)} %bitcast.50, bf16[512,768]{1,0:T(8,128)(2,1)S(1)} %copy-done.2), custom_call_target="tpu_custom_call" | custom-call | flops 1610612736 | bytes 6291456 | tf_op jit(solution)/shard_map/tendency_rows/pallas_call | solution.py:450
  (10 shorter events, 0.1 us)
Async XLA Ops:
  1.3 1.9 %copy-start = (f32[32,32,768]{2,1,0:T(8,128)S(1)}, f32[32,32,768]{2,1,0:T(8,128)}, u32[]{:S(2)}) copy-start(f32[32,32,768]{2,1,0:T(8,128)} %air.1) | copy-start | bytes 9437188
  3.2 9.6 %copy-start.10 = (s32[32,32]{1,0:T(8,128)S(1)}, s32[32,32]{1,0:T(8,128)}, u32[]{:S(2)}) copy-start(s32[32,32]{1,0:T(8,128)} %param.9) | copy-start | bytes 12292
  3.2 9.7 %copy-start.9 = (s32[32,32]{1,0:T(8,128)S(1)}, s32[32,32]{1,0:T(8,128)}, u32[]{:S(2)}) copy-start(s32[32,32]{1,0:T(8,128)} %param.10) | copy-start | bytes 12292
  4.7 58.5 %collective-permute-start = (f32[64,768]{1,0:T(8,128)S(1)}, f32[64,768]{1,0:T(8,128)S(1)}, u32[]{:S(2)}, u32[]{:S(2)}) collective-permute-start(f32[64,768]{1,0:T(8,128)S(1)} %get-tuple-element.25), channel_id=1, source_target_pairs={{0,1},{1,2},{2,3},{3,4},{4,5},{5,6},{6,7},{7,0},{8,9},{9,10},{10,1... | collective-permute-start | bytes 589832 | tf_op jit(solution)/shard_map/ppermute | solution.py:355
  7.7 55.5 %collective-permute-start.1 = (f32[64,768]{1,0:T(8,128)S(1)}, f32[64,768]{1,0:T(8,128)S(1)}, u32[]{:S(2)}, u32[]{:S(2)}) collective-permute-start(f32[64,768]{1,0:T(8,128)S(1)} %get-tuple-element.26), channel_id=1, source_target_pairs={{0,8},{8,16},{16,24},{24,0},{1,9},{9,17},{17,25},{25,1},{2,10},{10... | collective-permute-start | bytes 589832 | tf_op jit(solution)/shard_map/ppermute | solution.py:356
  7.7 55.5 %collective-permute-start.2 = (f32[64,768]{1,0:T(8,128)S(1)}, f32[64,768]{1,0:T(8,128)S(1)}, u32[]{:S(2)}, u32[]{:S(2)}) collective-permute-start(f32[64,768]{1,0:T(8,128)S(1)} %get-tuple-element.27), channel_id=1, source_target_pairs={{0,7},{1,0},{2,1},{3,2},{4,3},{5,4},{6,5},{7,6},{8,15},{9,8},{10,9... | collective-permute-start | bytes 589832 | tf_op jit(solution)/shard_map/ppermute | solution.py:357
  10.9 6.7 %collective-permute-start.4 = (f32[1,768]{1,0:T(1,128)S(1)}, f32[1,768]{1,0:T(1,128)S(1)}, u32[]{:S(2)}, u32[]{:S(2)}) collective-permute-start(f32[1,768]{1,0:T(1,128)S(1)} %get-tuple-element.29), channel_id=1, source_target_pairs={{0,9},{1,10},{2,11},{3,12},{4,13},{5,14},{6,15},{7,8},{8,17},{9,18... | collective-permute-start | bytes 9224 | tf_op jit(solution)/shard_map/ppermute | solution.py:361
  10.9 7.1 %collective-permute-start.5 = (f32[1,768]{1,0:T(1,128)S(1)}, f32[1,768]{1,0:T(1,128)S(1)}, u32[]{:S(2)}, u32[]{:S(2)}) collective-permute-start(f32[1,768]{1,0:T(1,128)S(1)} %get-tuple-element.30), channel_id=1, source_target_pairs={{0,25},{1,26},{2,27},{3,28},{4,29},{5,30},{6,31},{7,24},{8,1},{9,2... | collective-permute-start | bytes 9224 | tf_op jit(solution)/shard_map/ppermute | solution.py:361
  17.6 45.6 %collective-permute-start.3 = (f32[64,768]{1,0:T(8,128)S(1)}, f32[64,768]{1,0:T(8,128)S(1)}, u32[]{:S(2)}, u32[]{:S(2)}) collective-permute-start(f32[64,768]{1,0:T(8,128)S(1)} %get-tuple-element.28), channel_id=1, source_target_pairs={{0,24},{8,0},{16,8},{24,16},{1,25},{9,1},{17,9},{25,17},{2,26},{10... | collective-permute-start | bytes 589832 | tf_op jit(solution)/shard_map/ppermute | solution.py:358
  18.0 41.2 %collective-permute-start.6 = (f32[1,768]{1,0:T(1,128)S(1)}, f32[1,768]{1,0:T(1,128)S(1)}, u32[]{:S(2)}, u32[]{:S(2)}) collective-permute-start(f32[1,768]{1,0:T(1,128)S(1)} %get-tuple-element.31), channel_id=1, source_target_pairs={{0,31},{1,24},{2,25},{3,26},{4,27},{5,28},{6,29},{7,30},{8,7},{9,0... | collective-permute-start | bytes 9224 | tf_op jit(solution)/shard_map/ppermute | solution.py:361
  23.4 39.9 %copy-start.1 = (bf16[512,768]{1,0:T(8,128)(2,1)S(1)}, bf16[512,768]{1,0:T(8,128)(2,1)}, u32[]{:S(2)}) copy-start(bf16[512,768]{1,0:T(8,128)(2,1)} %w_out.7) | copy-start | bytes 2359300
  23.4 39.9 %copy-start.3 = (bf16[768,512]{1,0:T(8,128)(2,1)S(1)}, bf16[768,512]{1,0:T(8,128)(2,1)}, u32[]{:S(2)}) copy-start(bf16[768,512]{1,0:T(8,128)(2,1)} %w_in.5) | copy-start | bytes 2359300
  23.4 39.9 %copy-start.5 = (s32[1024]{0:T(1024)S(1)}, s32[1024]{0:T(1024)}, u32[]{:S(2)}) copy-start(s32[1024]{0:T(1024)} %reshape.54.dest) | copy-start | bytes 12292
  59.2 4.0 %collective-permute-start.7 = (f32[1,768]{1,0:T(1,128)S(1)}, f32[1,768]{1,0:T(1,128)S(1)}, u32[]{:S(2)}, u32[]{:S(2)}) collective-permute-start(f32[1,768]{1,0:T(1,128)S(1)} %get-tuple-element.32), channel_id=1, source_target_pairs={{0,15},{1,8},{2,9},{3,10},{4,11},{5,12},{6,13},{7,14},{8,23},{9,16... | collective-permute-start | bytes 9224 | tf_op jit(solution)/shard_map/ppermute | solution.py:361
  63.3 0.9 copy-start.4
  78.7 1.0 copy-start.6
  79.7 0.9 copy-start.7
  80.6 0.7 copy-start.8
  81.3 73.8 %all-to-all-start = ((f32[32,32,512]{2,1,0:T(8,128)}), f32[32,32,512]{2,1,0:T(8,128)S(1)}, u32[]{:S(2)}, u32[]{:S(2)}) async-start(f32[32,32,512]{2,1,0:T(8,128)} %bitcast.55), calls=%async_computation | async-start | bytes 4194304 | tf_op jit(solution)/shard_map/all_to_all | solution.py:407
  109.5 3.6 %collective-permute-start.8 = (f32[16,96,256]{2,1,0:T(8,128)}, f32[16,96,256]{2,1,0:T(8,128)S(1)}, u32[]{:S(2)}, u32[]{:S(2)}) collective-permute-start(f32[16,96,256]{2,1,0:T(8,128)} %get-tuple-element.46), channel_id=1, source_target_pairs={{0,8},{8,0},{16,24},{24,16},{1,9},{9,1},{17,25},{25,17},{2,10},{10... | collective-permute-start | bytes 4718600 | tf_op jit(solution)/shard_map/ppermute | solution.py:433
  114.8 40.2 %copy-start.2 = (bf16[512,768]{1,0:T(8,128)(2,1)S(1)}, bf16[512,768]{1,0:T(8,128)(2,1)}, u32[]{:S(2)}) copy-start(bf16[512,768]{1,0:T(8,128)(2,1)} %w_out.7) | copy-start | bytes 2359300
  114.8 13.3 %collective-permute-start.10 = (f32[4,96,256]{2,1,0:T(8,128)S(1)}, f32[4,96,256]{2,1,0:T(8,128)S(1)}, u32[]{:S(2)}, u32[]{:S(2)}) collective-permute-start(f32[4,96,256]{2,1,0:T(8,128)S(1)} %get-tuple-element.49), channel_id=1, source_target_pairs={{0,16},{1,17},{2,18},{3,19},{4,20},{5,21},{6,22},{7,23},{8,24},{9,... | collective-permute-start | bytes 1179656 | tf_op jit(solution)/shard_map/ppermute | solution.py:439
  116.5 23.9 %collective-permute-start.11 = (f32[4,96,256]{2,1,0:T(8,128)S(1)}, f32[4,96,256]{2,1,0:T(8,128)S(1)}, u32[]{:S(2)}, u32[]{:S(2)}) collective-permute-start(f32[4,96,256]{2,1,0:T(8,128)S(1)} %get-tuple-element.48), channel_id=1, source_target_pairs={{0,17},{1,16},{2,19},{3,18},{4,21},{5,20},{6,23},{7,22},{8,25},{9,... | collective-permute-start | bytes 1179656 | tf_op jit(solution)/shard_map/ppermute | solution.py:439
  118.0 22.6 %collective-permute-start.9 = (f32[4,96,256]{2,1,0:T(8,128)S(1)}, f32[4,96,256]{2,1,0:T(8,128)S(1)}, u32[]{:S(2)}, u32[]{:S(2)}) collective-permute-start(f32[4,96,256]{2,1,0:T(8,128)S(1)} %get-tuple-element.47), channel_id=1, source_target_pairs={{0,1},{1,0},{2,3},{3,2},{4,5},{5,4},{6,7},{7,6},{8,9},{9,8},{10,11... | collective-permute-start | bytes 1179656 | tf_op jit(solution)/shard_map/ppermute | solution.py:439
  140.7 6.8 %collective-permute-start.12 = (f32[96,256]{1,0:T(8,128)S(1)}, f32[96,256]{1,0:T(8,128)S(1)}, u32[]{:S(2)}, u32[]{:S(2)}) collective-permute-start(f32[96,256]{1,0:T(8,128)S(1)} %get-tuple-element.50), channel_id=1, source_target_pairs={{0,2},{1,3},{2,0},{3,1},{4,6},{5,7},{6,4},{7,5},{8,10},{9,11},{10,... | collective-permute-start | bytes 294920 | tf_op jit(solution)/shard_map/ppermute | solution.py:444
  144.3 9.4 %collective-permute-start.13 = (f32[96,256]{1,0:T(8,128)S(1)}, f32[96,256]{1,0:T(8,128)S(1)}, u32[]{:S(2)}, u32[]{:S(2)}) collective-permute-start(f32[96,256]{1,0:T(8,128)S(1)} %get-tuple-element.52), channel_id=1, source_target_pairs={{0,4},{1,5},{2,6},{3,7},{4,0},{5,1},{6,2},{7,3},{8,12},{9,13},{10,... | collective-permute-start | bytes 294920 | tf_op jit(solution)/shard_map/ppermute | solution.py:444
  145.0 8.7 %collective-permute-start.14 = (f32[96,256]{1,0:T(8,128)S(1)}, f32[96,256]{1,0:T(8,128)S(1)}, u32[]{:S(2)}, u32[]{:S(2)}) collective-permute-start(f32[96,256]{1,0:T(8,128)S(1)} %get-tuple-element.51), channel_id=1, source_target_pairs={{0,6},{1,7},{2,4},{3,5},{4,2},{5,3},{6,0},{7,1},{8,14},{9,15},{10,... | collective-permute-start | bytes 294920 | tf_op jit(solution)/shard_map/ppermute | solution.py:444

commit v2 on v1

--- a/solution.py
+++ b/solution.py
@@ -26,8 +26,13 @@
 
 def side_cells(k, n):
     pick = lambda a, b, c, e: jnp.where(k == 0, a, jnp.where(k == 1, b, jnp.where(k == 2, c, e)))
-    base = pick(0, (n - 1) * n, n * n - 1, n - 1)
-    return base, pick(1, -n, -1, n), pick(n, 1, -n, -1)
+    return (pick(0, n - 1, n - 1, 0), pick(1, 0, -1, 0), pick(0, -1, 0, 1)), (
+        pick(0, 0, n - 1, n - 1), pick(0, 1, 0, -1), pick(1, 0, -1, 0))
+
+
+def side_rows(k, n):
+    (bi, di, mi), (bj, dj, mj) = side_cells(k, n)
+    return bi * n + bj, mi * n + mj, di * n + dj
 
 
 def turn_winds(ref, rows, quarter, levels):
@@ -84,37 +89,37 @@
     size, feats = src.shape[1], src.shape[2]
     chunks = feats // LANES
     period = face_lead.shape[2] // LANES
-
-    def faces(a, carry):
-        here, there = wind_row(src, a, lead, levels), wind_row(src, a + 1, lead, levels)
-        for c, part in enumerate(repeat_levels((0.5 * lead_sign) * (here + there), levels, period)):
-            face_lead[a, :, c * LANES : (c + 1) * LANES] = part
-        here = wind_row(src, a, sub, levels)
-        ahead = pltpu.roll(here, size - 1, 0)
-        for c, part in enumerate(repeat_levels((0.5 * sub_sign) * (here + ahead), levels, period)):
-            face_sub[a, :, c * LANES : (c + 1) * LANES] = part
-        return carry
-
-    lax.fori_loop(lo - 1, hi, faces, 0)
-
-    def update(a, carry):
+    block = next(b for b in range(face_sub.shape[0], 0, -1) if (hi - lo) % b == 0)
+
+    def store(ref, at, face):
+        for c, part in enumerate(repeat_levels(face, levels, period)):
+            ref[at, :, c * LANES : (c + 1) * LANES] = part
+
+    def body(b, carry):
+        first = lo + b * block
+        for r in range(block + 1):
+            wind = wind_row(src, first - 1 + r, lead, levels) + wind_row(src, first + r, lead, levels)
+            store(face_lead, r, (0.5 * COURANT * lead_sign) * wind)
+        for r in range(block):
+            wind = wind_row(src, first + r, sub, levels)
+            store(face_sub, r, (0.5 * COURANT * sub_sign) * (wind + pltpu.roll(wind, size - 1, 0)))
         for c3 in range(period):
             lanes3 = slice(c3 * LANES, (c3 + 1) * LANES)
-            high, low, side = face_lead[a, :, lanes3], face_lead[a - 1, :, lanes3], face_sub[a, :, lanes3]
-            high_p, high_m = jnp.maximum(high, 0.0), jnp.minimum(high, 0.0)
-            low_p, low_m = jnp.maximum(low, 0.0), jnp.minimum(low, 0.0)
-            side_p, side_m = jnp.maximum(side, 0.0), jnp.minimum(side, 0.0)
-            for c in range(c3, chunks, period):
-                lanes = slice(c * LANES, (c + 1) * LANES)
-                q = src[a, :, lanes]
-                flux_high = high_p * q + high_m * src[a + 1, :, lanes]
-                flux_low = low_p * src[a - 1, :, lanes] + low_m * q
-                flux_side = side_p * q + side_m * pltpu.roll(q, size - 1, 0)
-                flux_back = pltpu.roll(flux_side, 1, 0)
-                dst[a, :, lanes] = q - COURANT * ((flux_high - flux_low) + (flux_side - flux_back))
+            group = [slice(c * LANES, (c + 1) * LANES) for c in range(c3, chunks, period)]
+            face = face_lead[0, :, lanes3]
+            q = [src[first, :, lanes] for lanes in group]
+            before = [face * jnp.where(face > 0.0, src[first - 1, :, lanes], here) for lanes, here in zip(group, q)]
+            for r in range(block):
+                face, side = face_lead[r + 1, :, lanes3], face_sub[r, :, lanes3]
+                for i, lanes in enumerate(group):
+                    ahead = src[first + r + 1, :, lanes]
+                    flux = face * jnp.where(face > 0.0, q[i], ahead)
+                    cross = side * jnp.where(side > 0.0, q[i], pltpu.roll(q[i], size - 1, 0))
+                    dst[first + r, :, lanes] = q[i] - ((flux - before[i]) + (cross - pltpu.roll(cross, 1, 0)))
+                    q[i], before[i] = ahead, flux
         return carry
 
-    lax.fori_loop(lo, hi, update, 0)
+    lax.fori_loop(0, (hi - lo) // block, body, 0)
 
 
 def network_forward(x, mask, w_in, w_out, normed, scale, slope, hidden, hsum, rows):
@@ -138,48 +143,45 @@
             hsum[rows, :] = total + h.astype(F32) * mask
 
 
-def pack_kernel(n, levels, turn, air, s0, s1, s2, s3, c0, c1, c2, c3):
-    o = turn[0]
-    for k, out in enumerate((s0, s1, s2, s3)):
-        base, cm, cd = side_cells((k - o + 4) % 4, n)
-        for d in range(2):
-            copy_rows(out, d * n, air, base + cd * d + cm * (n - 1), -cm, n)
-        turn_winds(out, (0, 2 * n), o, levels)
-    c0[...] = s2[n - 1 : n, :]
-    c1[...] = s2[0:1, :]
-    c2[...] = s0[n - 1 : n, :]
-    c3[...] = s0[0:1, :]
-
-
-def inner_kernel(n, levels, turn, dest, air, air_rows, mask, w_in, w_out,
-                 own, mask_rim, normed, scale, slope, hidden, outgoing,
-                 q_one, q_two, face_lead, face_sub, hsum):
-    o = turn[0]
+def pack_strip(n, levels, k, o, air, out):
+    base, cm, cd = side_rows((k - o + 4) % 4, n)
+    for d in range(2):
+        copy_rows(out, d * n, air, base + cd * d + cm * (n - 1), -cm, n)
+    turn_winds(out, (0, 2 * n), o, levels)
+
+
+def pack_kernel(n, levels, turn, air, s1, s3):
+    pack_strip(n, levels, 1, turn[0, 0], air, s1)
+    pack_strip(n, levels, 3, turn[0, 0], air, s3)
+
+
+def pack_with_corners_kernel(n, levels, turn, air, h1, h3, order, s0, s2):
+    del order
+    pack_strip(n, levels, 0, turn[0, 0], air, s0)
+    pack_strip(n, levels, 2, turn[0, 0], air, s2)
+    s0[2 * n : 2 * n + 1, :] = h1[n - 1 : n, :]
+    s0[2 * n + 1 : 2 * n + 2, :] = h3[0:1, :]
+    s2[2 * n : 2 * n + 1, :] = h1[0:1, :]
+    s2[2 * n + 1 : 2 * n + 2, :] = h3[n - 1 : n, :]
+
+
+def inner_transport_kernel(n, levels, turn, cost, air_rows, moved, own, mask, mask_rim, q_one, face_lead, face_sub):
+    o = turn[0, 0]
+    air = air_rows.reshape(n, n, air_rows.shape[1])
     winds = ((0, 1.0), (1, 1.0))
     transport(air, q_one, face_lead, face_sub, 1, n - 1, winds, levels)
-    transport(q_one, q_two, face_lead, face_sub, 2, n - 2, winds, levels)
-    inner = n - 4
-    parts = 2
-    size = inner // parts * n
-    feats = air.shape[2]
-
-    def chunk(part, carry):
-        rows = pl.ds(pl.multiple_of(part * size, size), size)
-        x = q_two[pl.ds(2 + part * (inner // parts), inner // parts), :, :].reshape(size, feats)
-        m = mask[pl.ds(pl.multiple_of(2 * n + part * size, 8), size), 0:1]
-        network_forward(x, m, w_in[...], w_out[...], normed, scale, slope, hidden, hsum, rows)
+    transport(q_one, moved, face_lead, face_sub, 2, n - 2, winds, levels)
+    diagonal = lax.broadcasted_iota(jnp.int32, (n, n), 0) == lax.broadcasted_iota(jnp.int32, (n, n), 1)
+
+    def mask_row(i, carry):
+        two = jnp.broadcast_to((cost[pl.ds(i, 1), :] == 2).astype(F32), (n, n))
+        column = jnp.sum(jnp.where(diagonal, two, 0.0), axis=1, keepdims=True)
+        mask[pl.ds(pl.multiple_of(i * n, 8), n), :] = jnp.broadcast_to(column, (n, LANES))
         return carry
 
-    lax.fori_loop(0, parts, chunk, 0)
-
-    def place(i, carry):
-        for j in range(2, n - 2):
-            outgoing[pl.ds(dest[i * n + j], 1), :] = hsum[pl.ds((i - 2) * n + j, 1), :]
-        return carry
-
-    lax.fori_loop(2, n - 2, place, 0)
+    lax.fori_loop(0, n, mask_row, 0, unroll=8)
     for k in range(4):
-        base, cm, cd = side_cells((k - o + 4) % 4, n)
+        base, cm, cd = side_rows((k - o + 4) % 4, n)
         for d in range(4):
             copy_rows(own, (k * 4 + d) * n, air_rows, base + cd * d, cm, n)
         for d in range(2):
@@ -187,11 +189,34 @@
         turn_winds(own, (k * 4 * n, 4 * n), o, levels)
 
 
-def rim_kernel(n, levels, turn, dest, h0, h1, h2, h3, c_mm, c_mp, c_pp, c_pm, own, mask_rim, w_in, w_out, before,
+def inner_network_kernel(n, dest, moved, mask, w_in, w_out, normed, scale, slope, hidden, outgoing, hsum):
+    inner = n - 4
+    parts = 2
+    size = inner // parts * n
+    feats = moved.shape[2]
+
+    def chunk(part, carry):
+        rows = pl.ds(pl.multiple_of(part * size, size), size)
+        x = moved[pl.ds(2 + part * (inner // parts), inner // parts), :, :].reshape(size, feats)
+        m = mask[pl.ds(pl.multiple_of(2 * n + part * size, 8), size), 0:1]
+        network_forward(x, m, w_in[...], w_out[...], normed, scale, slope, hidden, hsum, rows)
+        return carry
+
+    lax.fori_loop(0, parts, chunk, 0)
+
+    def place(i, carry):
+        for j in range(2, n - 2):
+            outgoing[pl.ds(dest[i, j], 1), :] = hsum[pl.ds((i - 2) * n + j, 1), :]
+        return carry
+
+    lax.fori_loop(2, n - 2, place, 0)
+
+
+def rim_kernel(n, levels, turn, dest, h0, h1, h2, h3, own, mask_rim, w_in, w_out, before,
                normed, scale, slope, hidden, outgoing,
                wide, wide_one, wide_two, slim, slim_one, slim_two, lead_wide, sub_wide, lead_slim, sub_slim, x_rim, hsum):
     outgoing[...] = before[...]
-    o = turn[0]
+    o = turn[0, 0]
     halo = (h0, h1, h2, h3)
     for k in range(4):
         ends = k % 2 == 0
@@ -204,11 +229,12 @@
             if ends:
                 src[depth, n + 2 : n + 8, :] = row[0:6, :]
                 src[depth, n + 8 : n + 14, :] = row[n - 6 : n, :]
-                first, last = (c_mm, c_mp) if k == 0 else (c_pp, c_pm)
                 for e in range(2):
                     if d < 0:
-                        src[depth, n + 1 - e : n + 2 - e, :] = first[...]
-                        src[depth, n + 14 + e : n + 15 + e, :] = last[...]
+                        at = 2 * n + k // 2
+                        src[depth, n + 1 - e : n + 2 - e, :] = halo[k][at : at + 1, :]
+                        at = 2 * n + 1 - k // 2
+                        src[depth, n + 14 + e : n + 15 + e, :] = halo[k][at : at + 1, :]
                     else:
                         at = e * n + n - 1 - d
                         src[depth, n + 1 - e : n + 2 - e, :] = halo[(k + 1) % 4][at : at + 1, :]
@@ -226,12 +252,13 @@
     network_forward(x_rim[...], mask_rim[:, 0:1], w_in[...], w_out[...], normed, scale, slope, hidden, hsum,
                     slice(0, 8 * n))
     for k in range(4):
-        base, cm, cd = side_cells((k - o + 4) % 4, n)
+        (bi, di, mi), (bj, dj, mj) = side_cells((k - o + 4) % 4, n)
         skip = 2 * (k % 2)
         for d in range(2):
             for m in range(skip, n - skip):
                 at = (k * 2 + d) * n + m
-                outgoing[pl.ds(dest[base + cd * d + cm * m], 1), :] = hsum[at : at + 1, :]
+                row = dest[bi + di * d + mi * m, bj + dj * d + mj * m]
+                outgoing[pl.ds(row, 1), :] = hsum[at : at + 1, :]
 
 
 def contract_rows(a, b):
@@ -258,12 +285,12 @@
 
 def backward_kernel(n, grid_shape, place, turn, cot, mask, mask_rim, w_in, w_out, n_i, s_i, g_i, h_i, n_r, s_r, g_r, h_r,
                     keep, send, eo_i, ei_i, eo_r, ei_r, cot_rim, grad_in, grad_out):
-    o = turn[0]
+    o = turn[0, 0]
     inner = n - 4
     parts = 2
     size = inner // parts * n
     for k in range(4):
-        base, cm, cd = side_cells((k - o + 4) % 4, n)
+        base, cm, cd = side_rows((k - o + 4) % 4, n)
         for d in range(2):
             copy_rows(cot_rim, (k * 2 + d) * n, cot, base + cd * d, cm, n)
 
@@ -335,74 +362,90 @@
     period = next(c for c in range(1, feats // LANES + 1) if c * LANES % levels == 0)
     shape = jax.ShapeDtypeStruct
 
-    turn = orientation.reshape(1)
-    dest = assignment.reshape(cells)
     air_rows = air_state.reshape(cells, feats)
     cot_rows = cotangent.reshape(cells, feats)
-    mask = jnp.broadcast_to((cost_count.reshape(cells, 1) == 2).astype(F32), (cells, LANES))
+    both = ("grp", "tile")
+
+    def state(rows):
+        return [
+            pltpu.VMEM((3, rows, feats), BF16),
+            pltpu.VMEM((2, rows, LANES), F32),
+            pltpu.VMEM((3, rows, units), F32),
+            pltpu.VMEM((3, rows, units), BF16),
+        ]
 
     strips = pl.pallas_call(
         functools.partial(pack_kernel, n, levels),
-        out_shape=[shape((2 * n, feats), F32)] * 4 + [shape((1, feats), F32)] * 4,
+        out_shape=[shape((2 * n, feats), F32)] * 2,
         in_specs=[SMEM, VMEM],
-        out_specs=[VMEM] * 8,
-        compiler_params=params(32),
+        out_specs=[VMEM] * 2,
+        compiler_params=params(8),
         name="pack_strips",
-    )(turn, air_rows)
-
-    both = ("grp", "tile")
-    halo = [
-        lax.ppermute(strips[2], "tile", shift_perm(tiles, 1)),
-        lax.ppermute(strips[3], "grp", shift_perm(groups, 1)),
-        lax.ppermute(strips[0], "tile", shift_perm(tiles, -1)),
-        lax.ppermute(strips[1], "grp", shift_perm(groups, -1)),
-    ]
-    corners = [
-        lax.ppermute(strips[4 + i], both, joint_perm(groups, tiles, lambda g, t: ((g + dg) % groups, (t + dt) % tiles)))
-        for i, (dt, dg) in enumerate(((1, 1), (1, -1), (-1, -1), (-1, 1)))
-    ]
-
-    def state(rows):
-        return [
-            shape((3, rows, feats), BF16),
-            shape((2, rows, LANES), F32),
-            shape((3, rows, units), F32),
-            shape((3, rows, units), BF16),
-        ]
-
-    flops = 10 * inner * feats * units
-    own, mask_rim, *saved_inner, outgoing = pl.pallas_call(
-        functools.partial(inner_kernel, n, levels),
-        out_shape=[shape((16 * n, feats), F32), shape((rim, LANES), F32), *state(inner), shape((cells, units), F32)],
-        in_specs=[SMEM, SMEM] + [VMEM] * 5,
-        out_specs=[VMEM] * 7,
+    )(orientation, air_rows)
+    from_left = lax.ppermute(strips[1], "grp", shift_perm(groups, 1))
+    from_right = lax.ppermute(strips[0], "grp", shift_perm(groups, -1))
+
+    moved, own, mask, mask_rim = pl.pallas_call(
+        functools.partial(inner_transport_kernel, n, levels),
+        out_shape=[
+            pltpu.VMEM((n, n, feats), F32),
+            pltpu.VMEM((16 * n, feats), F32),
+            pltpu.VMEM((cells, LANES), F32),
+            pltpu.VMEM((rim, LANES), F32),
+        ],
+        in_specs=[SMEM] + [VMEM] * 2,
+        out_specs=[VMEM] * 4,
         scratch_shapes=[
             pltpu.VMEM((n, n, feats), F32),
-            pltpu.VMEM((n, n, feats), F32),
-            pltpu.VMEM((n, n, period * LANES), F32),
-            pltpu.VMEM((n, n, period * LANES), F32),
-            pltpu.VMEM((inner, units), F32),
+            pltpu.VMEM((8, n, period * LANES), F32),
+            pltpu.VMEM((7, n, period * LANES), F32),
         ],
-        compiler_params=params(56),
-        cost_estimate=pl.CostEstimate(flops=flops * 2, bytes_accessed=40 << 20, transcendentals=0),
-        name="inner_columns",
-    )(turn, dest, air_state, air_rows, mask, weight_in, weight_out)
+        compiler_params=params(20),
+        cost_estimate=pl.CostEstimate(flops=60 * cells * feats, bytes_accessed=16 << 20, transcendentals=0),
+        name="inner_transport",
+    )(orientation, cost_count, air_rows)
+
+    strips = pl.pallas_call(
+        functools.partial(pack_with_corners_kernel, n, levels),
+        out_shape=[shape((2 * n + 8, feats), F32)] * 2,
+        in_specs=[SMEM] + [VMEM] * 4,
+        out_specs=[VMEM] * 2,
+        compiler_params=params(8),
+        name="pack_strips_corners",
+    )(orientation, air_rows, from_left, from_right, mask_rim)
+    from_above = lax.ppermute(strips[1], "tile", shift_perm(tiles, 1))
+    from_below = lax.ppermute(strips[0], "tile", shift_perm(tiles, -1))
+
+    *saved_inner, outgoing = pl.pallas_call(
+        functools.partial(inner_network_kernel, n),
+        out_shape=[*state(inner), pltpu.VMEM((cells, units), F32)],
+        in_specs=[SMEM] + [VMEM] * 4,
+        out_specs=[VMEM] * 5,
+        scratch_shapes=[pltpu.VMEM((inner, units), F32)],
+        compiler_params=params(16),
+        cost_estimate=pl.CostEstimate(
+            flops=10 * inner * feats * units, bytes_accessed=16 << 20, transcendentals=3 * inner * units
+        ),
+        name="inner_network",
+    )(assignment, moved, mask, weight_in, weight_out)
 
     wide, slim = n + 16, n
     *saved_rim, outgoing = pl.pallas_call(
         functools.partial(rim_kernel, n, levels),
         out_shape=[*state(rim), shape((cells, units), F32)],
-        in_specs=[SMEM, SMEM] + [VMEM] * 13,
+        in_specs=[SMEM, SMEM] + [VMEM] * 9,
         out_specs=[VMEM] * 5,
         scratch_shapes=[pltpu.VMEM((6, wide, feats), F32)] * 3
         + [pltpu.VMEM((6, slim, feats), F32)] * 3
-        + [pltpu.VMEM((6, wide, period * LANES), F32)] * 2
-        + [pltpu.VMEM((6, slim, period * LANES), F32)] * 2
+        + [pltpu.VMEM((5, wide, period * LANES), F32), pltpu.VMEM((4, wide, period * LANES), F32)]
+        + [pltpu.VMEM((5, slim, period * LANES), F32), pltpu.VMEM((4, slim, period * LANES), F32)]
         + [pltpu.VMEM((rim, feats), F32), pltpu.VMEM((rim, units), F32)],
-        compiler_params=params(48),
-        cost_estimate=pl.CostEstimate(flops=10 * rim * feats * units, bytes_accessed=20 << 20, transcendentals=0),
+        compiler_params=params(16),
+        cost_estimate=pl.CostEstimate(
+            flops=10 * rim * feats * units, bytes_accessed=20 << 20, transcendentals=3 * rim * units
+        ),
         name="rim_columns",
-    )(turn, dest, *halo, *corners, own, mask_rim, weight_in, weight_out, outgoing)
+    )(orientation, assignment, from_above, from_left, from_below, from_right, own, mask_rim, weight_in, weight_out, outgoing)
 
     arrived = lax.all_to_all(
         outgoing.reshape(count, cells // count, units), both, split_axis=0, concat_axis=0, tiled=True
@@ -425,10 +468,10 @@
             pltpu.VMEM((feats, units), F32),
             pltpu.VMEM((units, feats), F32),
         ],
-        compiler_params=params(60),
+        compiler_params=params(36),
         cost_estimate=pl.CostEstimate(flops=22 * cells * feats * units, bytes_accessed=40 << 20, transcendentals=0),
         name="columns_backward",
-    )(place, turn, cot_rows, mask, mask_rim, weight_in, weight_out, *saved_inner, *saved_rim)
+    )(place, orientation, cot_rows, mask, mask_rim, weight_in, weight_out, *saved_inner, *saved_rim)
 
     sums = keep + lax.ppermute(send, "grp", [(i, i ^ 1) for i in range(groups)])
     sums = sums.reshape(groups // 2, 2, tiles // 2, piece, COL)

time: 159 us -> 134 us (0.84)
  Pallas kernels: 79.9 us -> 50.8 us
  local copies, waits for them, and re-layouts: 8.59 us -> 29.5 us
  waiting for transfers between devices: 40 us -> 31.3 us
  starting transfers between devices: 26.3 us -> 19.5 us
  other arithmetic: 2.42 us -> 0.43 us
    unnamed x23 -> x57, local copies, waits for them, and re-layouts: 6.03 us -> 28.7 us
    pallas_call x1 -> x3, Pallas kernels: 35.8 us -> 20.9 us  [the longest x1 10 us: per_device(): pl.pallas_call(functools.partial(inner_network_kernel, n), out_shape=[*st...]
    pallas_call x1, Pallas kernels: 14.6 us -> 6.37 us  [per_device(): pl.pallas_call(functools.partial(rim_kernel, n, levels), out_shape=[*stat...]
    ppermute x8 -> x4, waiting for transfers between devices: 7.33 us -> 0.01 us  [the longest x1 0.01 us: per_device(): from_left = lax.ppermute(strips[1], 'grp', shift_perm(groups, 1))]
    pallas_call x1, Pallas kernels: 24.4 us -> 19.3 us  [per_device(): pl.pallas_call(functools.partial(backward_kernel, n, (groups, tiles)), ou...]
    ppermute x8 -> x4, starting transfers between devices: 12.9 us -> 7.81 us  [the longest x1 3.04 us: per_device(): from_below = lax.ppermute(strips[0], 'tile', shift_perm(tiles, -1))]
  transfers between devices with their start and end apart: 16 -> 12, of which waited for: 8 -> 5; matrix products, arithmetic and copies ran while one was open for 4% -> 1% of each run, Pallas kernels for 38% -> 29%
where the time goes in v2:
time: 134 us; the launch traced here: 133 us
  Pallas kernels  50.8 us (38%)
  waiting for transfers between devices  31.3 us (23%)
  local copies, waits for them, and re-layouts  29.5 us (22%)
  starting transfers between devices  19.5 us (15%)
  between operations  1.52 us (1%)
    unnamed x57, local copies, waits for them, and re-layouts  28.7 us
    ppermute x3, waiting for transfers between devices, per_device(): lax.ppermute(sums[x, y], both, joint_perm(groups, tiles, lambda g, t: (g...  20.9 us
    pallas_call x1, Pallas kernels, per_device(): pl.pallas_call(functools.partial(backward_kernel, n, (groups, tiles)), ou...  19.3 us
    pallas_call x1, Pallas kernels, per_device(): pl.pallas_call(functools.partial(inner_network_kernel, n), out_shape=[*st...  10 us
    pallas_call x1, Pallas kernels, per_device(): pl.pallas_call(functools.partial(inner_transport_kernel, n, levels), out_...  9.39 us
    ppermute x3, waiting for transfers between devices, per_device(): lax.ppermute(total[z], 'tile', [(t, t ^ 2 * z) for t in range(tiles)])  7.09 us
    pallas_call x1, Pallas kernels, per_device(): pl.pallas_call(functools.partial(rim_kernel, n, levels), out_shape=[*stat...  6.37 us
    ppermute x3, starting transfers between devices, per_device(): lax.ppermute(total[z], 'tile', [(t, t ^ 2 * z) for t in range(tiles)])  4.45 us
  transfers between devices with their start and end apart: 12, of which 5 were waited for; matrix products, arithmetic and copies ran while one was open for 1% of the time, Pallas kernels for 29%

profile of v2, /device:TPU:0, one launch (start us, length us, event | category | flops | bytes accessed | tf_op | source)
XLA Modules:
  0.0 133.0 jit_solution(18157510551054294691)
XLA Ops:
  1.3 0.0 copy-start
  1.3 1.9 %copy-done = f32[32,32,768]{2,1,0:T(8,128)S(1)} copy-done((f32[32,32,768]{2,1,0:T(8,128)S(1)}, f32[32,32,768]{2,1,0:T(8,128)}, u32[]{:S(2)}) %copy-start) | copy-done | bytes 3145752
  3.2 0.8 pack_strips.1
  3.9 0.5 collective-permute-start
  4.4 2.0 %collective-permute-start.1 = (f32[64,768]{1,0:T(8,128)S(1)}, f32[64,768]{1,0:T(8,128)S(1)}, u32[]{:S(2)}, u32[]{:S(2)}) collective-permute-start(f32[64,768]{1,0:T(8,128)S(1)} %get-tuple-element.24), channel_id=1, source_target_pairs={{0,24},{8,0},{16,8},{24,16},{1,25},{9,1},{17,9},{25,17},{2,26},{10... | collective-permute-start | bytes 589832 | tf_op jit(solution)/shard_map/ppermute | solution.py:386
  6.4 0.0 copy-done.1
  6.4 0.7 copy-done.9
  7.2 9.4 %inner_transport.1 = (f32[32,32,768]{2,1,0:T(8,128)S(1)}, f32[512,768]{1,0:T(8,128)S(1)}, f32[1024,128]{1,0:T(8,128)S(1)}, f32[256,128]{1,0:T(8,128)S(1)}) custom-call(s32[1,1]{1,0:T(1,128)S(6)} %copy.15.turn, s32[32,32]{1,0:T(8,128)S(1)} %copy-done.9, f32[1024,768]{1,0:T(8,128)S(1)} %bitcast.46), custom_call_target="tpu_custom_call" | custom-call | flops 47185920 | bytes 16777216 | tf_op jit(solution)/shard_map/inner_transport/pallas_call | solution.py:388
  16.6 0.0 copy-start.2
  16.6 0.0 copy-start.6
  16.6 0.0 copy-start.10
  16.6 0.0 collective-permute-done.h1
  16.6 0.0 collective-permute-done.1.h3
  16.6 1.5 %pack_strips_corners.1 = (f32[72,768]{1,0:T(8,128)}, f32[72,768]{1,0:T(8,128)}) custom-call(s32[1,1]{1,0:T(1,128)S(6)} %copy.15.turn, f32[1024,768]{1,0:T(8,128)S(1)} %bitcast.47, f32[64,768]{1,0:T(8,128)S(1)} %collective-permute-done.h1, f32[64,768]{1,0:T(8,128)S(1)} %collective-permute-done.1.h3, f32[256,128]{1,0:T(8,128)S(1)} %get-tuple-element.25.order.mask_rim), custom_call_target="tpu_custom_call" | custom-call | tf_op jit(solution)/shard_map/pack_strips_corners/pallas_call | solution.py:408
  18.1 2.3 %collective-permute-start.2 = (f32[72,768]{1,0:T(8,128)}, f32[72,768]{1,0:T(8,128)}, u32[]{:S(2)}, u32[]{:S(2)}) collective-permute-start(f32[72,768]{1,0:T(8,128)} %get-tuple-element.26), channel_id=1, source_target_pairs={{0,1},{1,2},{2,3},{3,4},{4,5},{5,6},{6,7},{7,0},{8,9},{9,10},{10,1... | collective-permute-start | bytes 663560 | tf_op jit(solution)/shard_map/ppermute | solution.py:416
  20.4 3.0 %collective-permute-start.3 = (f32[72,768]{1,0:T(8,128)}, f32[72,768]{1,0:T(8,128)}, u32[]{:S(2)}, u32[]{:S(2)}) collective-permute-start(f32[72,768]{1,0:T(8,128)} %get-tuple-element.27), channel_id=1, source_target_pairs={{0,7},{1,0},{2,1},{3,2},{4,3},{5,4},{6,5},{7,6},{8,15},{9,8},{10,9... | collective-permute-start | bytes 663560 | tf_op jit(solution)/shard_map/ppermute | solution.py:417
  23.4 10.0 %inner_network.1 = (bf16[3,896,768]{2,1,0:T(8,128)(2,1)S(1)}, f32[2,896,128]{2,1,0:T(8,128)S(1)}, f32[3,896,512]{2,1,0:T(8,128)S(1)}, bf16[3,896,512]{2,1,0:T(8,128)(2,1)S(1)}, f32[1024,512]{1,0:T(8,128)S(1)}) custom-call(s32[32,32]{1,0:T(8,128)S(1)} %copy-done.10, f32[32,32,768]{2,1,0:T(8,128)S(1)} %get-tuple-element.29.moved, ...), custom_call_target="tpu_custom_call" | custom-call | flops 3523215360 | bytes 16777216 | tf_op jit(solution)/shard_map/inner_network/pallas_call | solution.py:419
  33.5 2.4 %copy-done.22 = f32[3,896,512]{2,1,0:T(8,128)} copy-done((f32[3,896,512]{2,1,0:T(8,128)}, f32[3,896,512]{2,1,0:T(8,128)S(1)}, u32[]{:S(2)}) %copy-start.22) | copy-done | bytes 5505048
  35.9 2.0 %copy-done.23 = bf16[3,896,768]{2,1,0:T(8,128)(2,1)} copy-done((bf16[3,896,768]{2,1,0:T(8,128)(2,1)}, bf16[3,896,768]{2,1,0:T(8,128)(2,1)S(1)}, u32[]{:S(2)}) %copy-start.23) | copy-done | bytes 4128792
  37.9 1.5 %copy-done.24 = bf16[3,896,512]{2,1,0:T(8,128)(2,1)} copy-done((bf16[3,896,512]{2,1,0:T(8,128)(2,1)}, bf16[3,896,512]{2,1,0:T(8,128)(2,1)S(1)}, u32[]{:S(2)}) %copy-start.24) | copy-done | bytes 2752536
  39.4 0.9 copy-done.26
  40.4 0.1 pad_add_fusion.place
  40.4 0.0 collective-permute-done.2.h0
  40.4 0.0 collective-permute-done.3.h2
  40.4 1.4 %copy-done.5 = f32[512,768]{1,0:T(8,128)S(1)} copy-done((f32[512,768]{1,0:T(8,128)S(1)}, f32[512,768]{1,0:T(8,128)}, u32[]{:S(2)}) %copy-start.5) | copy-done | bytes 1572888
  41.9 1.1 copy-done.7
  43.0 6.4 %rim_columns.1 = (bf16[3,256,768]{2,1,0:T(8,128)(2,1)S(1)}, f32[2,256,128]{2,1,0:T(8,128)S(1)}, f32[3,256,512]{2,1,0:T(8,128)S(1)}, bf16[3,256,512]{2,1,0:T(8,128)(2,1)S(1)}, f32[1024,512]{1,0:T(8,128)S(1)}) custom-call(s32[1,1]{1,0:T(1,128)S(6)} %copy.15.turn, s32[32,32]{1,0:T(8,128)S(1)} %copy-done.10, f32[72,768]{1,0:T(8,128)} %collective-permute-done.2.h0, ...), custom_call_target="tpu_custom_call" | custom-call | flops 1006632960 | bytes 20971520 | tf_op jit(solution)/shard_map/rim_columns/pallas_call | solution.py:433
  49.4 1.3 copy-done.3
  50.7 1.2 copy-done.12
  51.9 1.0 copy-done.14
  52.9 0.9 copy-done.16
  53.8 0.7 copy-done.20
  54.5 3.5 %all-to-all-start = ((f32[32,32,512]{2,1,0:T(8,128)}), f32[32,32,512]{2,1,0:T(8,128)S(1)}, u32[]{:S(2)}, u32[]{:S(2)}) async-start(f32[32,32,512]{2,1,0:T(8,128)} %bitcast.49), calls=%async_computation | async-start | bytes 4194304 | tf_op jit(solution)/shard_map/all_to_all | solution.py:450
  58.0 0.0 copy-start.8
  58.0 1.1 copy-done.8
  59.1 1.9 %copy-done.11 = f32[32,32,768]{2,1,0:T(8,128)S(1)} copy-done((f32[32,32,768]{2,1,0:T(8,128)S(1)}, f32[32,32,768]{2,1,0:T(8,128)}, u32[]{:S(2)}) %copy-start.11) | copy-done | bytes 3145752
  61.0 1.4 %copy-done.13 = f32[3,256,512]{2,1,0:T(8,128)S(1)} copy-done((f32[3,256,512]{2,1,0:T(8,128)S(1)}, f32[3,256,512]{2,1,0:T(8,128)}, u32[]{:S(2)}) %copy-start.13) | copy-done | bytes 1572888
  62.4 1.3 copy-done.15
  63.7 1.1 copy-done.17
  64.8 1.0 copy-done.19
  65.9 1.8 %copy-done.25 = bf16[3,896,512]{2,1,0:T(8,128)(2,1)S(1)} copy-done((bf16[3,896,512]{2,1,0:T(8,128)(2,1)S(1)}, bf16[3,896,512]{2,1,0:T(8,128)(2,1)}, u32[]{:S(2)}) %copy-start.25) | copy-done | bytes 2752536
  67.7 1.2 copy-done.27
  68.8 19.3 %columns_backward.1 = (f32[16,96,256]{2,1,0:T(8,128)S(1)}, f32[16,96,256]{2,1,0:T(8,128)S(1)}) custom-call(s32[2]{0:T(128)S(1)} %pad_add_fusion.place, s32[1,1]{1,0:T(1,128)S(6)} %copy.15.turn, f32[1024,768]{1,0:T(8,128)S(1)} %bitcast.50, f32[1024,128]{1,0:T(8,128)S(1)} %copy-done.19, f32[256,128]{1,0:T(8,128)S(1)} %get-tuple-element.25.order.mask_rim, ...), custom_call_target="tpu_custom_call" | custom-call | flops 8858370048 | bytes 41943040 | tf_op jit(solution)/shard_map/columns_backward/pallas_call | solution.py:457
  88.1 0.2 collective-permute-start.4
  88.3 3.3 %collective-permute-done.4 = f32[16,96,256]{2,1,0:T(8,128)S(1)} collective-permute-done((f32[16,96,256]{2,1,0:T(8,128)S(1)}, f32[16,96,256]{2,1,0:T(8,128)S(1)}, u32[]{:S(2)}, u32[]{:S(2)}) %collective-permute-start.4) | collective-permute-done | bytes 1572896 | tf_op jit(solution)/shard_map/ppermute | solution.py:476
  91.6 0.2 add.21
  91.8 0.1 slice_bitcast_fusion.2
  91.9 1.7 %collective-permute-start.5 = (f32[4,96,256]{2,1,0:T(8,128)S(1)}, f32[4,96,256]{2,1,0:T(8,128)S(1)}, u32[]{:S(2)}, u32[]{:S(2)}) collective-permute-start(f32[4,96,256]{2,1,0:T(8,128)S(1)} %get-tuple-element.43), channel_id=1, source_target_pairs={{0,1},{1,0},{2,3},{3,2},{4,5},{5,4},{6,7},{7,6},{8,9},{9,8},{10,11... | collective-permute-start | bytes 1179656 | tf_op jit(solution)/shard_map/ppermute | solution.py:482
  93.6 1.5 %collective-permute-start.6 = (f32[4,96,256]{2,1,0:T(8,128)S(1)}, f32[4,96,256]{2,1,0:T(8,128)S(1)}, u32[]{:S(2)}, u32[]{:S(2)}) collective-permute-start(f32[4,96,256]{2,1,0:T(8,128)S(1)} %get-tuple-element.45), channel_id=1, source_target_pairs={{0,16},{1,17},{2,18},{3,19},{4,20},{5,21},{6,22},{7,23},{8,24},{9,... | collective-permute-start | bytes 1179656 | tf_op jit(solution)/shard_map/ppermute | solution.py:482
  95.0 0.4 collective-permute-start.7
  95.5 20.9 %collective-permute-done.5 = f32[4,96,256]{2,1,0:T(8,128)S(1)} collective-permute-done((f32[4,96,256]{2,1,0:T(8,128)S(1)}, f32[4,96,256]{2,1,0:T(8,128)S(1)}, u32[]{:S(2)}, u32[]{:S(2)}) %collective-permute-start.5) | collective-permute-done | bytes 393248 | tf_op jit(solution)/shard_map/ppermute | solution.py:482
  116.3 0.0 collective-permute-done.6
  116.3 0.0 collective-permute-done.7
  116.3 0.1 fusion.2
  116.5 2.0 %collective-permute-start.10 = (f32[96,256]{1,0:T(8,128)S(1)}, f32[96,256]{1,0:T(8,128)S(1)}, u32[]{:S(2)}, u32[]{:S(2)}) collective-permute-start(f32[96,256]{1,0:T(8,128)S(1)} %get-tuple-element.47), channel_id=1, source_target_pairs={{0,6},{1,7},{2,4},{3,5},{4,2},{5,3},{6,0},{7,1},{8,14},{9,15},{10,... | collective-permute-start | bytes 294920 | tf_op jit(solution)/shard_map/ppermute | solution.py:487
  118.5 0.8 collective-permute-start.8
  119.3 1.6 %collective-permute-start.9 = (f32[96,256]{1,0:T(8,128)S(1)}, f32[96,256]{1,0:T(8,128)S(1)}, u32[]{:S(2)}, u32[]{:S(2)}) collective-permute-start(f32[96,256]{1,0:T(8,128)S(1)} %get-tuple-element.48), channel_id=1, source_target_pairs={{0,4},{1,5},{2,6},{3,7},{4,0},{5,1},{6,2},{7,3},{8,12},{9,13},{10,... | collective-permute-start | bytes 294920 | tf_op jit(solution)/shard_map/ppermute | solution.py:487
  120.9 3.2 %collective-permute-done.10 = f32[96,256]{1,0:T(8,128)S(1)} collective-permute-done((f32[96,256]{1,0:T(8,128)S(1)}, f32[96,256]{1,0:T(8,128)S(1)}, u32[]{:S(2)}, u32[]{:S(2)}) %collective-permute-start.10) | collective-permute-done | bytes 98336 | tf_op jit(solution)/shard_map/ppermute | solution.py:487
  124.1 0.5 collective-permute-done.8
  124.6 3.4 %collective-permute-done.9 = f32[96,256]{1,0:T(8,128)S(1)} collective-permute-done((f32[96,256]{1,0:T(8,128)S(1)}, f32[96,256]{1,0:T(8,128)S(1)}, u32[]{:S(2)}, u32[]{:S(2)}) %collective-permute-start.9) | collective-permute-done | bytes 98336 | tf_op jit(solution)/shard_map/ppermute | solution.py:487
  128.1 0.6 reshape.41
  128.8 0.6 copy.12
  129.4 0.0 all-to-all-done
  129.4 3.5 %tendency_rows.1 = f32[1024,768]{1,0:T(8,128)} custom-call(f32[1024,512]{1,0:T(8,128)S(1)} %bitcast.48, bf16[512,768]{1,0:T(8,128)(2,1)S(1)} %copy-done.2), custom_call_target="tpu_custom_call" | custom-call | flops 1610612736 | bytes 6291456 | tf_op jit(solution)/shard_map/tendency_rows/pallas_call | solution.py:493
  (34 shorter events, 0.2 us)
Async XLA Ops:
  1.3 1.9 %copy-start = (f32[32,32,768]{2,1,0:T(8,128)S(1)}, f32[32,32,768]{2,1,0:T(8,128)}, u32[]{:S(2)}) copy-start(f32[32,32,768]{2,1,0:T(8,128)} %param.7) | copy-start | bytes 9437188
  3.2 3.3 %copy-start.1 = (f32[32,32,768]{2,1,0:T(8,128)S(1)}, f32[32,32,768]{2,1,0:T(8,128)}, u32[]{:S(2)}) copy-start(f32[32,32,768]{2,1,0:T(8,128)} %param.7) | copy-start | bytes 9437188
  3.9 12.7 %collective-permute-start = (f32[64,768]{1,0:T(8,128)S(1)}, f32[64,768]{1,0:T(8,128)S(1)}, u32[]{:S(2)}, u32[]{:S(2)}) collective-permute-start(f32[64,768]{1,0:T(8,128)S(1)} %get-tuple-element.23), channel_id=1, source_target_pairs={{0,8},{8,16},{16,24},{24,0},{1,9},{9,17},{17,25},{25,1},{2,10},{10... | collective-permute-start | bytes 589832 | tf_op jit(solution)/shard_map/ppermute | solution.py:385
  4.4 12.2 %collective-permute-start.1 = (f32[64,768]{1,0:T(8,128)S(1)}, f32[64,768]{1,0:T(8,128)S(1)}, u32[]{:S(2)}, u32[]{:S(2)}) collective-permute-start(f32[64,768]{1,0:T(8,128)S(1)} %get-tuple-element.24), channel_id=1, source_target_pairs={{0,24},{8,0},{16,8},{24,16},{1,25},{9,1},{17,9},{25,17},{2,26},{10... | collective-permute-start | bytes 589832 | tf_op jit(solution)/shard_map/ppermute | solution.py:386
  6.4 0.7 copy-start.9
  16.5 6.9 %copy-start.4 = (f32[512,768]{1,0:T(8,128)}, f32[512,768]{1,0:T(8,128)S(1)}, u32[]{:S(2)}) copy-start(f32[512,768]{1,0:T(8,128)S(1)} %get-tuple-element.28.own) | copy-start | bytes 4718596
  16.6 16.9 %copy-start.18 = (f32[1024,128]{1,0:T(8,128)}, f32[1024,128]{1,0:T(8,128)S(1)}, u32[]{:S(2)}) copy-start(f32[1024,128]{1,0:T(8,128)S(1)} %get-tuple-element.30.mask) | copy-start | bytes 1572868
  16.6 6.9 %copy-start.2 = (bf16[512,768]{1,0:T(8,128)(2,1)S(1)}, bf16[512,768]{1,0:T(8,128)(2,1)}, u32[]{:S(2)}) copy-start(bf16[512,768]{1,0:T(8,128)(2,1)} %w_out.7) | copy-start | bytes 2359300
  16.6 6.8 %copy-start.6 = (bf16[768,512]{1,0:T(8,128)(2,1)S(1)}, bf16[768,512]{1,0:T(8,128)(2,1)}, u32[]{:S(2)}) copy-start(bf16[768,512]{1,0:T(8,128)(2,1)} %w_in.5) | copy-start | bytes 2359300
  16.6 6.8 %copy-start.10 = (s32[32,32]{1,0:T(8,128)S(1)}, s32[32,32]{1,0:T(8,128)}, u32[]{:S(2)}) copy-start(s32[32,32]{1,0:T(8,128)} %dest.3) | copy-start | bytes 12292
  18.1 22.3 %collective-permute-start.2 = (f32[72,768]{1,0:T(8,128)}, f32[72,768]{1,0:T(8,128)}, u32[]{:S(2)}, u32[]{:S(2)}) collective-permute-start(f32[72,768]{1,0:T(8,128)} %get-tuple-element.26), channel_id=1, source_target_pairs={{0,1},{1,2},{2,3},{3,4},{4,5},{5,6},{6,7},{7,0},{8,9},{9,10},{10,1... | collective-permute-start | bytes 663560 | tf_op jit(solution)/shard_map/ppermute | solution.py:416
  20.4 20.1 %collective-permute-start.3 = (f32[72,768]{1,0:T(8,128)}, f32[72,768]{1,0:T(8,128)}, u32[]{:S(2)}, u32[]{:S(2)}) collective-permute-start(f32[72,768]{1,0:T(8,128)} %get-tuple-element.27), channel_id=1, source_target_pairs={{0,7},{1,0},{2,1},{3,2},{4,3},{5,4},{6,5},{7,6},{8,15},{9,8},{10,9... | collective-permute-start | bytes 663560 | tf_op jit(solution)/shard_map/ppermute | solution.py:417
  33.5 2.4 %copy-start.22 = (f32[3,896,512]{2,1,0:T(8,128)}, f32[3,896,512]{2,1,0:T(8,128)S(1)}, u32[]{:S(2)}) copy-start(f32[3,896,512]{2,1,0:T(8,128)S(1)} %get-tuple-element.35.g_i) | copy-start | bytes 16515076
  35.9 2.0 %copy-start.23 = (bf16[3,896,768]{2,1,0:T(8,128)(2,1)}, bf16[3,896,768]{2,1,0:T(8,128)(2,1)S(1)}, u32[]{:S(2)}) copy-start(bf16[3,896,768]{2,1,0:T(8,128)(2,1)S(1)} %get-tuple-element.33.n_i) | copy-start | bytes 12386308
  37.9 1.5 %copy-start.24 = (bf16[3,896,512]{2,1,0:T(8,128)(2,1)}, bf16[3,896,512]{2,1,0:T(8,128)(2,1)S(1)}, u32[]{:S(2)}) copy-start(bf16[3,896,512]{2,1,0:T(8,128)(2,1)S(1)} %get-tuple-element.36.h_i) | copy-start | bytes 8257540
  39.4 0.9 copy-start.26
  40.4 1.4 %copy-start.5 = (f32[512,768]{1,0:T(8,128)S(1)}, f32[512,768]{1,0:T(8,128)}, u32[]{:S(2)}) copy-start(f32[512,768]{1,0:T(8,128)} %copy-done.4) | copy-start | bytes 4718596
  41.9 1.1 copy-start.7
  49.4 1.3 copy-start.3
  50.7 1.2 copy-start.12
  51.9 1.0 copy-start.14
  52.9 0.9 copy-start.16
  53.8 0.7 copy-start.20
  54.5 3.5 %copy-start.21 = (f32[2,256,128]{2,1,0:T(8,128)S(1)}, f32[2,256,128]{2,1,0:T(8,128)}, u32[]{:S(2)}) copy-start(f32[2,256,128]{2,1,0:T(8,128)} %copy-done.20) | copy-start | bytes 786436
  54.5 74.9 %all-to-all-start = ((f32[32,32,512]{2,1,0:T(8,128)}), f32[32,32,512]{2,1,0:T(8,128)S(1)}, u32[]{:S(2)}, u32[]{:S(2)}) async-start(f32[32,32,512]{2,1,0:T(8,128)} %bitcast.49), calls=%async_computation | async-start | bytes 4194304 | tf_op jit(solution)/shard_map/all_to_all | solution.py:450
  58.0 1.1 copy-start.8
  59.1 1.9 %copy-start.11 = (f32[32,32,768]{2,1,0:T(8,128)S(1)}, f32[32,32,768]{2,1,0:T(8,128)}, u32[]{:S(2)}) copy-start(f32[32,32,768]{2,1,0:T(8,128)} %param.8) | copy-start | bytes 9437188
  61.0 1.4 %copy-start.13 = (f32[3,256,512]{2,1,0:T(8,128)S(1)}, f32[3,256,512]{2,1,0:T(8,128)}, u32[]{:S(2)}) copy-start(f32[3,256,512]{2,1,0:T(8,128)} %copy-done.12) | copy-start | bytes 4718596
  62.4 1.3 copy-start.15
  63.7 1.1 copy-start.17
  64.8 1.0 copy-start.19
  65.9 1.8 %copy-start.25 = (bf16[3,896,512]{2,1,0:T(8,128)(2,1)S(1)}, bf16[3,896,512]{2,1,0:T(8,128)(2,1)}, u32[]{:S(2)}) copy-start(bf16[3,896,512]{2,1,0:T(8,128)(2,1)} %copy-done.24) | copy-start | bytes 8257540
  67.7 1.2 copy-start.27
  88.1 3.5 %collective-permute-start.4 = (f32[16,96,256]{2,1,0:T(8,128)S(1)}, f32[16,96,256]{2,1,0:T(8,128)S(1)}, u32[]{:S(2)}, u32[]{:S(2)}) collective-permute-start(f32[16,96,256]{2,1,0:T(8,128)S(1)} %get-tuple-element.42), channel_id=1, source_target_pairs={{0,8},{8,0},{16,24},{24,16},{1,9},{9,1},{17,25},{25,17},{2,10},{10... | collective-permute-start | bytes 4718600 | tf_op jit(solution)/shard_map/ppermute | solution.py:476
  91.9 24.4 %collective-permute-start.5 = (f32[4,96,256]{2,1,0:T(8,128)S(1)}, f32[4,96,256]{2,1,0:T(8,128)S(1)}, u32[]{:S(2)}, u32[]{:S(2)}) collective-permute-start(f32[4,96,256]{2,1,0:T(8,128)S(1)} %get-tuple-element.43), channel_id=1, source_target_pairs={{0,1},{1,0},{2,3},{3,2},{4,5},{5,4},{6,7},{7,6},{8,9},{9,8},{10,11... | collective-permute-start | bytes 1179656 | tf_op jit(solution)/shard_map/ppermute | solution.py:482
  93.6 22.8 %collective-permute-start.6 = (f32[4,96,256]{2,1,0:T(8,128)S(1)}, f32[4,96,256]{2,1,0:T(8,128)S(1)}, u32[]{:S(2)}, u32[]{:S(2)}) collective-permute-start(f32[4,96,256]{2,1,0:T(8,128)S(1)} %get-tuple-element.45), channel_id=1, source_target_pairs={{0,16},{1,17},{2,18},{3,19},{4,20},{5,21},{6,22},{7,23},{8,24},{9,... | collective-permute-start | bytes 1179656 | tf_op jit(solution)/shard_map/ppermute | solution.py:482
  95.0 21.3 %collective-permute-start.7 = (f32[4,96,256]{2,1,0:T(8,128)S(1)}, f32[4,96,256]{2,1,0:T(8,128)S(1)}, u32[]{:S(2)}, u32[]{:S(2)}) collective-permute-start(f32[4,96,256]{2,1,0:T(8,128)S(1)} %get-tuple-element.44), channel_id=1, source_target_pairs={{0,17},{1,16},{2,19},{3,18},{4,21},{5,20},{6,23},{7,22},{8,25},{9,... | collective-permute-start | bytes 1179656 | tf_op jit(solution)/shard_map/ppermute | solution.py:482
  116.5 7.6 %collective-permute-start.10 = (f32[96,256]{1,0:T(8,128)S(1)}, f32[96,256]{1,0:T(8,128)S(1)}, u32[]{:S(2)}, u32[]{:S(2)}) collective-permute-start(f32[96,256]{1,0:T(8,128)S(1)} %get-tuple-element.47), channel_id=1, source_target_pairs={{0,6},{1,7},{2,4},{3,5},{4,2},{5,3},{6,0},{7,1},{8,14},{9,15},{10,... | collective-permute-start | bytes 294920 | tf_op jit(solution)/shard_map/ppermute | solution.py:487
  118.5 6.1 %collective-permute-start.8 = (f32[96,256]{1,0:T(8,128)S(1)}, f32[96,256]{1,0:T(8,128)S(1)}, u32[]{:S(2)}, u32[]{:S(2)}) collective-permute-start(f32[96,256]{1,0:T(8,128)S(1)} %get-tuple-element.46), channel_id=1, source_target_pairs={{0,2},{1,3},{2,0},{3,1},{4,6},{5,7},{6,4},{7,5},{8,10},{9,11},{10,... | collective-permute-start | bytes 294920 | tf_op jit(solution)/shard_map/ppermute | solution.py:487
  119.3 8.7 %collective-permute-start.9 = (f32[96,256]{1,0:T(8,128)S(1)}, f32[96,256]{1,0:T(8,128)S(1)}, u32[]{:S(2)}, u32[]{:S(2)}) collective-permute-start(f32[96,256]{1,0:T(8,128)S(1)} %get-tuple-element.48), channel_id=1, source_target_pairs={{0,4},{1,5},{2,6},{3,7},{4,0},{5,1},{6,2},{7,3},{8,12},{9,13},{10,... | collective-permute-start | bytes 294920 | tf_op jit(solution)/shard_map/ppermute | solution.py:487

commit v3 on v2

--- a/solution.py
+++ b/solution.py
@@ -17,6 +17,7 @@
 SIDE_WINDS = (((0, 1.0), (1, 1.0)), ((1, 1.0), (0, -1.0)), ((0, -1.0), (1, -1.0)), ((1, -1.0), (0, 1.0)))
 
 VMEM = pl.BlockSpec(memory_space=pltpu.VMEM)
+HBM = pl.BlockSpec(memory_space=pltpu.HBM)
 SMEM = pl.BlockSpec(memory_space=pltpu.SMEM)
 
 
@@ -122,25 +123,33 @@
     lax.fori_loop(0, (hi - lo) // block, body, 0)
 
 
-def network_forward(x, mask, w_in, w_out, normed, scale, slope, hidden, hsum, rows):
+def network_forward(x, mask, w_in, w_out, state, hsum, rows, kept):
+    normed, scale, slope, hidden = state
     total = None
     for use in range(3):
         inv = lax.rsqrt(jnp.mean(x * x, axis=1, keepdims=True) + EPS)
         unit = (x * inv).astype(BF16)
         normed[use, rows, :] = unit
-        if use > 0:
-            scale[use - 1, rows, :] = jnp.broadcast_to(inv, (x.shape[0], LANES))
+        scale[use, rows, :] = mask if use == 0 else jnp.broadcast_to(inv, (x.shape[0], LANES))
         p = jnp.dot(unit, w_in, preferred_element_type=F32)
         s = 0.5 + 0.5 * jnp.tanh(0.5 * p)
         silu = p * s
-        slope[use, rows, :] = s + silu * (1.0 - s)
+        slope[use, rows, :] = (s + silu * (1.0 - s)).astype(BF16)
         h = silu.astype(BF16)
         hidden[use, rows, :] = h
+        kept(use)
         if use < 2:
             total = h.astype(F32) if use == 0 else total + h.astype(F32)
             x = x + TAU * jnp.dot(h, w_out, preferred_element_type=F32)
         else:
-            hsum[rows, :] = total + h.astype(F32) * mask
+            hsum[rows, :] = total + h.astype(F32) * mask[:, 0:1]
+
+
+def state_copies(source, target, sems, use, part, rows):
+    return [
+        pltpu.make_async_copy(a.at[use, rows, :], b.at[use, rows, :], sems.at[part, use, i])
+        for i, (a, b) in enumerate(zip(source, target))
+    ]
 
 
 def pack_strip(n, levels, k, o, air, out):
@@ -165,12 +174,21 @@
     s2[2 * n + 1 : 2 * n + 2, :] = h3[n - 1 : n, :]
 
 
-def inner_transport_kernel(n, levels, turn, cost, air_rows, moved, own, mask, mask_rim, q_one, face_lead, face_sub):
+def inner_transport_kernel(n, levels, turn, air_rows, moved, own, token, q_one, face_lead, face_sub):
     o = turn[0, 0]
     air = air_rows.reshape(n, n, air_rows.shape[1])
     winds = ((0, 1.0), (1, 1.0))
     transport(air, q_one, face_lead, face_sub, 1, n - 1, winds, levels)
     transport(q_one, moved, face_lead, face_sub, 2, n - 2, winds, levels)
+    for k in range(4):
+        base, cm, cd = side_rows((k - o + 4) % 4, n)
+        for d in range(4):
+            copy_rows(own, (k * 4 + d) * n, air_rows, base + cd * d, cm, n)
+        turn_winds(own, (k * 4 * n, 4 * n), o, levels)
+    token[...] = jnp.zeros_like(token)
+
+
+def cost_mask(n, cost, mask):
     diagonal = lax.broadcasted_iota(jnp.int32, (n, n), 0) == lax.broadcasted_iota(jnp.int32, (n, n), 1)
 
     def mask_row(i, carry):
@@ -180,29 +198,35 @@
         return carry
 
     lax.fori_loop(0, n, mask_row, 0, unroll=8)
+
+
+def inner_parts(n):
+    inner, parts = n - 4, 2
+    size = inner // parts * n
+    return [(part, part * size, size) for part in range(parts)]
+
+
+def inner_network_kernel(n, dest, turn, moved, cost, w_in, w_out, n_o, s_o, g_o, h_o, outgoing, mask_rim,
+                         normed, scale, slope, hidden, hsum, mask, sems):
+    state, out = (normed, scale, slope, hidden), (n_o, s_o, g_o, h_o)
+    feats = moved.shape[2]
+    cost_mask(n, cost, mask)
     for k in range(4):
-        base, cm, cd = side_rows((k - o + 4) % 4, n)
-        for d in range(4):
-            copy_rows(own, (k * 4 + d) * n, air_rows, base + cd * d, cm, n)
+        base, cm, cd = side_rows((k - turn[0, 0] + 4) % 4, n)
         for d in range(2):
             copy_rows(mask_rim, (k * 2 + d) * n, mask, base + cd * d, cm, n)
-        turn_winds(own, (k * 4 * n, 4 * n), o, levels)
-
-
-def inner_network_kernel(n, dest, moved, mask, w_in, w_out, normed, scale, slope, hidden, outgoing, hsum):
-    inner = n - 4
-    parts = 2
-    size = inner // parts * n
-    feats = moved.shape[2]
-
-    def chunk(part, carry):
-        rows = pl.ds(pl.multiple_of(part * size, size), size)
-        x = moved[pl.ds(2 + part * (inner // parts), inner // parts), :, :].reshape(size, feats)
-        m = mask[pl.ds(pl.multiple_of(2 * n + part * size, 8), size), 0:1]
-        network_forward(x, m, w_in[...], w_out[...], normed, scale, slope, hidden, hsum, rows)
-        return carry
-
-    lax.fori_loop(0, parts, chunk, 0)
+    copies = []
+    for part, start, size in inner_parts(n):
+        rows = slice(start, start + size)
+        x = moved[2 + start // n : 2 + (start + size) // n, :, :].reshape(size, feats)
+        m = mask[2 * n + start : 2 * n + start + size, :]
+
+        def kept(use, part=part, rows=pl.ds(start, size)):
+            for copy in state_copies(state, out, sems, use, part, rows):
+                copy.start()
+                copies.append(copy)
+
+        network_forward(x, m, w_in[...], w_out[...], state, hsum, rows, kept)
 
     def place(i, carry):
         for j in range(2, n - 2):
@@ -210,12 +234,16 @@
         return carry
 
     lax.fori_loop(2, n - 2, place, 0)
+    for copy in copies:
+        copy.wait()
 
 
 def rim_kernel(n, levels, turn, dest, h0, h1, h2, h3, own, mask_rim, w_in, w_out, before,
-               normed, scale, slope, hidden, outgoing,
+               n_o, s_o, g_o, h_o, outgoing, sent,
+               normed, scale, slope, hidden, sems,
                wide, wide_one, wide_two, slim, slim_one, slim_two, lead_wide, sub_wide, lead_slim, sub_slim, x_rim, hsum):
-    outgoing[...] = before[...]
+    del before
+    state, out = (normed, scale, slope, hidden), (n_o, s_o, g_o, h_o)
     o = turn[0, 0]
     halo = (h0, h1, h2, h3)
     for k in range(4):
@@ -249,8 +277,14 @@
                 x_rim[at : at + 2, :] = two[2 + d, n + 2 : n + 4, :]
                 x_rim[at + n - 2 : at + n, :] = two[2 + d, n + 12 : n + 14, :]
     turn_winds(x_rim, (0, 8 * n), (4 - o) % 4, levels)
-    network_forward(x_rim[...], mask_rim[:, 0:1], w_in[...], w_out[...], normed, scale, slope, hidden, hsum,
-                    slice(0, 8 * n))
+    copies = []
+
+    def kept(use):
+        for copy in state_copies(state, out, sems, use, 0, pl.ds(0, 8 * n)):
+            copy.start()
+            copies.append(copy)
+
+    network_forward(x_rim[...], mask_rim[...], w_in[...], w_out[...], state, hsum, slice(0, 8 * n), kept)
     for k in range(4):
         (bi, di, mi), (bj, dj, mj) = side_cells((k - o + 4) % 4, n)
         skip = 2 * (k % 2)
@@ -259,6 +293,10 @@
                 at = (k * 2 + d) * n + m
                 row = dest[bi + di * d + mi * m, bj + dj * d + mj * m]
                 outgoing[pl.ds(row, 1), :] = hsum[at : at + 1, :]
+    copies.append(pltpu.make_async_copy(outgoing, sent, sems.at[1, 0, 0]))
+    copies[-1].start()
+    for copy in copies:
+        copy.wait()
 
 
 def contract_rows(a, b):
@@ -269,71 +307,141 @@
     return lax.dot_general(a, b, (((1,), (1,)), ((), ())), preferred_element_type=F32)
 
 
-def network_backward(cot, mask, w_in, w_out, normed, scale, slope, err_out, err_in, rows):
-    grad = cot * mask
+def network_backward(cot, valid, w_in, w_out, state, err_out, err_in, rows, at, arrived):
+    normed, scale, slope, _ = state
+    arrived("chain")
+    cot = cot * valid
+    grad = cot * scale[0, rows, 0:1]
     for use in (2, 1, 0):
         e = (TAU * grad).astype(BF16)
-        err_out[use, rows, :] = e
-        inner = (contract_last(e, w_out) * slope[use, rows, :]).astype(BF16)
+        err_out[use, at, :] = e
+        inner = (contract_last(e, w_out) * slope[use, rows, :].astype(F32)).astype(BF16)
         err_in[use, rows, :] = inner
         if use > 0:
             d = contract_last(inner, w_in)
             unit = normed[use, rows, :].astype(F32)
-            d = scale[use - 1, rows, 0:1] * (d - unit * jnp.mean(d * unit, axis=1, keepdims=True))
+            d = scale[use, rows, 0:1] * (d - unit * jnp.mean(d * unit, axis=1, keepdims=True))
             grad = (cot if use == 2 else grad) + d
 
 
-def backward_kernel(n, grid_shape, place, turn, cot, mask, mask_rim, w_in, w_out, n_i, s_i, g_i, h_i, n_r, s_r, g_r, h_r,
-                    keep, send, eo_i, ei_i, eo_r, ei_r, cot_rim, grad_in, grad_out):
+def store_pieces(grid_shape, me, grad, keep, send):
+    groups, tiles = grid_shape
+    rows = grad.shape[0] // (groups * tiles)
+    bits = (tiles // 2).bit_length() - 1
+    for g in range(groups):
+        for t in range(tiles):
+            p = g * tiles + t
+            rg, rt = me[0] ^ g, me[1] ^ t
+            at = (rg // 2) * 2 + rt % 2
+            for b in range(bits):
+                at = at * 2 + (rt >> (b + 1)) % 2
+
+            def store(ref, p=p, at=at):
+                for c in range(grad.shape[1] // COL):
+                    ref[at, c * rows : (c + 1) * rows, :] = grad[p * rows : (p + 1) * rows, c * COL : (c + 1) * COL]
+
+            pl.when(rg % 2 == 0)(functools.partial(store, keep))
+            pl.when(rg % 2 == 1)(functools.partial(store, send))
+
+
+def backward_kernel(n, grid_shape, me, turn, cot_in, w_in, w_out, in_ni, in_si, in_gi, in_nr, in_sr, in_gr,
+                    keep, send, err_out, n_i, s_i, g_i, n_r, s_r, g_r, sems, ei_i, ei_r, cot, cot_rim, grad_in):
     o = turn[0, 0]
-    inner = n - 4
-    parts = 2
-    size = inner // parts * n
+    parts = inner_parts(n)
+    inner = (n - 4) * n
+    edge = 2 * n
+    index = 0
+
+    def fetch(source, target):
+        nonlocal index
+        copy = pltpu.make_async_copy(source, target, sems.at[index])
+        index += 1
+        copy.start()
+        return copy
+
+    chain, late = {}, []
+    groups = [(part, (in_ni, in_si, in_gi), (n_i, s_i, g_i), start, size) for part, start, size in parts]
+    groups.append((len(parts), (in_nr, in_sr, in_gr), (n_r, s_r, g_r), 0, 8 * n))
+    for part, source, here, start, size in groups:
+        rows = pl.ds(start, size)
+        chain[part] = []
+        if part < len(parts):
+            at = pl.ds(edge + start, size)
+            chain[part].append(fetch(cot_in.at[at, :], cot.at[at, :]))
+        else:
+            for at in (pl.ds(0, edge), pl.ds(edge + inner, edge)):
+                chain[part].append(fetch(cot_in.at[at, :], cot.at[at, :]))
+        chain[part].append(fetch(source[1].at[:, rows, :], here[1].at[:, rows, :]))
+        chain[part].append(fetch(source[2].at[:, rows, :], here[2].at[:, rows, :]))
+        chain[part].append(fetch(source[0].at[pl.ds(1, 2), rows, :], here[0].at[pl.ds(1, 2), rows, :]))
+    for part, source, here, start, size in groups:
+        rows = pl.ds(start, size)
+        late.append(fetch(source[0].at[0, rows, :], here[0].at[0, rows, :]))
+
+    def wait_for(part):
+        def arrived(_):
+            for copy in chain[part]:
+                copy.wait()
+
+        return arrived
+
+    for part, start, size in parts:
+        wait_for(part)(None)
+        at = slice(edge + start, edge + start + size)
+        j = lax.broadcasted_iota(jnp.int32, (size, 1), 0) % n
+        valid = ((j >= 2) & (j < n - 2)).astype(F32)
+        network_backward(cot[at, :], valid, w_in[...], w_out[...], (n_i, s_i, g_i, None), err_out, ei_i,
+                         slice(start, start + size), slice(start, start + size), lambda _: None)
+    wait_for(len(parts))(None)
     for k in range(4):
         base, cm, cd = side_rows((k - o + 4) % 4, n)
         for d in range(2):
             copy_rows(cot_rim, (k * 2 + d) * n, cot, base + cd * d, cm, n)
-
-    def chunk(part, carry):
-        rows = pl.ds(pl.multiple_of(part * size, size), size)
-        at = pl.ds(pl.multiple_of(2 * n + part * size, 8), size)
-        j = lax.broadcasted_iota(jnp.int32, (size, 1), 0) % n
-        valid = ((j >= 2) & (j < n - 2)).astype(F32)
-        network_backward(cot[at, :] * valid, mask[at, 0:1], w_in[...], w_out[...], n_i, s_i, g_i, eo_i, ei_i, rows)
-        return carry
-
-    lax.fori_loop(0, parts, chunk, 0)
     e = lax.broadcasted_iota(jnp.int32, (8 * n, 1), 0)
     m = e % n
     valid = (((e // (2 * n)) % 2 == 0) | ((m >= 2) & (m < n - 2))).astype(F32)
-    network_backward(cot_rim[...] * valid, mask_rim[:, 0:1], w_in[...], w_out[...], n_r, s_r, g_r, eo_r, ei_r,
-                     slice(0, 8 * n))
+    network_backward(cot_rim[...], valid, w_in[...], w_out[...], (n_r, s_r, g_r, None), err_out, ei_r,
+                     slice(0, 8 * n), slice(inner, inner + 8 * n), lambda _: None)
+    for copy in late:
+        copy.wait()
     flat = lambda ref: ref[...].reshape(ref.shape[0] * ref.shape[1], ref.shape[2])
-    grad_out[...] = contract_rows(flat(h_i), flat(eo_i)) + contract_rows(flat(h_r), flat(eo_r))
     grad_in[...] = contract_rows(flat(n_i), flat(ei_i)) + contract_rows(flat(n_r), flat(ei_r))
-    groups, tiles = grid_shape
-    count = groups * tiles
-    feats, units = grad_in.shape
-    rows_in, rows_out = feats // count, units // count
-    for g in range(groups):
-        for t in range(tiles):
-            p = g * tiles + t
-            rg, rt = place[0] ^ g, place[1] ^ t
-            at = ((rg // 2) * 2 + rt % 2) * (tiles // 2) + rt // 2
-            pieces = []
-            for c in range(units // COL):
-                pieces.append(grad_in[p * rows_in : (p + 1) * rows_in, c * COL : (c + 1) * COL])
-            for c in range(feats // COL):
-                pieces.append(grad_out[p * rows_out : (p + 1) * rows_out, c * COL : (c + 1) * COL])
-
-            def store(ref, pieces=pieces, at=at):
-                row = 0
-                for piece in pieces:
-                    ref[at, row : row + piece.shape[0], :] = piece
-                    row += piece.shape[0]
-
-            pl.when(rg % 2 == 0)(functools.partial(store, keep))
-            pl.when(rg % 2 == 1)(functools.partial(store, send))
+    store_pieces(grid_shape, me, grad_in, keep, send)
+
+
+def output_gradient_kernel(n, grid_shape, me, err_out, in_hi, in_hr, keep, send, h, grad_out, sems):
+    inner = (n - 4) * n
+    copies = []
+    for use in (2, 1, 0):
+        for source, rows in ((in_hi, pl.ds(0, inner)), (in_hr, pl.ds(inner, 8 * n))):
+            copy = pltpu.make_async_copy(source.at[use], h.at[use, rows, :], sems.at[len(copies)])
+            copy.start()
+            copies.append(copy)
+    for copy in copies:
+        copy.wait()
+    flat = lambda ref: ref[...].reshape(ref.shape[0] * ref.shape[1], ref.shape[2])
+    grad_out[...] = contract_rows(flat(h), flat(err_out))
+    store_pieces(grid_shape, me, grad_out, keep, send)
+
+
+def sum_over_devices(keep, send, groups, tiles):
+    both = ("grp", "tile")
+    piece = keep.shape[1:]
+    sums = keep + lax.ppermute(send, "grp", [(i, i ^ 1) for i in range(groups)])
+    sums = sums.reshape(groups // 2, 2, tiles // 2, *piece)
+    total = sums[0, 0]
+    for x in range(groups // 2):
+        for y in range(2):
+            if x or y:
+                total = total + lax.ppermute(
+                    sums[x, y], both, joint_perm(groups, tiles, lambda g, t: (g ^ (2 * x), t ^ y))
+                )
+    step = 2
+    while step < tiles:
+        half = total.shape[0] // 2
+        total = total[:half] + lax.ppermute(total[half:], "tile", [(t, t ^ step) for t in range(tiles)])
+        step *= 2
+    return total[0]
 
 
 def output_kernel(rows, w_out, out):
@@ -366,14 +474,15 @@
     cot_rows = cotangent.reshape(cells, feats)
     both = ("grp", "tile")
 
-    def state(rows):
+    def state(space, rows):
         return [
-            pltpu.VMEM((3, rows, feats), BF16),
-            pltpu.VMEM((2, rows, LANES), F32),
-            pltpu.VMEM((3, rows, units), F32),
-            pltpu.VMEM((3, rows, units), BF16),
+            space((3, rows, feats), BF16),
+            space((3, rows, LANES), F32),
+            space((3, rows, units), BF16),
+            space((3, rows, units), BF16),
         ]
 
+    parts = len(inner_parts(n))
     strips = pl.pallas_call(
         functools.partial(pack_kernel, n, levels),
         out_shape=[shape((2 * n, feats), F32)] * 2,
@@ -385,25 +494,24 @@
     from_left = lax.ppermute(strips[1], "grp", shift_perm(groups, 1))
     from_right = lax.ppermute(strips[0], "grp", shift_perm(groups, -1))
 
-    moved, own, mask, mask_rim = pl.pallas_call(
+    moved, own, token = pl.pallas_call(
         functools.partial(inner_transport_kernel, n, levels),
         out_shape=[
             pltpu.VMEM((n, n, feats), F32),
             pltpu.VMEM((16 * n, feats), F32),
-            pltpu.VMEM((cells, LANES), F32),
-            pltpu.VMEM((rim, LANES), F32),
+            shape((8, LANES), F32),
         ],
-        in_specs=[SMEM] + [VMEM] * 2,
-        out_specs=[VMEM] * 4,
+        in_specs=[SMEM, VMEM],
+        out_specs=[VMEM] * 3,
         scratch_shapes=[
             pltpu.VMEM((n, n, feats), F32),
             pltpu.VMEM((8, n, period * LANES), F32),
             pltpu.VMEM((7, n, period * LANES), F32),
         ],
-        compiler_params=params(20),
+        compiler_params=params(10),
         cost_estimate=pl.CostEstimate(flops=60 * cells * feats, bytes_accessed=16 << 20, transcendentals=0),
         name="inner_transport",
-    )(orientation, cost_count, air_rows)
+    )(orientation, air_rows)
 
     strips = pl.pallas_call(
         functools.partial(pack_with_corners_kernel, n, levels),
@@ -412,30 +520,37 @@
         out_specs=[VMEM] * 2,
         compiler_params=params(8),
         name="pack_strips_corners",
-    )(orientation, air_rows, from_left, from_right, mask_rim)
+    )(orientation, air_rows, from_left, from_right, token)
     from_above = lax.ppermute(strips[1], "tile", shift_perm(tiles, 1))
     from_below = lax.ppermute(strips[0], "tile", shift_perm(tiles, -1))
 
-    *saved_inner, outgoing = pl.pallas_call(
+    *saved_inner, outgoing, mask_rim = pl.pallas_call(
         functools.partial(inner_network_kernel, n),
-        out_shape=[*state(inner), pltpu.VMEM((cells, units), F32)],
-        in_specs=[SMEM] + [VMEM] * 4,
-        out_specs=[VMEM] * 5,
-        scratch_shapes=[pltpu.VMEM((inner, units), F32)],
-        compiler_params=params(16),
+        out_shape=[*state(pltpu.HBM, inner), pltpu.VMEM((cells, units), F32), pltpu.VMEM((rim, LANES), F32)],
+        in_specs=[SMEM] * 2 + [VMEM] * 4,
+        out_specs=[HBM] * 4 + [VMEM] * 2,
+        scratch_shapes=[
+            *state(pltpu.VMEM, inner),
+            pltpu.VMEM((inner, units), F32),
+            pltpu.VMEM((cells, LANES), F32),
+            pltpu.SemaphoreType.DMA((parts, 3, 4)),
+        ],
+        compiler_params=params(24),
         cost_estimate=pl.CostEstimate(
             flops=10 * inner * feats * units, bytes_accessed=16 << 20, transcendentals=3 * inner * units
         ),
         name="inner_network",
-    )(assignment, moved, mask, weight_in, weight_out)
+    )(assignment, orientation, moved, cost_count, weight_in, weight_out)
 
     wide, slim = n + 16, n
-    *saved_rim, outgoing = pl.pallas_call(
+    *saved_rim, _, outgoing = pl.pallas_call(
         functools.partial(rim_kernel, n, levels),
-        out_shape=[*state(rim), shape((cells, units), F32)],
+        out_shape=[*state(pltpu.HBM, rim), pltpu.VMEM((cells, units), F32), pltpu.HBM((cells, units), F32)],
         in_specs=[SMEM, SMEM] + [VMEM] * 9,
-        out_specs=[VMEM] * 5,
-        scratch_shapes=[pltpu.VMEM((6, wide, feats), F32)] * 3
+        out_specs=[HBM] * 4 + [VMEM, HBM],
+        input_output_aliases={10: 4},
+        scratch_shapes=[*state(pltpu.VMEM, rim), pltpu.SemaphoreType.DMA((2, 3, 4))]
+        + [pltpu.VMEM((6, wide, feats), F32)] * 3
         + [pltpu.VMEM((6, slim, feats), F32)] * 3
         + [pltpu.VMEM((5, wide, period * LANES), F32), pltpu.VMEM((4, wide, period * LANES), F32)]
         + [pltpu.VMEM((5, slim, period * LANES), F32), pltpu.VMEM((4, slim, period * LANES), F32)]
@@ -451,43 +566,48 @@
         outgoing.reshape(count, cells // count, units), both, split_axis=0, concat_axis=0, tiled=True
     ).reshape(cells, units)
 
-    place = jnp.stack([lax.axis_index("grp"), lax.axis_index("tile")]).astype(jnp.int32)
-    rows_in, rows_out = feats // count, units // count
-    piece = rows_in * (units // COL) + rows_out * (feats // COL)
-    keep, send = pl.pallas_call(
+    me = jnp.stack([lax.axis_index("grp"), lax.axis_index("tile")]).astype(jnp.int32)
+    n_i, s_i, g_i, h_i = saved_inner
+    n_r, s_r, g_r, h_r = saved_rim
+    saved = lambda rows: state(pltpu.VMEM, rows)[:3]
+    halves = lambda rows, columns: [shape((count // 2, rows // count * (columns // COL), COL), F32)] * 2
+    *pieces_in, err_out = pl.pallas_call(
         functools.partial(backward_kernel, n, (groups, tiles)),
-        out_shape=[shape((count // 2, piece, COL), F32)] * 2,
-        in_specs=[SMEM, SMEM] + [VMEM] * 13,
+        out_shape=[*halves(feats, units), pltpu.VMEM((3, inner + rim, feats), BF16)],
+        in_specs=[SMEM, SMEM, HBM, VMEM, VMEM] + [HBM] * 6,
+        out_specs=[VMEM] * 3,
+        scratch_shapes=[
+            *saved(inner),
+            *saved(rim),
+            pltpu.SemaphoreType.DMA((5 * parts + 6,)),
+            pltpu.VMEM((3, inner, units), BF16),
+            pltpu.VMEM((3, rim, units), BF16),
+            pltpu.VMEM((cells, feats), F32),
+            pltpu.VMEM((rim, feats), F32),
+            pltpu.VMEM((feats, units), F32),
+        ],
+        compiler_params=params(36),
+        cost_estimate=pl.CostEstimate(flops=16 * cells * feats * units, bytes_accessed=20 << 20, transcendentals=0),
+        name="columns_backward",
+    )(me, orientation, cot_rows, weight_in, weight_out, n_i, s_i, g_i, n_r, s_r, g_r)
+    pieces_out = pl.pallas_call(
+        functools.partial(output_gradient_kernel, n, (groups, tiles)),
+        out_shape=halves(units, feats),
+        in_specs=[SMEM, VMEM, HBM, HBM],
         out_specs=[VMEM] * 2,
         scratch_shapes=[
-            pltpu.VMEM((3, inner, feats), BF16),
-            pltpu.VMEM((3, inner, units), BF16),
-            pltpu.VMEM((3, rim, feats), BF16),
-            pltpu.VMEM((3, rim, units), BF16),
-            pltpu.VMEM((rim, feats), F32),
-            pltpu.VMEM((feats, units), F32),
+            pltpu.VMEM((3, inner + rim, units), BF16),
             pltpu.VMEM((units, feats), F32),
+            pltpu.SemaphoreType.DMA((6,)),
         ],
-        compiler_params=params(36),
-        cost_estimate=pl.CostEstimate(flops=22 * cells * feats * units, bytes_accessed=40 << 20, transcendentals=0),
-        name="columns_backward",
-    )(place, orientation, cot_rows, mask, mask_rim, weight_in, weight_out, *saved_inner, *saved_rim)
-
-    sums = keep + lax.ppermute(send, "grp", [(i, i ^ 1) for i in range(groups)])
-    sums = sums.reshape(groups // 2, 2, tiles // 2, piece, COL)
-    total = sums[0, 0]
-    for x in range(groups // 2):
-        for y in range(2):
-            if x or y:
-                total = total + lax.ppermute(
-                    sums[x, y], both, joint_perm(groups, tiles, lambda g, t: (g ^ (2 * x), t ^ y))
-                )
-    mine = total[0]
-    for z in range(1, tiles // 2):
-        mine = mine + lax.ppermute(total[z], "tile", [(t, t ^ (2 * z)) for t in range(tiles)])
-    split = rows_in * (units // COL)
+        compiler_params=params(24),
+        cost_estimate=pl.CostEstimate(flops=6 * cells * feats * units, bytes_accessed=8 << 20, transcendentals=0),
+        name="output_gradient",
+    )(me, err_out, h_i, h_r)
+
     flat = lambda part, rows: part.reshape(-1, rows, COL).transpose(1, 0, 2).reshape(-1)
-    summed_in, summed_out = flat(mine[:split], rows_in), flat(mine[split:], rows_out)
+    summed_in = flat(sum_over_devices(*pieces_in, groups, tiles), feats // count)
+    summed_out = flat(sum_over_devices(*pieces_out, groups, tiles), units // count)
 
     block = cells // 4
     tendency = pl.pallas_call(

time: 134 us -> 118 us (0.88)
  local copies, waits for them, and re-layouts: 29.5 us -> 11.9 us
  waiting for transfers between devices: 31.3 us -> 21 us
  starting transfers between devices: 19.5 us -> 29.1 us
  Pallas kernels: 50.8 us -> 53.7 us
    unnamed x57 -> x31, local copies, waits for them, and re-layouts: 28.7 us -> 11.1 us
    ppermute x7 -> x12, waiting for transfers between devices: 31.3 us -> 21 us  [the longest x6 13.7 us: sum_over_devices(): lax.ppermute(sums[x, y], both, joint_perm(groups, tiles, lambda g, t: (g...]
    ppermute x7 -> x12, starting transfers between devices: 8.16 us -> 17.6 us  [the longest x4 8.92 us: sum_over_devices(): lax.ppermute(total[half:], 'tile', [(t, t ^ step) for t in range(tiles)])]
    pallas_call x0 -> x1, Pallas kernels: none -> 5.51 us  [per_device(): pl.pallas_call(functools.partial(output_gradient_kernel, n, (groups, tile...]
    pallas_call x1, Pallas kernels: 19.3 us -> 15.2 us  [per_device(): pl.pallas_call(functools.partial(backward_kernel, n, (groups, tiles)), ou...]
    pallas_call x1, Pallas kernels: 6.37 us -> 8.15 us  [per_device(): pl.pallas_call(functools.partial(rim_kernel, n, levels), out_shape=[*stat...]
  transfers between devices with their start and end apart: 12 -> 17, of which waited for: 5 -> 5; matrix products, arithmetic and copies ran while one was open for 1% -> 2% of each run, Pallas kernels for 29% -> 34%
where the time goes in v3:
time: 118 us
  Pallas kernels  53.7 us (46%)
  starting transfers between devices  29.1 us (25%)
  waiting for transfers between devices  21 us (18%)
  local copies, waits for them, and re-layouts  11.9 us (10%)
  between operations  1.53 us (1%)
    pallas_call x1, Pallas kernels, per_device(): pl.pallas_call(functools.partial(backward_kernel, n, (groups, tiles)), ou...  15.2 us
    ppermute x6, waiting for transfers between devices, sum_over_devices(): lax.ppermute(sums[x, y], both, joint_perm(groups, tiles, lambda g, t: (g...  13.7 us
    pallas_call x1, Pallas kernels, per_device(): pl.pallas_call(functools.partial(inner_network_kernel, n), out_shape=[*st...  11.3 us
    unnamed x31, local copies, waits for them, and re-layouts  11.1 us
    ppermute x4, starting transfers between devices, sum_over_devices(): lax.ppermute(total[half:], 'tile', [(t, t ^ step) for t in range(tiles)])  8.92 us
    pallas_call x1, Pallas kernels, per_device(): pl.pallas_call(functools.partial(inner_transport_kernel, n, levels), out_...  8.53 us
    pallas_call x1, Pallas kernels, per_device(): pl.pallas_call(functools.partial(rim_kernel, n, levels), out_shape=[*stat...  8.15 us
    ppermute x6, starting transfers between devices, sum_over_devices(): lax.ppermute(sums[x, y], both, joint_perm(groups, tiles, lambda g, t: (g...  8.05 us
  transfers between devices with their start and end apart: 17, of which 5 were waited for; matrix products, arithmetic and copies ran while one was open for 2% of the time, Pallas kernels for 34%

profile of v3, /device:TPU:0, one launch (start us, length us, event | category | flops | bytes accessed | tf_op | source)
XLA Modules:
  0.0 117.7 jit_solution(12394637245634061847)
XLA Ops:
  1.3 0.0 copy-start
  1.3 1.9 %copy-done = f32[32,32,768]{2,1,0:T(8,128)S(1)} copy-done((f32[32,32,768]{2,1,0:T(8,128)S(1)}, f32[32,32,768]{2,1,0:T(8,128)}, u32[]{:S(2)}) %copy-start) | copy-done | bytes 3145752
  3.2 0.8 pack_strips.1
  3.9 0.5 collective-permute-start
  4.5 2.0 %collective-permute-start.1 = (f32[64,768]{1,0:T(8,128)S(1)}, f32[64,768]{1,0:T(8,128)S(1)}, u32[]{:S(2)}, u32[]{:S(2)}) collective-permute-start(f32[64,768]{1,0:T(8,128)S(1)} %get-tuple-element.27), channel_id=1, source_target_pairs={{0,24},{8,0},{16,8},{24,16},{1,25},{9,1},{17,9},{25,17},{2,26},{10... | collective-permute-start | bytes 589832 | tf_op jit(solution)/shard_map/ppermute | solution.py:495
  6.5 0.0 copy-done.1
  6.5 8.5 %inner_transport.1 = (f32[32,32,768]{2,1,0:T(8,128)S(1)}, f32[512,768]{1,0:T(8,128)S(1)}, f32[8,128]{1,0:T(8,128)S(1)}) custom-call(s32[1,1]{1,0:T(1,128)S(6)} %copy.17.turn, f32[1024,768]{1,0:T(8,128)S(1)} %bitcast.47), custom_call_target="tpu_custom_call" | custom-call | flops 47185920 | bytes 16777216 | tf_op jit(solution)/shard_map/inner_transport/pallas_call | solution.py:497
  15.0 0.0 collective-permute-done.h1
  15.0 0.0 collective-permute-done.1.h3
  15.0 0.8 pack_strips_corners.1
  15.8 2.3 %collective-permute-start.2 = (f32[72,768]{1,0:T(8,128)S(1)}, f32[72,768]{1,0:T(8,128)S(1)}, u32[]{:S(2)}, u32[]{:S(2)}) collective-permute-start(f32[72,768]{1,0:T(8,128)S(1)} %get-tuple-element.29), channel_id=1, source_target_pairs={{0,1},{1,2},{2,3},{3,4},{4,5},{5,6},{6,7},{7,0},{8,9},{9,10},{10,1... | collective-permute-start | bytes 663560 | tf_op jit(solution)/shard_map/ppermute | solution.py:524
  18.2 3.3 %collective-permute-start.3 = (f32[72,768]{1,0:T(8,128)S(1)}, f32[72,768]{1,0:T(8,128)S(1)}, u32[]{:S(2)}, u32[]{:S(2)}) collective-permute-start(f32[72,768]{1,0:T(8,128)S(1)} %get-tuple-element.30), channel_id=1, source_target_pairs={{0,7},{1,0},{2,1},{3,2},{4,3},{5,4},{6,5},{7,6},{8,15},{9,8},{10,9... | collective-permute-start | bytes 663560 | tf_op jit(solution)/shard_map/ppermute | solution.py:525
  21.5 0.0 copy-done.2
  21.5 0.0 copy-done.3
  21.5 0.0 copy-done.5
  21.5 0.0 copy-done.11
  21.5 11.3 %inner_network.1 = (bf16[3,896,768]{2,1,0:T(8,128)(2,1)}, f32[3,896,128]{2,1,0:T(8,128)}, bf16[3,896,512]{2,1,0:T(8,128)(2,1)}, bf16[3,896,512]{2,1,0:T(8,128)(2...) custom-call(s32[32,32]{1,0:T(8,128)S(1)} %copy-done.5, s32[1,1]{1,0:T(1,128)S(6)} %copy.17.turn, ...), custom_call_target="tpu_custom_call" | custom-call | flops 3523215360 | bytes 16777216 | tf_op jit(solution)/shard_map/inner_network/pallas_call | solution.py:527
  32.8 0.0 collective-permute-done.2.h0
  32.8 0.0 collective-permute-done.3.h2
  32.8 8.1 %rim_columns.1 = (bf16[3,256,768]{2,1,0:T(8,128)(2,1)}, f32[3,256,128]{2,1,0:T(8,128)}, bf16[3,256,512]{2,1,0:T(8,128)(2,1)}, bf16[3,256,512]{2,1,0:T(8,128)(2,1...) custom-call(s32[1,1]{1,0:T(1,128)S(6)} %copy.17.turn, ...), custom_call_target="tpu_custom_call", output_to_operand_aliasing={{4}: (10, {})} | custom-call | flops 1006632960 | bytes 20971520 | tf_op jit(solution)/shard_map/rim_columns/pallas_call | solution.py:546
  40.9 0.0 copy-start.10
  40.9 3.3 %all-to-all-start = ((f32[32,32,512]{2,1,0:T(8,128)}), f32[32,32,512]{2,1,0:T(8,128)S(1)}, u32[]{:S(2)}, u32[]{:S(2)}) async-start(f32[32,32,512]{2,1,0:T(8,128)} %bitcast.55), calls=%async_computation | async-start | bytes 4194304 | tf_op jit(solution)/shard_map/all_to_all | solution.py:565
  44.2 0.1 pad_add_fusion.me
  44.3 1.1 copy-done.4
  45.5 1.9 %copy-done.6 = f32[32,32,768]{2,1,0:T(8,128)S(1)} copy-done((f32[32,32,768]{2,1,0:T(8,128)S(1)}, f32[32,32,768]{2,1,0:T(8,128)}, u32[]{:S(2)}) %copy-start.6) | copy-done | bytes 3145752
  47.3 1.3 %copy-done.7 = bf16[3,256,768]{2,1,0:T(8,128)(2,1)S(1)} copy-done((bf16[3,256,768]{2,1,0:T(8,128)(2,1)S(1)}, bf16[3,256,768]{2,1,0:T(8,128)(2,1)}, u32[]{:S(2)}) %copy-start.7) | copy-done | bytes 1179672
  48.6 1.1 copy-done.9
  49.7 1.8 %copy-done.13 = bf16[3,896,512]{2,1,0:T(8,128)(2,1)S(1)} copy-done((bf16[3,896,512]{2,1,0:T(8,128)(2,1)S(1)}, bf16[3,896,512]{2,1,0:T(8,128)(2,1)}, u32[]{:S(2)}) %copy-start.13) | copy-done | bytes 2752536
  51.5 1.3 %copy-done.14 = f32[3,896,128]{2,1,0:T(8,128)S(1)} copy-done((f32[3,896,128]{2,1,0:T(8,128)S(1)}, f32[3,896,128]{2,1,0:T(8,128)}, u32[]{:S(2)}) %copy-start.14) | copy-done | bytes 1376280
  52.9 15.2 %columns_backward.1 = (f32[16,48,256]{2,1,0:T(8,128)S(1)}, f32[16,48,256]{2,1,0:T(8,128)S(1)}, bf16[3,1152,768]{2,1,0:T(8,128)(2,1)S(1)}) custom-call(s32[2]{0:T(128)S(1)} %pad_add_fusion.me, s32[1,1]{1,0:T(1,128)S(6)} %copy.17.turn, f32[1024,768]{1,0:T(8,128)S(1)} %bitcast.50, bf16[768,512]{1,0:T(8,128)(2,1)S(1)} %copy-done.4, ...), custom_call_target="tpu_custom_call" | custom-call | flops 6442450944 | bytes 20971520 | tf_op jit(solution)/shard_map/columns_backward/pallas_call | solution.py:574
  68.1 0.1 collective-permute-start.4
  68.2 0.0 copy-done.8
  68.2 5.5 %output_gradient.1 = (f32[16,48,256]{2,1,0:T(8,128)S(1)}, f32[16,48,256]{2,1,0:T(8,128)S(1)}) custom-call(s32[2]{0:T(128)S(1)} %pad_add_fusion.me, bf16[3,1152,768]{2,1,0:T(8,128)(2,1)S(1)} %get-tuple-element.44.err_out, bf16[3,896,512]{2,1,0:T(8,128)(2,1)S(1)} %copy-done.12, bf16[3,256,512]{2,1,0:T(8,128)(2,1)S(1)} %copy-done.8), custom_call_target="tpu_custom_call" | custom-call | flops 2415919104 | bytes 8388608 | tf_op jit(solution)/shard_map/output_gradient/pallas_call | solution.py:593
  73.7 0.5 collective-permute-start.10
  74.2 0.0 collective-permute-done.4
  74.2 0.1 add.36
  74.4 1.6 %collective-permute-start.5 = (f32[4,48,256]{2,1,0:T(8,128)S(1)}, f32[4,48,256]{2,1,0:T(8,128)S(1)}, u32[]{:S(2)}, u32[]{:S(2)}) collective-permute-start(f32[4,48,256]{2,1,0:T(8,128)S(1)} %get-tuple-element.52), channel_id=1, source_target_pairs={{0,1},{1,0},{2,3},{3,2},{4,5},{5,4},{6,7},{7,6},{8,9},{9,8},{10,11... | collective-permute-start | bytes 589832 | tf_op jit(solution)/shard_map/ppermute | solution.py:436
  76.0 1.5 %collective-permute-start.7 = (f32[4,48,256]{2,1,0:T(8,128)S(1)}, f32[4,48,256]{2,1,0:T(8,128)S(1)}, u32[]{:S(2)}, u32[]{:S(2)}) collective-permute-start(f32[4,48,256]{2,1,0:T(8,128)S(1)} %get-tuple-element.53), channel_id=1, source_target_pairs={{0,17},{1,16},{2,19},{3,18},{4,21},{5,20},{6,23},{7,22},{8,25},{9,... | collective-permute-start | bytes 589832 | tf_op jit(solution)/shard_map/ppermute | solution.py:436
  77.5 0.5 collective-permute-start.6
  77.9 0.0 collective-permute-done.10
  78.0 0.1 add.42
  78.1 1.6 %collective-permute-start.11 = (f32[4,48,256]{2,1,0:T(8,128)S(1)}, f32[4,48,256]{2,1,0:T(8,128)S(1)}, u32[]{:S(2)}, u32[]{:S(2)}) collective-permute-start(f32[4,48,256]{2,1,0:T(8,128)S(1)} %get-tuple-element.49), channel_id=1, source_target_pairs={{0,1},{1,0},{2,3},{3,2},{4,5},{5,4},{6,7},{7,6},{8,9},{9,8},{10,11... | collective-permute-start | bytes 589832 | tf_op jit(solution)/shard_map/ppermute | solution.py:436
  79.7 1.5 %collective-permute-start.13 = (f32[4,48,256]{2,1,0:T(8,128)S(1)}, f32[4,48,256]{2,1,0:T(8,128)S(1)}, u32[]{:S(2)}, u32[]{:S(2)}) collective-permute-start(f32[4,48,256]{2,1,0:T(8,128)S(1)} %get-tuple-element.50), channel_id=1, source_target_pairs={{0,17},{1,16},{2,19},{3,18},{4,21},{5,20},{6,23},{7,22},{8,25},{9,... | collective-permute-start | bytes 589832 | tf_op jit(solution)/shard_map/ppermute | solution.py:436
  81.2 13.2 %collective-permute-done.5 = f32[4,48,256]{2,1,0:T(8,128)S(1)} collective-permute-done((f32[4,48,256]{2,1,0:T(8,128)S(1)}, f32[4,48,256]{2,1,0:T(8,128)S(1)}, u32[]{:S(2)}, u32[]{:S(2)}) %collective-permute-start.5) | collective-permute-done | bytes 196640 | tf_op jit(solution)/shard_map/ppermute | solution.py:436
  94.4 1.4 %collective-permute-start.12 = (f32[4,48,256]{2,1,0:T(8,128)S(1)}, f32[4,48,256]{2,1,0:T(8,128)S(1)}, u32[]{:S(2)}, u32[]{:S(2)}) collective-permute-start(f32[4,48,256]{2,1,0:T(8,128)S(1)} %get-tuple-element.51), channel_id=1, source_target_pairs={{0,16},{1,17},{2,18},{3,19},{4,20},{5,21},{6,22},{7,23},{8,24},{9,... | collective-permute-start | bytes 589832 | tf_op jit(solution)/shard_map/ppermute | solution.py:436
  95.8 0.0 collective-permute-done.7
  95.8 0.0 collective-permute-done.6
  95.9 0.1 fusion.5
  95.9 3.7 %collective-permute-start.8 = (f32[2,48,256]{2,1,0:T(8,128)S(1)}, f32[2,48,256]{2,1,0:T(8,128)S(1)}, u32[]{:S(2)}, u32[]{:S(2)}) collective-permute-start(f32[2,48,256]{2,1,0:T(8,128)S(1)} %slice.69), channel_id=1, source_target_pairs={{0,2},{1,3},{2,0},{3,1},{4,6},{5,7},{6,4},{7,5},{8,10},{9,11},{10,... | collective-permute-start | bytes 294920 | tf_op jit(solution)/shard_map/ppermute | solution.py:442
  99.6 0.0 collective-permute-done.11
  99.6 0.0 collective-permute-done.13
  99.6 0.5 collective-permute-done.12
  100.1 0.1 fusion.2
  100.2 5.1 %collective-permute-start.14 = (f32[2,48,256]{2,1,0:T(8,128)S(1)}, f32[2,48,256]{2,1,0:T(8,128)S(1)}, u32[]{:S(2)}, u32[]{:S(2)}) collective-permute-start(f32[2,48,256]{2,1,0:T(8,128)S(1)} %slice.77), channel_id=1, source_target_pairs={{0,2},{1,3},{2,0},{3,1},{4,6},{5,7},{6,4},{7,5},{8,10},{9,11},{10,... | collective-permute-start | bytes 294920 | tf_op jit(solution)/shard_map/ppermute | solution.py:442
  105.3 0.0 collective-permute-done.8
  105.3 0.1 collective-permute-start.9
  105.4 3.0 %collective-permute-done.14 = f32[2,48,256]{2,1,0:T(8,128)S(1)} collective-permute-done((f32[2,48,256]{2,1,0:T(8,128)S(1)}, f32[2,48,256]{2,1,0:T(8,128)S(1)}, u32[]{:S(2)}, u32[]{:S(2)}) %collective-permute-start.14) | collective-permute-done | bytes 98336 | tf_op jit(solution)/shard_map/ppermute | solution.py:442
  108.4 0.1 collective-permute-start.15
  108.5 2.9 %collective-permute-done.9 = f32[1,48,256]{2,1,0:T(8,128)S(1)} collective-permute-done((f32[1,48,256]{2,1,0:T(8,128)S(1)}, f32[1,48,256]{2,1,0:T(8,128)S(1)}, u32[]{:S(2)}, u32[]{:S(2)}) %collective-permute-start.9) | collective-permute-done | bytes 49184 | tf_op jit(solution)/shard_map/ppermute | solution.py:442
  111.4 0.6 copy.13
  112.1 1.4 %collective-permute-done.15 = f32[1,48,256]{2,1,0:T(8,128)S(1)} collective-permute-done((f32[1,48,256]{2,1,0:T(8,128)S(1)}, f32[1,48,256]{2,1,0:T(8,128)S(1)}, u32[]{:S(2)}, u32[]{:S(2)}) %collective-permute-start.15) | collective-permute-done | bytes 49184 | tf_op jit(solution)/shard_map/ppermute | solution.py:442
  113.5 0.6 reshape.37
  114.2 0.0 all-to-all-done
  114.2 3.5 %tendency_rows.1 = f32[1024,768]{1,0:T(8,128)} custom-call(f32[1024,512]{1,0:T(8,128)S(1)} %bitcast.49, bf16[512,768]{1,0:T(8,128)(2,1)S(1)} %copy-done.2), custom_call_target="tpu_custom_call" | custom-call | flops 1610612736 | bytes 6291456 | tf_op jit(solution)/shard_map/tendency_rows/pallas_call | solution.py:613
  (27 shorter events, 0.2 us)
Async XLA Ops:
  1.3 1.9 %copy-start = (f32[32,32,768]{2,1,0:T(8,128)S(1)}, f32[32,32,768]{2,1,0:T(8,128)}, u32[]{:S(2)}) copy-start(f32[32,32,768]{2,1,0:T(8,128)} %param.7) | copy-start | bytes 9437188
  3.2 3.3 %copy-start.1 = (f32[32,32,768]{2,1,0:T(8,128)S(1)}, f32[32,32,768]{2,1,0:T(8,128)}, u32[]{:S(2)}) copy-start(f32[32,32,768]{2,1,0:T(8,128)} %param.7) | copy-start | bytes 9437188
  3.9 11.1 %collective-permute-start = (f32[64,768]{1,0:T(8,128)S(1)}, f32[64,768]{1,0:T(8,128)S(1)}, u32[]{:S(2)}, u32[]{:S(2)}) collective-permute-start(f32[64,768]{1,0:T(8,128)S(1)} %get-tuple-element.26), channel_id=1, source_target_pairs={{0,8},{8,16},{16,24},{24,0},{1,9},{9,17},{17,25},{25,1},{2,10},{10... | collective-permute-start | bytes 589832 | tf_op jit(solution)/shard_map/ppermute | solution.py:494
  4.4 17.0 %copy-start.2 = (bf16[512,768]{1,0:T(8,128)(2,1)S(1)}, bf16[512,768]{1,0:T(8,128)(2,1)}, u32[]{:S(2)}) copy-start(bf16[512,768]{1,0:T(8,128)(2,1)} %w_out.7) | copy-start | bytes 2359300
  4.4 17.0 %copy-start.3 = (bf16[768,512]{1,0:T(8,128)(2,1)S(1)}, bf16[768,512]{1,0:T(8,128)(2,1)}, u32[]{:S(2)}) copy-start(bf16[768,512]{1,0:T(8,128)(2,1)} %w_in.5) | copy-start | bytes 2359300
  4.4 17.0 %copy-start.5 = (s32[32,32]{1,0:T(8,128)S(1)}, s32[32,32]{1,0:T(8,128)}, u32[]{:S(2)}) copy-start(s32[32,32]{1,0:T(8,128)} %dest.3) | copy-start | bytes 12292
  4.5 17.0 %copy-start.11 = (s32[32,32]{1,0:T(8,128)S(1)}, s32[32,32]{1,0:T(8,128)}, u32[]{:S(2)}) copy-start(s32[32,32]{1,0:T(8,128)} %cost.1) | copy-start | bytes 12292
  4.5 10.6 %collective-permute-start.1 = (f32[64,768]{1,0:T(8,128)S(1)}, f32[64,768]{1,0:T(8,128)S(1)}, u32[]{:S(2)}, u32[]{:S(2)}) collective-permute-start(f32[64,768]{1,0:T(8,128)S(1)} %get-tuple-element.27), channel_id=1, source_target_pairs={{0,24},{8,0},{16,8},{24,16},{1,25},{9,1},{17,9},{25,17},{2,26},{10... | collective-permute-start | bytes 589832 | tf_op jit(solution)/shard_map/ppermute | solution.py:495
  15.8 16.9 %collective-permute-start.2 = (f32[72,768]{1,0:T(8,128)S(1)}, f32[72,768]{1,0:T(8,128)S(1)}, u32[]{:S(2)}, u32[]{:S(2)}) collective-permute-start(f32[72,768]{1,0:T(8,128)S(1)} %get-tuple-element.29), channel_id=1, source_target_pairs={{0,1},{1,2},{2,3},{3,4},{4,5},{5,6},{6,7},{7,0},{8,9},{9,10},{10,1... | collective-permute-start | bytes 663560 | tf_op jit(solution)/shard_map/ppermute | solution.py:524
  18.2 14.6 %collective-permute-start.3 = (f32[72,768]{1,0:T(8,128)S(1)}, f32[72,768]{1,0:T(8,128)S(1)}, u32[]{:S(2)}, u32[]{:S(2)}) collective-permute-start(f32[72,768]{1,0:T(8,128)S(1)} %get-tuple-element.30), channel_id=1, source_target_pairs={{0,7},{1,0},{2,1},{3,2},{4,3},{5,4},{6,5},{7,6},{8,15},{9,8},{10,9... | collective-permute-start | bytes 663560 | tf_op jit(solution)/shard_map/ppermute | solution.py:525
  40.9 3.4 %copy-start.10 = (f32[3,256,128]{2,1,0:T(8,128)S(1)}, f32[3,256,128]{2,1,0:T(8,128)}, u32[]{:S(2)}) copy-start(f32[3,256,128]{2,1,0:T(8,128)} %get-tuple-element.40.in_sr) | copy-start | bytes 1179652
  40.9 73.2 %all-to-all-start = ((f32[32,32,512]{2,1,0:T(8,128)}), f32[32,32,512]{2,1,0:T(8,128)S(1)}, u32[]{:S(2)}, u32[]{:S(2)}) async-start(f32[32,32,512]{2,1,0:T(8,128)} %bitcast.55), calls=%async_computation | async-start | bytes 4194304 | tf_op jit(solution)/shard_map/all_to_all | solution.py:565
  44.3 1.1 copy-start.4
  45.5 1.9 %copy-start.6 = (f32[32,32,768]{2,1,0:T(8,128)S(1)}, f32[32,32,768]{2,1,0:T(8,128)}, u32[]{:S(2)}) copy-start(f32[32,32,768]{2,1,0:T(8,128)} %param.8) | copy-start | bytes 9437188
  47.3 1.3 %copy-start.7 = (bf16[3,256,768]{2,1,0:T(8,128)(2,1)S(1)}, bf16[3,256,768]{2,1,0:T(8,128)(2,1)}, u32[]{:S(2)}) copy-start(bf16[3,256,768]{2,1,0:T(8,128)(2,1)} %get-tuple-element.39.in_nr) | copy-start | bytes 3538948
  48.6 1.1 copy-start.9
  49.7 1.8 %copy-start.13 = (bf16[3,896,512]{2,1,0:T(8,128)(2,1)S(1)}, bf16[3,896,512]{2,1,0:T(8,128)(2,1)}, u32[]{:S(2)}) copy-start(bf16[3,896,512]{2,1,0:T(8,128)(2,1)} %get-tuple-element.38.in_gi) | copy-start | bytes 8257540
  51.5 1.3 %copy-start.14 = (f32[3,896,128]{2,1,0:T(8,128)S(1)}, f32[3,896,128]{2,1,0:T(8,128)}, u32[]{:S(2)}) copy-start(f32[3,896,128]{2,1,0:T(8,128)} %get-tuple-element.37.in_si) | copy-start | bytes 4128772
  52.9 15.3 %copy-start.8 = (bf16[3,256,512]{2,1,0:T(8,128)(2,1)S(1)}, bf16[3,256,512]{2,1,0:T(8,128)(2,1)}, u32[]{:S(2)}) copy-start(bf16[3,256,512]{2,1,0:T(8,128)(2,1)} %get-tuple-element.46.in_hr) | copy-start | bytes 2359300
  52.9 15.3 %copy-start.12 = (bf16[3,896,512]{2,1,0:T(8,128)(2,1)S(1)}, bf16[3,896,512]{2,1,0:T(8,128)(2,1)}, u32[]{:S(2)}) copy-start(bf16[3,896,512]{2,1,0:T(8,128)(2,1)} %get-tuple-element.45.in_hi) | copy-start | bytes 8257540
  68.1 6.2 %collective-permute-start.4 = (f32[16,48,256]{2,1,0:T(8,128)S(1)}, f32[16,48,256]{2,1,0:T(8,128)S(1)}, u32[]{:S(2)}, u32[]{:S(2)}) collective-permute-start(f32[16,48,256]{2,1,0:T(8,128)S(1)} %get-tuple-element.43), channel_id=1, source_target_pairs={{0,8},{8,0},{16,24},{24,16},{1,9},{9,1},{17,25},{25,17},{2,10},{10... | collective-permute-start | bytes 2359304 | tf_op jit(solution)/shard_map/ppermute | solution.py:430
  73.7 4.3 %collective-permute-start.10 = (f32[16,48,256]{2,1,0:T(8,128)S(1)}, f32[16,48,256]{2,1,0:T(8,128)S(1)}, u32[]{:S(2)}, u32[]{:S(2)}) collective-permute-start(f32[16,48,256]{2,1,0:T(8,128)S(1)} %get-tuple-element.48), channel_id=1, source_target_pairs={{0,8},{8,0},{16,24},{24,16},{1,9},{9,1},{17,25},{25,17},{2,10},{10... | collective-permute-start | bytes 2359304 | tf_op jit(solution)/shard_map/ppermute | solution.py:430
  74.4 20.0 %collective-permute-start.5 = (f32[4,48,256]{2,1,0:T(8,128)S(1)}, f32[4,48,256]{2,1,0:T(8,128)S(1)}, u32[]{:S(2)}, u32[]{:S(2)}) collective-permute-start(f32[4,48,256]{2,1,0:T(8,128)S(1)} %get-tuple-element.52), channel_id=1, source_target_pairs={{0,1},{1,0},{2,3},{3,2},{4,5},{5,4},{6,7},{7,6},{8,9},{9,8},{10,11... | collective-permute-start | bytes 589832 | tf_op jit(solution)/shard_map/ppermute | solution.py:436
  76.0 19.8 %collective-permute-start.7 = (f32[4,48,256]{2,1,0:T(8,128)S(1)}, f32[4,48,256]{2,1,0:T(8,128)S(1)}, u32[]{:S(2)}, u32[]{:S(2)}) collective-permute-start(f32[4,48,256]{2,1,0:T(8,128)S(1)} %get-tuple-element.53), channel_id=1, source_target_pairs={{0,17},{1,16},{2,19},{3,18},{4,21},{5,20},{6,23},{7,22},{8,25},{9,... | collective-permute-start | bytes 589832 | tf_op jit(solution)/shard_map/ppermute | solution.py:436
  77.5 18.4 %collective-permute-start.6 = (f32[4,48,256]{2,1,0:T(8,128)S(1)}, f32[4,48,256]{2,1,0:T(8,128)S(1)}, u32[]{:S(2)}, u32[]{:S(2)}) collective-permute-start(f32[4,48,256]{2,1,0:T(8,128)S(1)} %get-tuple-element.54), channel_id=1, source_target_pairs={{0,16},{1,17},{2,18},{3,19},{4,20},{5,21},{6,22},{7,23},{8,24},{9,... | collective-permute-start | bytes 589832 | tf_op jit(solution)/shard_map/ppermute | solution.py:436
  78.1 21.5 %collective-permute-start.11 = (f32[4,48,256]{2,1,0:T(8,128)S(1)}, f32[4,48,256]{2,1,0:T(8,128)S(1)}, u32[]{:S(2)}, u32[]{:S(2)}) collective-permute-start(f32[4,48,256]{2,1,0:T(8,128)S(1)} %get-tuple-element.49), channel_id=1, source_target_pairs={{0,1},{1,0},{2,3},{3,2},{4,5},{5,4},{6,7},{7,6},{8,9},{9,8},{10,11... | collective-permute-start | bytes 589832 | tf_op jit(solution)/shard_map/ppermute | solution.py:436
  79.7 19.9 %collective-permute-start.13 = (f32[4,48,256]{2,1,0:T(8,128)S(1)}, f32[4,48,256]{2,1,0:T(8,128)S(1)}, u32[]{:S(2)}, u32[]{:S(2)}) collective-permute-start(f32[4,48,256]{2,1,0:T(8,128)S(1)} %get-tuple-element.50), channel_id=1, source_target_pairs={{0,17},{1,16},{2,19},{3,18},{4,21},{5,20},{6,23},{7,22},{8,25},{9,... | collective-permute-start | bytes 589832 | tf_op jit(solution)/shard_map/ppermute | solution.py:436
  94.4 5.7 %collective-permute-start.12 = (f32[4,48,256]{2,1,0:T(8,128)S(1)}, f32[4,48,256]{2,1,0:T(8,128)S(1)}, u32[]{:S(2)}, u32[]{:S(2)}) collective-permute-start(f32[4,48,256]{2,1,0:T(8,128)S(1)} %get-tuple-element.51), channel_id=1, source_target_pairs={{0,16},{1,17},{2,18},{3,19},{4,20},{5,21},{6,22},{7,23},{8,24},{9,... | collective-permute-start | bytes 589832 | tf_op jit(solution)/shard_map/ppermute | solution.py:436
  95.9 9.3 %collective-permute-start.8 = (f32[2,48,256]{2,1,0:T(8,128)S(1)}, f32[2,48,256]{2,1,0:T(8,128)S(1)}, u32[]{:S(2)}, u32[]{:S(2)}) collective-permute-start(f32[2,48,256]{2,1,0:T(8,128)S(1)} %slice.69), channel_id=1, source_target_pairs={{0,2},{1,3},{2,0},{3,1},{4,6},{5,7},{6,4},{7,5},{8,10},{9,11},{10,... | collective-permute-start | bytes 294920 | tf_op jit(solution)/shard_map/ppermute | solution.py:442
  100.2 8.2 %collective-permute-start.14 = (f32[2,48,256]{2,1,0:T(8,128)S(1)}, f32[2,48,256]{2,1,0:T(8,128)S(1)}, u32[]{:S(2)}, u32[]{:S(2)}) collective-permute-start(f32[2,48,256]{2,1,0:T(8,128)S(1)} %slice.77), channel_id=1, source_target_pairs={{0,2},{1,3},{2,0},{3,1},{4,6},{5,7},{6,4},{7,5},{8,10},{9,11},{10,... | collective-permute-start | bytes 294920 | tf_op jit(solution)/shard_map/ppermute | solution.py:442
  105.3 6.1 %collective-permute-start.9 = (f32[1,48,256]{2,1,0:T(8,128)S(1)}, f32[1,48,256]{2,1,0:T(8,128)S(1)}, u32[]{:S(2)}, u32[]{:S(2)}) collective-permute-start(f32[1,48,256]{2,1,0:T(8,128)S(1)} %slice.71), channel_id=1, source_target_pairs={{0,4},{1,5},{2,6},{3,7},{4,0},{5,1},{6,2},{7,3},{8,12},{9,13},{10,... | collective-permute-start | bytes 147464 | tf_op jit(solution)/shard_map/ppermute | solution.py:442
  108.4 5.1 %collective-permute-start.15 = (f32[1,48,256]{2,1,0:T(8,128)S(1)}, f32[1,48,256]{2,1,0:T(8,128)S(1)}, u32[]{:S(2)}, u32[]{:S(2)}) collective-permute-start(f32[1,48,256]{2,1,0:T(8,128)S(1)} %slice.79), channel_id=1, source_target_pairs={{0,4},{1,5},{2,6},{3,7},{4,0},{5,1},{6,2},{7,3},{8,12},{9,13},{10,... | collective-permute-start | bytes 147464 | tf_op jit(solution)/shard_map/ppermute | solution.py:442

commit v4 on v3

--- a/solution.py
+++ b/solution.py
@@ -125,31 +125,54 @@
 
 def network_forward(x, mask, w_in, w_out, state, hsum, rows, kept):
     normed, scale, slope, hidden = state
-    total = None
+    x, total = x(), None
     for use in range(3):
         inv = lax.rsqrt(jnp.mean(x * x, axis=1, keepdims=True) + EPS)
         unit = (x * inv).astype(BF16)
         normed[use, rows, :] = unit
-        scale[use, rows, :] = mask if use == 0 else jnp.broadcast_to(inv, (x.shape[0], LANES))
-        p = jnp.dot(unit, w_in, preferred_element_type=F32)
+        if use == 0:
+            packed = mask()
+            lane = lax.broadcasted_iota(jnp.int32, packed.shape, 1)
+        else:
+            packed = jnp.where(lane < 32 * use, packed, inv)
+        yield
+        p = jnp.dot(unit, w_in[...], preferred_element_type=F32)
+        yield
         s = 0.5 + 0.5 * jnp.tanh(0.5 * p)
         silu = p * s
-        slope[use, rows, :] = (s + silu * (1.0 - s)).astype(BF16)
+        slope[use, rows, :] = s + silu * (1.0 - s)
         h = silu.astype(BF16)
         hidden[use, rows, :] = h
+        if use == 2:
+            scale[rows, :] = packed
         kept(use)
         if use < 2:
             total = h.astype(F32) if use == 0 else total + h.astype(F32)
-            x = x + TAU * jnp.dot(h, w_out, preferred_element_type=F32)
+            yield
+            x = x + TAU * jnp.dot(h, w_out[...], preferred_element_type=F32)
+            yield
         else:
-            hsum[rows, :] = total + h.astype(F32) * mask[:, 0:1]
+            hsum[rows, :] = total + h.astype(F32) * mask()[:, 0:1]
+
+
+def run_together(steps, lag):
+    steps = list(steps)
+    live, tick = set(range(len(steps))), 0
+    while live:
+        for i in sorted(live):
+            if tick >= lag * i and next(steps[i], 1) == 1:
+                live.discard(i)
+        tick += 1
 
 
 def state_copies(source, target, sems, use, part, rows):
-    return [
-        pltpu.make_async_copy(a.at[use, rows, :], b.at[use, rows, :], sems.at[part, use, i])
-        for i, (a, b) in enumerate(zip(source, target))
-    ]
+    copies = []
+    for i, (a, b) in enumerate(zip(source, target)):
+        if i == 1 and use < 2:
+            continue
+        at = (rows, slice(None)) if i == 1 else (use, rows, slice(None))
+        copies.append(pltpu.make_async_copy(a.at[at], b.at[at], sems.at[part, use, i]))
+    return copies
 
 
 def pack_strip(n, levels, k, o, air, out):
@@ -200,10 +223,14 @@
     lax.fori_loop(0, n, mask_row, 0, unroll=8)
 
 
+PARTS = 2
+LAG = 0
+
+
 def inner_parts(n):
-    inner, parts = n - 4, 2
-    size = inner // parts * n
-    return [(part, part * size, size) for part in range(parts)]
+    inner = n - 4
+    size = inner // PARTS * n
+    return [(part, part * size, size) for part in range(PARTS)]
 
 
 def inner_network_kernel(n, dest, turn, moved, cost, w_in, w_out, n_o, s_o, g_o, h_o, outgoing, mask_rim,
@@ -216,17 +243,19 @@
         for d in range(2):
             copy_rows(mask_rim, (k * 2 + d) * n, mask, base + cd * d, cm, n)
     copies = []
+    steps = []
     for part, start, size in inner_parts(n):
         rows = slice(start, start + size)
-        x = moved[2 + start // n : 2 + (start + size) // n, :, :].reshape(size, feats)
-        m = mask[2 * n + start : 2 * n + start + size, :]
+        x = lambda start=start, size=size: moved[2 + start // n : 2 + (start + size) // n, :, :].reshape(size, feats)
+        m = lambda start=start, size=size: mask[2 * n + start : 2 * n + start + size, :]
 
         def kept(use, part=part, rows=pl.ds(start, size)):
             for copy in state_copies(state, out, sems, use, part, rows):
                 copy.start()
                 copies.append(copy)
 
-        network_forward(x, m, w_in[...], w_out[...], state, hsum, rows, kept)
+        steps.append(network_forward(x, m, w_in, w_out, state, hsum, rows, kept))
+    run_together(steps, LAG)
 
     def place(i, carry):
         for j in range(2, n - 2):
@@ -284,7 +313,10 @@
             copy.start()
             copies.append(copy)
 
-    network_forward(x_rim[...], mask_rim[...], w_in[...], w_out[...], state, hsum, slice(0, 8 * n), kept)
+    rows = slice(0, 8 * n)
+    run_together(
+        [network_forward(lambda: x_rim[...], lambda: mask_rim[...], w_in, w_out, state, hsum, rows, kept)], 0
+    )
     for k in range(4):
         (bi, di, mi), (bj, dj, mj) = side_cells((k - o + 4) % 4, n)
         skip = 2 * (k % 2)
@@ -308,139 +340,137 @@
 
 
 def network_backward(cot, valid, w_in, w_out, state, err_out, err_in, rows, at, arrived):
-    normed, scale, slope, _ = state
-    arrived("chain")
-    cot = cot * valid
-    grad = cot * scale[0, rows, 0:1]
+    normed, scale, slope = state
+    arrived("cotangent")
+    cot = cot() * valid
+    grad = cot * scale[rows, 0:1]
     for use in (2, 1, 0):
         e = (TAU * grad).astype(BF16)
         err_out[use, at, :] = e
-        inner = (contract_last(e, w_out) * slope[use, rows, :].astype(F32)).astype(BF16)
+        yield
+        back = contract_last(e, w_out[...])
+        yield
+        arrived(("slope", use))
+        inner = (back * slope[use, rows, :]).astype(BF16)
         err_in[use, rows, :] = inner
+        yield
         if use > 0:
-            d = contract_last(inner, w_in)
+            d = contract_last(inner, w_in[...])
+            yield
+            arrived(("normed", use))
             unit = normed[use, rows, :].astype(F32)
-            d = scale[use, rows, 0:1] * (d - unit * jnp.mean(d * unit, axis=1, keepdims=True))
+            d = scale[rows, 32 * use : 32 * use + 1] * (d - unit * jnp.mean(d * unit, axis=1, keepdims=True))
             grad = (cot if use == 2 else grad) + d
 
 
-def store_pieces(grid_shape, me, grad, keep, send):
+def exchange_order(groups, tiles, tile_first):
+    bits = lambda axis, low, count: [(axis, low << b) for b in range(((count // low) - 1).bit_length())]
+    plane = [bits("grp", 2, groups), [("tile", 1)]]
+    first, second = plane[::-1] if tile_first else plane
+    return [("grp", 1)] + first + second + bits("tile", 2, tiles)
+
+
+def store_pieces(grid_shape, me, order, grad, keep, send):
     groups, tiles = grid_shape
     rows = grad.shape[0] // (groups * tiles)
-    bits = (tiles // 2).bit_length() - 1
     for g in range(groups):
         for t in range(tiles):
             p = g * tiles + t
-            rg, rt = me[0] ^ g, me[1] ^ t
-            at = (rg // 2) * 2 + rt % 2
-            for b in range(bits):
-                at = at * 2 + (rt >> (b + 1)) % 2
+            away = {"grp": me[0] ^ g, "tile": me[1] ^ t}
+            at = 0
+            for axis, bit in order[1:]:
+                at = at * 2 + (away[axis] // bit) % 2
 
             def store(ref, p=p, at=at):
                 for c in range(grad.shape[1] // COL):
                     ref[at, c * rows : (c + 1) * rows, :] = grad[p * rows : (p + 1) * rows, c * COL : (c + 1) * COL]
 
-            pl.when(rg % 2 == 0)(functools.partial(store, keep))
-            pl.when(rg % 2 == 1)(functools.partial(store, send))
-
-
-def backward_kernel(n, grid_shape, me, turn, cot_in, w_in, w_out, in_ni, in_si, in_gi, in_nr, in_sr, in_gr,
-                    keep, send, err_out, n_i, s_i, g_i, n_r, s_r, g_r, sems, ei_i, ei_r, cot, cot_rim, grad_in):
+            pl.when(away["grp"] % 2 == 0)(functools.partial(store, keep))
+            pl.when(away["grp"] % 2 == 1)(functools.partial(store, send))
+
+
+def backward_kernel(n, grid_shape, order, me, turn, cot_in, in_weights, out_weights, in_ni, in_si, in_gi, in_hi,
+                    in_nr, in_sr, in_gr, in_hr, keep, send, err_out, h, n_i, s_i, g_i, n_r, s_r, g_r, sems,
+                    w_in, w_out, ei_i, ei_r, cot, cot_rim, grad_in):
     o = turn[0, 0]
     parts = inner_parts(n)
     inner = (n - 4) * n
     edge = 2 * n
+    pairs = ((in_ni, n_i), (in_nr, n_r)), ((in_gi, g_i), (in_gr, g_r))
+    normed = lambda use: [(a.at[use], b.at[use]) for a, b in pairs[0]]
+    slope = lambda use: [(a.at[use], b.at[use]) for a, b in pairs[1]]
+    plan = [
+        ("cotangent", [(out_weights, w_out), (cot_in, cot), (in_si, s_i), (in_sr, s_r)]),
+        (("slope", 2), [(in_weights, w_in), *slope(2)]),
+        (("normed", 2), normed(2)),
+        (("slope", 1), slope(1)),
+        (("normed", 1), normed(1)),
+        (("slope", 0), slope(0)),
+        ("rest", [*normed(0), (in_hi, h.at[:, pl.ds(0, inner), :]), (in_hr, h.at[:, pl.ds(inner, 8 * n), :])]),
+    ]
     index = 0
-
-    def fetch(source, target):
+    flight = []
+
+    def start_next():
         nonlocal index
-        copy = pltpu.make_async_copy(source, target, sems.at[index])
-        index += 1
-        copy.start()
-        return copy
-
-    chain, late = {}, []
-    groups = [(part, (in_ni, in_si, in_gi), (n_i, s_i, g_i), start, size) for part, start, size in parts]
-    groups.append((len(parts), (in_nr, in_sr, in_gr), (n_r, s_r, g_r), 0, 8 * n))
-    for part, source, here, start, size in groups:
-        rows = pl.ds(start, size)
-        chain[part] = []
-        if part < len(parts):
-            at = pl.ds(edge + start, size)
-            chain[part].append(fetch(cot_in.at[at, :], cot.at[at, :]))
-        else:
-            for at in (pl.ds(0, edge), pl.ds(edge + inner, edge)):
-                chain[part].append(fetch(cot_in.at[at, :], cot.at[at, :]))
-        chain[part].append(fetch(source[1].at[:, rows, :], here[1].at[:, rows, :]))
-        chain[part].append(fetch(source[2].at[:, rows, :], here[2].at[:, rows, :]))
-        chain[part].append(fetch(source[0].at[pl.ds(1, 2), rows, :], here[0].at[pl.ds(1, 2), rows, :]))
-    for part, source, here, start, size in groups:
-        rows = pl.ds(start, size)
-        late.append(fetch(source[0].at[0, rows, :], here[0].at[0, rows, :]))
-
-    def wait_for(part):
-        def arrived(_):
-            for copy in chain[part]:
+        if plan:
+            name, refs = plan.pop(0)
+            copies = []
+            for source, target in refs:
+                copies.append(pltpu.make_async_copy(source, target, sems.at[index]))
+                copies[-1].start()
+                index += 1
+            flight.append((name, copies))
+
+    def arrived(name):
+        if flight and flight[0][0] == name:
+            for copy in flight.pop(0)[1]:
                 copy.wait()
-
-        return arrived
-
+            start_next()
+
+    start_next()
+    start_next()
+    steps = []
     for part, start, size in parts:
-        wait_for(part)(None)
         at = slice(edge + start, edge + start + size)
         j = lax.broadcasted_iota(jnp.int32, (size, 1), 0) % n
         valid = ((j >= 2) & (j < n - 2)).astype(F32)
-        network_backward(cot[at, :], valid, w_in[...], w_out[...], (n_i, s_i, g_i, None), err_out, ei_i,
-                         slice(start, start + size), slice(start, start + size), lambda _: None)
-    wait_for(len(parts))(None)
-    for k in range(4):
-        base, cm, cd = side_rows((k - o + 4) % 4, n)
-        for d in range(2):
-            copy_rows(cot_rim, (k * 2 + d) * n, cot, base + cd * d, cm, n)
+        rows = slice(start, start + size)
+        steps.append(network_backward(lambda at=at: cot[at, :], valid, w_in, w_out, (n_i, s_i, g_i), err_out, ei_i,
+                                      rows, rows, arrived))
+
+    def rim_cotangent():
+        for k in range(4):
+            base, cm, cd = side_rows((k - o + 4) % 4, n)
+            for d in range(2):
+                copy_rows(cot_rim, (k * 2 + d) * n, cot, base + cd * d, cm, n)
+        return cot_rim[...]
+
     e = lax.broadcasted_iota(jnp.int32, (8 * n, 1), 0)
     m = e % n
     valid = (((e // (2 * n)) % 2 == 0) | ((m >= 2) & (m < n - 2))).astype(F32)
-    network_backward(cot_rim[...], valid, w_in[...], w_out[...], (n_r, s_r, g_r, None), err_out, ei_r,
-                     slice(0, 8 * n), slice(inner, inner + 8 * n), lambda _: None)
-    for copy in late:
-        copy.wait()
+    steps.append(network_backward(rim_cotangent, valid, w_in, w_out, (n_r, s_r, g_r), err_out, ei_r,
+                                  slice(0, 8 * n), slice(inner, inner + 8 * n), arrived))
+    run_together(steps, LAG)
+    arrived("rest")
     flat = lambda ref: ref[...].reshape(ref.shape[0] * ref.shape[1], ref.shape[2])
     grad_in[...] = contract_rows(flat(n_i), flat(ei_i)) + contract_rows(flat(n_r), flat(ei_r))
-    store_pieces(grid_shape, me, grad_in, keep, send)
-
-
-def output_gradient_kernel(n, grid_shape, me, err_out, in_hi, in_hr, keep, send, h, grad_out, sems):
-    inner = (n - 4) * n
-    copies = []
-    for use in (2, 1, 0):
-        for source, rows in ((in_hi, pl.ds(0, inner)), (in_hr, pl.ds(inner, 8 * n))):
-            copy = pltpu.make_async_copy(source.at[use], h.at[use, rows, :], sems.at[len(copies)])
-            copy.start()
-            copies.append(copy)
-    for copy in copies:
-        copy.wait()
+    store_pieces(grid_shape, me, order, grad_in, keep, send)
+
+
+def output_gradient_kernel(grid_shape, order, me, err_out, h, keep, send, grad_out):
     flat = lambda ref: ref[...].reshape(ref.shape[0] * ref.shape[1], ref.shape[2])
     grad_out[...] = contract_rows(flat(h), flat(err_out))
-    store_pieces(grid_shape, me, grad_out, keep, send)
-
-
-def sum_over_devices(keep, send, groups, tiles):
-    both = ("grp", "tile")
-    piece = keep.shape[1:]
-    sums = keep + lax.ppermute(send, "grp", [(i, i ^ 1) for i in range(groups)])
-    sums = sums.reshape(groups // 2, 2, tiles // 2, *piece)
-    total = sums[0, 0]
-    for x in range(groups // 2):
-        for y in range(2):
-            if x or y:
-                total = total + lax.ppermute(
-                    sums[x, y], both, joint_perm(groups, tiles, lambda g, t: (g ^ (2 * x), t ^ y))
-                )
-    step = 2
-    while step < tiles:
-        half = total.shape[0] // 2
-        total = total[:half] + lax.ppermute(total[half:], "tile", [(t, t ^ step) for t in range(tiles)])
-        step *= 2
+    store_pieces(grid_shape, me, order, grad_out, keep, send)
+
+
+def sum_over_devices(keep, send, order, sizes):
+    total = None
+    for axis, bit in order:
+        if total is not None:
+            half = total.shape[0] // 2
+            keep, send = total[:half], total[half:]
+        total = keep + lax.ppermute(send, axis, [(i, i ^ bit) for i in range(sizes[axis])])
     return total[0]
 
 
@@ -477,8 +507,8 @@
     def state(space, rows):
         return [
             space((3, rows, feats), BF16),
-            space((3, rows, LANES), F32),
-            space((3, rows, units), BF16),
+            space((rows, LANES), F32),
+            space((3, rows, units), F32),
             space((3, rows, units), BF16),
         ]
 
@@ -567,19 +597,25 @@
     ).reshape(cells, units)
 
     me = jnp.stack([lax.axis_index("grp"), lax.axis_index("tile")]).astype(jnp.int32)
-    n_i, s_i, g_i, h_i = saved_inner
-    n_r, s_r, g_r, h_r = saved_rim
+    stay = lambda x: pltpu.with_memory_space_constraint(x, pltpu.HBM)
     saved = lambda rows: state(pltpu.VMEM, rows)[:3]
     halves = lambda rows, columns: [shape((count // 2, rows // count * (columns // COL), COL), F32)] * 2
-    *pieces_in, err_out = pl.pallas_call(
-        functools.partial(backward_kernel, n, (groups, tiles)),
-        out_shape=[*halves(feats, units), pltpu.VMEM((3, inner + rim, feats), BF16)],
-        in_specs=[SMEM, SMEM, HBM, VMEM, VMEM] + [HBM] * 6,
-        out_specs=[VMEM] * 3,
+    orders = [exchange_order(groups, tiles, tile_first) for tile_first in (False, True)]
+    *pieces_in, err_out, hidden = pl.pallas_call(
+        functools.partial(backward_kernel, n, (groups, tiles), orders[0]),
+        out_shape=[
+            *halves(feats, units),
+            pltpu.VMEM((3, inner + rim, feats), BF16),
+            pltpu.VMEM((3, inner + rim, units), BF16),
+        ],
+        in_specs=[SMEM, SMEM] + [HBM] * 11,
+        out_specs=[VMEM] * 4,
         scratch_shapes=[
             *saved(inner),
             *saved(rim),
-            pltpu.SemaphoreType.DMA((5 * parts + 6,)),
+            pltpu.SemaphoreType.DMA((19,)),
+            pltpu.VMEM((feats, units), BF16),
+            pltpu.VMEM((units, feats), BF16),
             pltpu.VMEM((3, inner, units), BF16),
             pltpu.VMEM((3, rim, units), BF16),
             pltpu.VMEM((cells, feats), F32),
@@ -589,25 +625,22 @@
         compiler_params=params(36),
         cost_estimate=pl.CostEstimate(flops=16 * cells * feats * units, bytes_accessed=20 << 20, transcendentals=0),
         name="columns_backward",
-    )(me, orientation, cot_rows, weight_in, weight_out, n_i, s_i, g_i, n_r, s_r, g_r)
+    )(me, orientation, *map(stay, (cot_rows, weight_in, weight_out, *saved_inner, *saved_rim)))
     pieces_out = pl.pallas_call(
-        functools.partial(output_gradient_kernel, n, (groups, tiles)),
+        functools.partial(output_gradient_kernel, (groups, tiles), orders[1]),
         out_shape=halves(units, feats),
-        in_specs=[SMEM, VMEM, HBM, HBM],
+        in_specs=[SMEM, VMEM, VMEM],
         out_specs=[VMEM] * 2,
-        scratch_shapes=[
-            pltpu.VMEM((3, inner + rim, units), BF16),
-            pltpu.VMEM((units, feats), F32),
-            pltpu.SemaphoreType.DMA((6,)),
-        ],
+        scratch_shapes=[pltpu.VMEM((units, feats), F32)],
         compiler_params=params(24),
         cost_estimate=pl.CostEstimate(flops=6 * cells * feats * units, bytes_accessed=8 << 20, transcendentals=0),
         name="output_gradient",
-    )(me, err_out, h_i, h_r)
+    )(me, err_out, hidden)
 
     flat = lambda part, rows: part.reshape(-1, rows, COL).transpose(1, 0, 2).reshape(-1)
-    summed_in = flat(sum_over_devices(*pieces_in, groups, tiles), feats // count)
-    summed_out = flat(sum_over_devices(*pieces_out, groups, tiles), units // count)
+    sizes = {"grp": groups, "tile": tiles}
+    summed_in = flat(sum_over_devices(*pieces_in, orders[0], sizes), feats // count)
+    summed_out = flat(sum_over_devices(*pieces_out, orders[1], sizes), units // count)
 
     block = cells // 4
     tendency = pl.pallas_call(

time: 118 us -> 109 us (0.924)
  local copies, waits for them, and re-layouts: 11.9 us -> 3.38 us
  starting transfers between devices: 29.1 us -> 32.4 us
  waiting for transfers between devices: 21 us -> 18.2 us
    unnamed x31 -> x15, local copies, waits for them, and re-layouts: 11.1 us -> 2.55 us
    ppermute x12 -> x10, starting transfers between devices: 17.6 us -> 21 us  [sum_over_devices(): lax.ppermute(send, axis, [(i, i ^ bit) for i in range(sizes[axis])])]
    ppermute x12 -> x10, waiting for transfers between devices: 21 us -> 18.2 us  [sum_over_devices(): lax.ppermute(send, axis, [(i, i ^ bit) for i in range(sizes[axis])])]
    pallas_call x1, Pallas kernels: 11.3 us -> 9.9 us  [per_device(): pl.pallas_call(functools.partial(inner_network_kernel, n), out_shape=[*st...]
  transfers between devices with their start and end apart: 17 -> 15, of which waited for: 5 -> 7; matrix products, arithmetic and copies ran while one was open for 2% -> 2% of each run, Pallas kernels for 34% -> 37%
where the time goes in v4:
time: 109 us
  Pallas kernels  53.1 us (49%)
  starting transfers between devices  32.4 us (30%)
  waiting for transfers between devices  18.2 us (17%)
  local copies, waits for them, and re-layouts  3.38 us (3%)
  between operations  1.53 us (1%)
    ppermute x10, starting transfers between devices, sum_over_devices(): lax.ppermute(send, axis, [(i, i ^ bit) for i in range(sizes[axis])])  21 us
    ppermute x10, waiting for transfers between devices, sum_over_devices(): lax.ppermute(send, axis, [(i, i ^ bit) for i in range(sizes[axis])])  18.2 us
    pallas_call x1, Pallas kernels, per_device(): pl.pallas_call(functools.partial(backward_kernel, n, (groups, tiles), ord...  16.5 us
    pallas_call x1, Pallas kernels, per_device(): pl.pallas_call(functools.partial(inner_network_kernel, n), out_shape=[*st...  9.9 us
    pallas_call x1, Pallas kernels, per_device(): pl.pallas_call(functools.partial(inner_transport_kernel, n, levels), out_...  8.53 us
    pallas_call x1, Pallas kernels, per_device(): pl.pallas_call(functools.partial(rim_kernel, n, levels), out_shape=[*stat...  8.15 us
    pallas_call x1, Pallas kernels, per_device(): pl.pallas_call(functools.partial(output_gradient_kernel, (groups, tiles),...  4.94 us
    pallas_call x1, Pallas kernels, per_device(): pl.pallas_call(output_kernel, out_shape=shape((cells, feats), F32), grid=...  3.54 us
  transfers between devices with their start and end apart: 15, of which 7 were waited for; matrix products, arithmetic and copies ran while one was open for 2% of the time, Pallas kernels for 37%

profile of v4, /device:TPU:0, one launch (start us, length us, event | category | flops | bytes accessed | tf_op | source)
XLA Modules:
  0.0 109.1 jit_solution(8966300893999907374)
XLA Ops:
  1.3 0.0 copy-start
  1.3 1.9 %copy-done = f32[32,32,768]{2,1,0:T(8,128)S(1)} copy-done((f32[32,32,768]{2,1,0:T(8,128)S(1)}, f32[32,32,768]{2,1,0:T(8,128)}, u32[]{:S(2)}) %copy-start) | copy-done | bytes 3145752
  3.2 0.0 copy-start.1
  3.2 0.8 pack_strips.1
  3.9 0.5 collective-permute-start
  4.4 0.0 copy-start.2
  4.4 0.0 copy-start.4
  4.4 0.0 copy-start.5
  4.5 0.0 copy-start.6
  4.5 2.0 %collective-permute-start.1 = (f32[64,768]{1,0:T(8,128)S(1)}, f32[64,768]{1,0:T(8,128)S(1)}, u32[]{:S(2)}, u32[]{:S(2)}) collective-permute-start(f32[64,768]{1,0:T(8,128)S(1)} %get-tuple-element.28), channel_id=1, source_target_pairs={{0,24},{8,0},{16,8},{24,16},{1,25},{9,1},{17,9},{25,17},{2,26},{10... | collective-permute-start | bytes 589832 | tf_op jit(solution)/shard_map/ppermute | solution.py:525
  6.5 0.0 copy-done.1
  6.5 8.5 %inner_transport.1 = (f32[32,32,768]{2,1,0:T(8,128)S(1)}, f32[512,768]{1,0:T(8,128)S(1)}, f32[8,128]{1,0:T(8,128)S(1)}) custom-call(s32[1,1]{1,0:T(1,128)S(6)} %copy.19.turn, f32[1024,768]{1,0:T(8,128)S(1)} %bitcast.17), custom_call_target="tpu_custom_call" | custom-call | flops 47185920 | bytes 16777216 | tf_op jit(solution)/shard_map/inner_transport/pallas_call | solution.py:527
  15.0 0.0 collective-permute-done.h1
  15.0 0.0 collective-permute-done.1.h3
  15.0 0.8 pack_strips_corners.1
  15.8 2.3 %collective-permute-start.2 = (f32[72,768]{1,0:T(8,128)S(1)}, f32[72,768]{1,0:T(8,128)S(1)}, u32[]{:S(2)}, u32[]{:S(2)}) collective-permute-start(f32[72,768]{1,0:T(8,128)S(1)} %get-tuple-element.30), channel_id=1, source_target_pairs={{0,1},{1,2},{2,3},{3,4},{4,5},{5,6},{6,7},{7,0},{8,9},{9,10},{10,1... | collective-permute-start | bytes 663560 | tf_op jit(solution)/shard_map/ppermute | solution.py:554
  18.2 3.3 %collective-permute-start.3 = (f32[72,768]{1,0:T(8,128)S(1)}, f32[72,768]{1,0:T(8,128)S(1)}, u32[]{:S(2)}, u32[]{:S(2)}) collective-permute-start(f32[72,768]{1,0:T(8,128)S(1)} %get-tuple-element.31), channel_id=1, source_target_pairs={{0,7},{1,0},{2,1},{3,2},{4,3},{5,4},{6,5},{7,6},{8,15},{9,8},{10,9... | collective-permute-start | bytes 663560 | tf_op jit(solution)/shard_map/ppermute | solution.py:555
  21.5 0.0 copy-done.2
  21.5 0.0 copy-done.4
  21.5 0.0 copy-done.5
  21.5 0.0 copy-done.6
  21.5 9.9 %inner_network.1 = (bf16[3,896,768]{2,1,0:T(8,128)(2,1)}, f32[896,128]{1,0:T(8,128)}, f32[3,896,512]{2,1,0:T(8,128)}, bf16[3,896,512]{2,1,0:T(8,128)(2,1)}, f32[...) custom-call(s32[32,32]{1,0:T(8,128)S(1)} %copy-done.5, s32[1,1]{1,0:T(1,128)S(6)} %copy.19.turn, ...), custom_call_target="tpu_custom_call" | custom-call | flops 3523215360 | bytes 16777216 | tf_op jit(solution)/shard_map/inner_network/pallas_call | solution.py:557
  31.4 0.0 collective-permute-done.2.h0
  31.4 0.0 collective-permute-done.3.h2
  31.4 8.1 %rim_columns.1 = (bf16[3,256,768]{2,1,0:T(8,128)(2,1)}, f32[256,128]{1,0:T(8,128)}, f32[3,256,512]{2,1,0:T(8,128)}, bf16[3,256,512]{2,1,0:T(8,128)(2,1)}, f32[1024,512]{1,0:T(8,128)S(1)}, /*index=5*/f32[1024,512]{1,0:T(8,128)}) custom-call(s32[1,1]{1,0:T(1,128)S(6)} %copy.19.turn, s32[32,32]{1,0:T(8,128)S(1)} %copy-done.5, ...), custom_call_target="tpu_custom_call", output_to_operand_aliasing={{4}: (10, {})} | custom-call | flops 1006632960 | bytes 20971520 | tf_op jit(solution)/shard_map/rim_columns/pallas_call | solution.py:576
  39.6 3.3 %all-to-all-start = ((f32[32,32,512]{2,1,0:T(8,128)}), f32[32,32,512]{2,1,0:T(8,128)S(1)}, u32[]{:S(2)}, u32[]{:S(2)}) async-start(f32[32,32,512]{2,1,0:T(8,128)} %bitcast.20), calls=%async_computation | async-start | bytes 4194304 | tf_op jit(solution)/shard_map/all_to_all | solution.py:595
  42.9 0.1 pad_add_fusion.me
  43.0 16.5 %columns_backward.1 = (f32[16,48,256]{2,1,0:T(8,128)S(1)}, f32[16,48,256]{2,1,0:T(8,128)S(1)}, bf16[3,1152,768]{2,1,0:T(8,128)(2,1)S(1)}, bf16[3,1152,512]{2,1,0:T(8,128)(2,1)S(1)}) custom-call(s32[2]{0:T(128)S(1)} %pad_add_fusion.me, s32[1,1]{1,0:T(1,128)S(6)} %copy.19.turn, f32[1024,768]{1,0:T(8,128)} %bitcast.26, bf16[768,512]{1,0:T(8,128)(2,1)} %in_weights.1, ...), custom_call_target="tpu_custom_call" | custom-call | flops 6442450944 | bytes 20971520 | tf_op jit(solution)/shard_map/columns_backward/pallas_call | solution.py:604
  59.4 0.1 collective-permute-start.4
  59.5 4.9 %output_gradient.1 = (f32[16,48,256]{2,1,0:T(8,128)S(1)}, f32[16,48,256]{2,1,0:T(8,128)S(1)}) custom-call(s32[2]{0:T(128)S(1)} %pad_add_fusion.me, bf16[3,1152,768]{2,1,0:T(8,128)(2,1)S(1)} %get-tuple-element.47.err_out, bf16[3,1152,512]{2,1,0:T(8,128)(2,1)S(1)} %get-tuple-element.48.h), custom_call_target="tpu_custom_call" | custom-call | flops 2415919104 | bytes 8388608 | tf_op jit(solution)/shard_map/output_gradient/pallas_call | solution.py:629
  64.5 0.5 collective-permute-start.9
  65.0 0.0 collective-permute-done.4
  65.0 0.1 add.30
  65.2 1.6 %collective-permute-start.5 = (f32[8,48,256]{2,1,0:T(8,128)S(1)}, f32[8,48,256]{2,1,0:T(8,128)S(1)}, u32[]{:S(2)}, u32[]{:S(2)}) collective-permute-start(f32[8,48,256]{2,1,0:T(8,128)S(1)} %slice.65), channel_id=1, source_target_pairs={{0,16},{8,24},{16,0},{24,8},{1,17},{9,25},{17,1},{25,9},{2,18},{10... | collective-permute-start | bytes 1179656 | tf_op jit(solution)/shard_map/ppermute | solution.py:473
  66.8 0.2 collective-permute-done.9
  66.9 0.1 add.35
  67.1 0.0 copy-start.3
  67.1 1.6 %collective-permute-start.10 = (f32[8,48,256]{2,1,0:T(8,128)S(1)}, f32[8,48,256]{2,1,0:T(8,128)S(1)}, u32[]{:S(2)}, u32[]{:S(2)}) collective-permute-start(f32[8,48,256]{2,1,0:T(8,128)S(1)} %slice.73), channel_id=1, source_target_pairs={{0,1},{1,0},{2,3},{3,2},{4,5},{5,4},{6,7},{7,6},{8,9},{9,8},{10,11... | collective-permute-start | bytes 1179656 | tf_op jit(solution)/shard_map/ppermute | solution.py:473
  68.7 10.7 %collective-permute-done.5 = f32[8,48,256]{2,1,0:T(8,128)S(1)} collective-permute-done((f32[8,48,256]{2,1,0:T(8,128)S(1)}, f32[8,48,256]{2,1,0:T(8,128)S(1)}, u32[]{:S(2)}, u32[]{:S(2)}) %collective-permute-start.5) | collective-permute-done | bytes 393248 | tf_op jit(solution)/shard_map/ppermute | solution.py:473
  79.5 0.1 slice_add_fusion.1
  79.5 2.1 %collective-permute-start.6 = (f32[4,48,256]{2,1,0:T(8,128)S(1)}, f32[4,48,256]{2,1,0:T(8,128)S(1)}, u32[]{:S(2)}, u32[]{:S(2)}) collective-permute-start(f32[4,48,256]{2,1,0:T(8,128)S(1)} %slice.67), channel_id=1, source_target_pairs={{0,1},{1,0},{2,3},{3,2},{4,5},{5,4},{6,7},{7,6},{8,9},{9,8},{10,11... | collective-permute-start | bytes 589832 | tf_op jit(solution)/shard_map/ppermute | solution.py:473
  81.6 0.0 collective-permute-done.10
  81.6 0.1 slice_add_fusion
  81.7 1.5 %collective-permute-start.11 = (f32[4,48,256]{2,1,0:T(8,128)S(1)}, f32[4,48,256]{2,1,0:T(8,128)S(1)}, u32[]{:S(2)}, u32[]{:S(2)}) collective-permute-start(f32[4,48,256]{2,1,0:T(8,128)S(1)} %slice.75), channel_id=1, source_target_pairs={{0,16},{8,24},{16,0},{24,8},{1,17},{9,25},{17,1},{25,9},{2,18},{10... | collective-permute-start | bytes 589832 | tf_op jit(solution)/shard_map/ppermute | solution.py:473
  83.2 2.8 %collective-permute-done.6 = f32[4,48,256]{2,1,0:T(8,128)S(1)} collective-permute-done((f32[4,48,256]{2,1,0:T(8,128)S(1)}, f32[4,48,256]{2,1,0:T(8,128)S(1)}, u32[]{:S(2)}, u32[]{:S(2)}) %collective-permute-start.6) | collective-permute-done | bytes 196640 | tf_op jit(solution)/shard_map/ppermute | solution.py:473
  86.0 8.2 %collective-permute-start.7 = (f32[2,48,256]{2,1,0:T(8,128)S(1)}, f32[2,48,256]{2,1,0:T(8,128)S(1)}, u32[]{:S(2)}, u32[]{:S(2)}) collective-permute-start(f32[2,48,256]{2,1,0:T(8,128)S(1)} %slice.69), channel_id=1, source_target_pairs={{0,2},{1,3},{2,0},{3,1},{4,6},{5,7},{6,4},{7,5},{8,10},{9,11},{10,... | collective-permute-start | bytes 294920 | tf_op jit(solution)/shard_map/ppermute | solution.py:473
  94.3 0.0 collective-permute-done.11
  94.3 2.5 %collective-permute-start.12 = (f32[2,48,256]{2,1,0:T(8,128)S(1)}, f32[2,48,256]{2,1,0:T(8,128)S(1)}, u32[]{:S(2)}, u32[]{:S(2)}) collective-permute-start(f32[2,48,256]{2,1,0:T(8,128)S(1)} %slice.77), channel_id=1, source_target_pairs={{0,2},{1,3},{2,0},{3,1},{4,6},{5,7},{6,4},{7,5},{8,10},{9,11},{10,... | collective-permute-start | bytes 294920 | tf_op jit(solution)/shard_map/ppermute | solution.py:473
  96.8 0.8 collective-permute-done.7
  97.6 1.5 %collective-permute-start.8 = (f32[1,48,256]{2,1,0:T(8,128)S(1)}, f32[1,48,256]{2,1,0:T(8,128)S(1)}, u32[]{:S(2)}, u32[]{:S(2)}) collective-permute-start(f32[1,48,256]{2,1,0:T(8,128)S(1)} %slice.71), channel_id=1, source_target_pairs={{0,4},{1,5},{2,6},{3,7},{4,0},{5,1},{6,2},{7,3},{8,12},{9,13},{10,... | collective-permute-start | bytes 147464 | tf_op jit(solution)/shard_map/ppermute | solution.py:473
  99.1 0.3 collective-permute-done.12
  99.4 1.3 %collective-permute-start.13 = (f32[1,48,256]{2,1,0:T(8,128)S(1)}, f32[1,48,256]{2,1,0:T(8,128)S(1)}, u32[]{:S(2)}, u32[]{:S(2)}) collective-permute-start(f32[1,48,256]{2,1,0:T(8,128)S(1)} %slice.79), channel_id=1, source_target_pairs={{0,4},{1,5},{2,6},{3,7},{4,0},{5,1},{6,2},{7,3},{8,12},{9,13},{10,... | collective-permute-start | bytes 147464 | tf_op jit(solution)/shard_map/ppermute | solution.py:473
  100.7 2.0 %collective-permute-done.8 = f32[1,48,256]{2,1,0:T(8,128)S(1)} collective-permute-done((f32[1,48,256]{2,1,0:T(8,128)S(1)}, f32[1,48,256]{2,1,0:T(8,128)S(1)}, u32[]{:S(2)}, u32[]{:S(2)}) %collective-permute-start.8) | collective-permute-done | bytes 49184 | tf_op jit(solution)/shard_map/ppermute | solution.py:473
  102.7 0.6 copy.13
  103.4 1.5 %collective-permute-done.13 = f32[1,48,256]{2,1,0:T(8,128)S(1)} collective-permute-done((f32[1,48,256]{2,1,0:T(8,128)S(1)}, f32[1,48,256]{2,1,0:T(8,128)S(1)}, u32[]{:S(2)}, u32[]{:S(2)}) %collective-permute-start.13) | collective-permute-done | bytes 49184 | tf_op jit(solution)/shard_map/ppermute | solution.py:473
  104.9 0.6 reshape.29
  105.5 0.0 all-to-all-done
  105.5 0.0 copy-done.3
  105.5 3.5 %tendency_rows.1 = f32[1024,768]{1,0:T(8,128)} custom-call(f32[1024,512]{1,0:T(8,128)S(1)} %bitcast.19, bf16[512,768]{1,0:T(8,128)(2,1)S(1)} %copy-done.3), custom_call_target="tpu_custom_call" | custom-call | flops 1610612736 | bytes 6291456 | tf_op jit(solution)/shard_map/tendency_rows/pallas_call | solution.py:646
  (16 shorter events, 0.3 us)
Async XLA Ops:
  1.3 1.9 %copy-start = (f32[32,32,768]{2,1,0:T(8,128)S(1)}, f32[32,32,768]{2,1,0:T(8,128)}, u32[]{:S(2)}) copy-start(f32[32,32,768]{2,1,0:T(8,128)} %param.7) | copy-start | bytes 9437188
  3.2 3.3 %copy-start.1 = (f32[32,32,768]{2,1,0:T(8,128)S(1)}, f32[32,32,768]{2,1,0:T(8,128)}, u32[]{:S(2)}) copy-start(f32[32,32,768]{2,1,0:T(8,128)} %param.7) | copy-start | bytes 9437188
  3.9 11.1 %collective-permute-start = (f32[64,768]{1,0:T(8,128)S(1)}, f32[64,768]{1,0:T(8,128)S(1)}, u32[]{:S(2)}, u32[]{:S(2)}) collective-permute-start(f32[64,768]{1,0:T(8,128)S(1)} %get-tuple-element.27), channel_id=1, source_target_pairs={{0,8},{8,16},{16,24},{24,0},{1,9},{9,17},{17,25},{25,1},{2,10},{10... | collective-permute-start | bytes 589832 | tf_op jit(solution)/shard_map/ppermute | solution.py:524
  4.4 17.0 %copy-start.2 = (bf16[512,768]{1,0:T(8,128)(2,1)S(1)}, bf16[512,768]{1,0:T(8,128)(2,1)}, u32[]{:S(2)}) copy-start(bf16[512,768]{1,0:T(8,128)(2,1)} %out_weights.1) | copy-start | bytes 2359300
  4.4 17.0 %copy-start.4 = (bf16[768,512]{1,0:T(8,128)(2,1)S(1)}, bf16[768,512]{1,0:T(8,128)(2,1)}, u32[]{:S(2)}) copy-start(bf16[768,512]{1,0:T(8,128)(2,1)} %in_weights.1) | copy-start | bytes 2359300
  4.4 17.0 %copy-start.5 = (s32[32,32]{1,0:T(8,128)S(1)}, s32[32,32]{1,0:T(8,128)}, u32[]{:S(2)}) copy-start(s32[32,32]{1,0:T(8,128)} %dest.3) | copy-start | bytes 12292
  4.5 17.0 %copy-start.6 = (s32[32,32]{1,0:T(8,128)S(1)}, s32[32,32]{1,0:T(8,128)}, u32[]{:S(2)}) copy-start(s32[32,32]{1,0:T(8,128)} %cost.1) | copy-start | bytes 12292
  4.5 10.6 %collective-permute-start.1 = (f32[64,768]{1,0:T(8,128)S(1)}, f32[64,768]{1,0:T(8,128)S(1)}, u32[]{:S(2)}, u32[]{:S(2)}) collective-permute-start(f32[64,768]{1,0:T(8,128)S(1)} %get-tuple-element.28), channel_id=1, source_target_pairs={{0,24},{8,0},{16,8},{24,16},{1,25},{9,1},{17,9},{25,17},{2,26},{10... | collective-permute-start | bytes 589832 | tf_op jit(solution)/shard_map/ppermute | solution.py:525
  15.8 15.5 %collective-permute-start.2 = (f32[72,768]{1,0:T(8,128)S(1)}, f32[72,768]{1,0:T(8,128)S(1)}, u32[]{:S(2)}, u32[]{:S(2)}) collective-permute-start(f32[72,768]{1,0:T(8,128)S(1)} %get-tuple-element.30), channel_id=1, source_target_pairs={{0,1},{1,2},{2,3},{3,4},{4,5},{5,6},{6,7},{7,0},{8,9},{9,10},{10,1... | collective-permute-start | bytes 663560 | tf_op jit(solution)/shard_map/ppermute | solution.py:554
  18.2 13.2 %collective-permute-start.3 = (f32[72,768]{1,0:T(8,128)S(1)}, f32[72,768]{1,0:T(8,128)S(1)}, u32[]{:S(2)}, u32[]{:S(2)}) collective-permute-start(f32[72,768]{1,0:T(8,128)S(1)} %get-tuple-element.31), channel_id=1, source_target_pairs={{0,7},{1,0},{2,1},{3,2},{4,3},{5,4},{6,5},{7,6},{8,15},{9,8},{10,9... | collective-permute-start | bytes 663560 | tf_op jit(solution)/shard_map/ppermute | solution.py:555
  39.6 66.0 %all-to-all-start = ((f32[32,32,512]{2,1,0:T(8,128)}), f32[32,32,512]{2,1,0:T(8,128)S(1)}, u32[]{:S(2)}, u32[]{:S(2)}) async-start(f32[32,32,512]{2,1,0:T(8,128)} %bitcast.20), calls=%async_computation | async-start | bytes 4194304 | tf_op jit(solution)/shard_map/all_to_all | solution.py:595
  59.4 5.6 %collective-permute-start.4 = (f32[16,48,256]{2,1,0:T(8,128)S(1)}, f32[16,48,256]{2,1,0:T(8,128)S(1)}, u32[]{:S(2)}, u32[]{:S(2)}) collective-permute-start(f32[16,48,256]{2,1,0:T(8,128)S(1)} %get-tuple-element.46), channel_id=1, source_target_pairs={{0,8},{8,0},{16,24},{24,16},{1,9},{9,1},{17,25},{25,17},{2,10},{10... | collective-permute-start | bytes 2359304 | tf_op jit(solution)/shard_map/ppermute | solution.py:473
  64.5 2.4 %collective-permute-start.9 = (f32[16,48,256]{2,1,0:T(8,128)S(1)}, f32[16,48,256]{2,1,0:T(8,128)S(1)}, u32[]{:S(2)}, u32[]{:S(2)}) collective-permute-start(f32[16,48,256]{2,1,0:T(8,128)S(1)} %get-tuple-element.50), channel_id=1, source_target_pairs={{0,8},{8,0},{16,24},{24,16},{1,9},{9,1},{17,25},{25,17},{2,10},{10... | collective-permute-start | bytes 2359304 | tf_op jit(solution)/shard_map/ppermute | solution.py:473
  65.2 14.3 %collective-permute-start.5 = (f32[8,48,256]{2,1,0:T(8,128)S(1)}, f32[8,48,256]{2,1,0:T(8,128)S(1)}, u32[]{:S(2)}, u32[]{:S(2)}) collective-permute-start(f32[8,48,256]{2,1,0:T(8,128)S(1)} %slice.65), channel_id=1, source_target_pairs={{0,16},{8,24},{16,0},{24,8},{1,17},{9,25},{17,1},{25,9},{2,18},{10... | collective-permute-start | bytes 1179656 | tf_op jit(solution)/shard_map/ppermute | solution.py:473
  67.1 38.5 %copy-start.3 = (bf16[512,768]{1,0:T(8,128)(2,1)S(1)}, bf16[512,768]{1,0:T(8,128)(2,1)}, u32[]{:S(2)}) copy-start(bf16[512,768]{1,0:T(8,128)(2,1)} %out_weights.1) | copy-start | bytes 2359300
  67.1 14.5 %collective-permute-start.10 = (f32[8,48,256]{2,1,0:T(8,128)S(1)}, f32[8,48,256]{2,1,0:T(8,128)S(1)}, u32[]{:S(2)}, u32[]{:S(2)}) collective-permute-start(f32[8,48,256]{2,1,0:T(8,128)S(1)} %slice.73), channel_id=1, source_target_pairs={{0,1},{1,0},{2,3},{3,2},{4,5},{5,4},{6,7},{7,6},{8,9},{9,8},{10,11... | collective-permute-start | bytes 1179656 | tf_op jit(solution)/shard_map/ppermute | solution.py:473
  79.5 6.5 %collective-permute-start.6 = (f32[4,48,256]{2,1,0:T(8,128)S(1)}, f32[4,48,256]{2,1,0:T(8,128)S(1)}, u32[]{:S(2)}, u32[]{:S(2)}) collective-permute-start(f32[4,48,256]{2,1,0:T(8,128)S(1)} %slice.67), channel_id=1, source_target_pairs={{0,1},{1,0},{2,3},{3,2},{4,5},{5,4},{6,7},{7,6},{8,9},{9,8},{10,11... | collective-permute-start | bytes 589832 | tf_op jit(solution)/shard_map/ppermute | solution.py:473
  81.7 12.6 %collective-permute-start.11 = (f32[4,48,256]{2,1,0:T(8,128)S(1)}, f32[4,48,256]{2,1,0:T(8,128)S(1)}, u32[]{:S(2)}, u32[]{:S(2)}) collective-permute-start(f32[4,48,256]{2,1,0:T(8,128)S(1)} %slice.75), channel_id=1, source_target_pairs={{0,16},{8,24},{16,0},{24,8},{1,17},{9,25},{17,1},{25,9},{2,18},{10... | collective-permute-start | bytes 589832 | tf_op jit(solution)/shard_map/ppermute | solution.py:473
  86.0 11.5 %collective-permute-start.7 = (f32[2,48,256]{2,1,0:T(8,128)S(1)}, f32[2,48,256]{2,1,0:T(8,128)S(1)}, u32[]{:S(2)}, u32[]{:S(2)}) collective-permute-start(f32[2,48,256]{2,1,0:T(8,128)S(1)} %slice.69), channel_id=1, source_target_pairs={{0,2},{1,3},{2,0},{3,1},{4,6},{5,7},{6,4},{7,5},{8,10},{9,11},{10,... | collective-permute-start | bytes 294920 | tf_op jit(solution)/shard_map/ppermute | solution.py:473
  94.3 5.1 %collective-permute-start.12 = (f32[2,48,256]{2,1,0:T(8,128)S(1)}, f32[2,48,256]{2,1,0:T(8,128)S(1)}, u32[]{:S(2)}, u32[]{:S(2)}) collective-permute-start(f32[2,48,256]{2,1,0:T(8,128)S(1)} %slice.77), channel_id=1, source_target_pairs={{0,2},{1,3},{2,0},{3,1},{4,6},{5,7},{6,4},{7,5},{8,10},{9,11},{10,... | collective-permute-start | bytes 294920 | tf_op jit(solution)/shard_map/ppermute | solution.py:473
  97.6 5.1 %collective-permute-start.8 = (f32[1,48,256]{2,1,0:T(8,128)S(1)}, f32[1,48,256]{2,1,0:T(8,128)S(1)}, u32[]{:S(2)}, u32[]{:S(2)}) collective-permute-start(f32[1,48,256]{2,1,0:T(8,128)S(1)} %slice.71), channel_id=1, source_target_pairs={{0,4},{1,5},{2,6},{3,7},{4,0},{5,1},{6,2},{7,3},{8,12},{9,13},{10,... | collective-permute-start | bytes 147464 | tf_op jit(solution)/shard_map/ppermute | solution.py:473
  99.4 5.4 %collective-permute-start.13 = (f32[1,48,256]{2,1,0:T(8,128)S(1)}, f32[1,48,256]{2,1,0:T(8,128)S(1)}, u32[]{:S(2)}, u32[]{:S(2)}) collective-permute-start(f32[1,48,256]{2,1,0:T(8,128)S(1)} %slice.79), channel_id=1, source_target_pairs={{0,4},{1,5},{2,6},{3,7},{4,0},{5,1},{6,2},{7,3},{8,12},{9,13},{10,... | collective-permute-start | bytes 147464 | tf_op jit(solution)/shard_map/ppermute | solution.py:473

commit v5 on v4

--- a/solution.py
+++ b/solution.py
@@ -25,15 +25,16 @@
     return pltpu.CompilerParams(vmem_limit_bytes=mib * 1024 * 1024)
 
 
-def side_cells(k, n):
+def side_cells(k, ni, nj):
     pick = lambda a, b, c, e: jnp.where(k == 0, a, jnp.where(k == 1, b, jnp.where(k == 2, c, e)))
-    return (pick(0, n - 1, n - 1, 0), pick(1, 0, -1, 0), pick(0, -1, 0, 1)), (
-        pick(0, 0, n - 1, n - 1), pick(0, 1, 0, -1), pick(1, 0, -1, 0))
-
-
-def side_rows(k, n):
-    (bi, di, mi), (bj, dj, mj) = side_cells(k, n)
-    return bi * n + bj, mi * n + mj, di * n + dj
+    return (pick(0, ni - 1, ni - 1, 0), pick(1, 0, -1, 0), pick(0, -1, 0, 1)), (
+        pick(0, 0, nj - 1, nj - 1), pick(0, 1, 0, -1), pick(1, 0, -1, 0))
+
+
+def side_rows(k, ni, nj=None):
+    nj = ni if nj is None else nj
+    (bi, di, mi), (bj, dj, mj) = side_cells(k, ni, nj)
+    return bi * nj + bj, mi * nj + mj, di * nj + dj
 
 
 def turn_winds(ref, rows, quarter, levels):
@@ -120,7 +121,10 @@
                     q[i], before[i] = ahead, flux
         return carry
 
-    lax.fori_loop(0, (hi - lo) // block, body, 0)
+    if hi - lo == block:
+        body(0, 0)
+    else:
+        lax.fori_loop(0, (hi - lo) // block, body, 0)
 
 
 def network_forward(x, mask, w_in, w_out, state, hsum, rows, kept):
@@ -175,22 +179,43 @@
     return copies
 
 
-def pack_strip(n, levels, k, o, air, out):
-    base, cm, cd = side_rows((k - o + 4) % 4, n)
+def pack_strip(n, levels, k, o, air, out, ni, nj):
+    base, cm, cd = side_rows((k - o + 4) % 4, ni, nj)
     for d in range(2):
         copy_rows(out, d * n, air, base + cd * d + cm * (n - 1), -cm, n)
     turn_winds(out, (0, 2 * n), o, levels)
 
 
-def pack_kernel(n, levels, turn, air, s1, s3):
-    pack_strip(n, levels, 1, turn[0, 0], air, s1)
-    pack_strip(n, levels, 3, turn[0, 0], air, s3)
+def pack_kernel(n, levels, turn, air, s1, s3, rows, columns, sems):
+    o = turn[0, 0]
+    feats = air.shape[2]
+    width = columns.shape[1] // 2
+
+    def pack(buffer, copies):
+        for copy in copies:
+            copy.start()
+        for copy in copies:
+            copy.wait()
+        ni, nj = buffer.shape[:2]
+        for k, out in ((1, s1), (3, s3)):
+            pack_strip(n, levels, k, o, buffer.reshape(ni * nj, feats), out, ni, nj)
+
+    @pl.when(o % 2 == 1)
+    def _():
+        pack(rows, [pltpu.make_async_copy(air.at[pl.ds(n - 2 if e else 0, 2)], rows.at[pl.ds(2 * e, 2)], sems.at[e])
+                    for e in range(2)])
+
+    @pl.when(o % 2 == 0)
+    def _():
+        pack(columns, [pltpu.make_async_copy(air.at[:, pl.ds(n - width if e else 0, width), :],
+                                             columns.at[:, pl.ds(width * e, width), :], sems.at[e])
+                       for e in range(2)])
 
 
 def pack_with_corners_kernel(n, levels, turn, air, h1, h3, order, s0, s2):
     del order
-    pack_strip(n, levels, 0, turn[0, 0], air, s0)
-    pack_strip(n, levels, 2, turn[0, 0], air, s2)
+    pack_strip(n, levels, 0, turn[0, 0], air, s0, n, n)
+    pack_strip(n, levels, 2, turn[0, 0], air, s2, n, n)
     s0[2 * n : 2 * n + 1, :] = h1[n - 1 : n, :]
     s0[2 * n + 1 : 2 * n + 2, :] = h3[0:1, :]
     s2[2 * n : 2 * n + 1, :] = h1[0:1, :]
@@ -270,20 +295,23 @@
 def rim_kernel(n, levels, turn, dest, h0, h1, h2, h3, own, mask_rim, w_in, w_out, before,
                n_o, s_o, g_o, h_o, outgoing, sent,
                normed, scale, slope, hidden, sems,
-               wide, wide_one, wide_two, slim, slim_one, slim_two, lead_wide, sub_wide, lead_slim, sub_slim, x_rim, hsum):
+               cells_wide, cells_slim, lead_wide, sub_wide, lead_slim, sub_slim, x_rim, hsum):
     del before
     state, out = (normed, scale, slope, hidden), (n_o, s_o, g_o, h_o)
     o = turn[0, 0]
     halo = (h0, h1, h2, h3)
-    for k in range(4):
-        ends = k % 2 == 0
-        src, one, two = (wide, wide_one, wide_two) if ends else (slim, slim_one, slim_two)
-        lead, sub = (lead_wide, sub_wide) if ends else (lead_slim, sub_slim)
+    sides = [
+        [ref.at[k // 2] for ref in (lead_slim, sub_slim)] + [cells_slim.at[k // 2, step] for step in range(3)]
+        if k % 2
+        else [ref.at[k // 2] for ref in (lead_wide, sub_wide)] + [cells_wide.at[k // 2, step] for step in range(3)]
+        for k in range(4)
+    ]
+    for k, (_, _, src, _, _) in enumerate(sides):
         for depth in range(6):
             d = depth - 2
             row = halo[k][(1 - depth) * n : (2 - depth) * n, :] if d < 0 else own[(k * 4 + d) * n : (k * 4 + d + 1) * n, :]
             src[depth, 0:n, :] = row
-            if ends:
+            if k % 2 == 0:
                 src[depth, n + 2 : n + 8, :] = row[0:6, :]
                 src[depth, n + 8 : n + 14, :] = row[n - 6 : n, :]
                 for e in range(2):
@@ -297,12 +325,15 @@
                         src[depth, n + 1 - e : n + 2 - e, :] = halo[(k + 1) % 4][at : at + 1, :]
                         at = e * n + d
                         src[depth, n + 14 + e : n + 15 + e, :] = halo[(k + 3) % 4][at : at + 1, :]
+    for k, (lead, sub, src, one, _) in enumerate(sides):
         transport(src, one, lead, sub, 1, 5, SIDE_WINDS[k], levels)
+    for k, (lead, sub, _, one, two) in enumerate(sides):
         transport(one, two, lead, sub, 2, 4, SIDE_WINDS[k], levels)
+    for k, (_, _, _, _, two) in enumerate(sides):
         for d in range(2):
             at = (k * 2 + d) * n
             x_rim[at : at + n, :] = two[2 + d, 0:n, :]
-            if ends:
+            if k % 2 == 0:
                 x_rim[at : at + 2, :] = two[2 + d, n + 2 : n + 4, :]
                 x_rim[at + n - 2 : at + n, :] = two[2 + d, n + 12 : n + 14, :]
     turn_winds(x_rim, (0, 8 * n), (4 - o) % 4, levels)
@@ -313,12 +344,13 @@
             copy.start()
             copies.append(copy)
 
-    rows = slice(0, 8 * n)
-    run_together(
-        [network_forward(lambda: x_rim[...], lambda: mask_rim[...], w_in, w_out, state, hsum, rows, kept)], 0
-    )
+    halves = ((slice(0, 4 * n), lambda use: None), (slice(4 * n, 8 * n), kept))
+    run_together([
+        network_forward(lambda r=r: x_rim[r, :], lambda r=r: mask_rim[r, :], w_in, w_out, state, hsum, r, done)
+        for r, done in halves
+    ], 0)
     for k in range(4):
-        (bi, di, mi), (bj, dj, mj) = side_cells((k - o + 4) % 4, n)
+        (bi, di, mi), (bj, dj, mj) = side_cells((k - o + 4) % 4, n, n)
         skip = 2 * (k % 2)
         for d in range(2):
             for m in range(skip, n - skip):
@@ -430,6 +462,7 @@
 
     start_next()
     start_next()
+    start_next()
     steps = []
     for part, start, size in parts:
         at = slice(edge + start, edge + start + size)
@@ -464,14 +497,13 @@
     store_pieces(grid_shape, me, order, grad_out, keep, send)
 
 
-def sum_over_devices(keep, send, order, sizes):
-    total = None
+def exchange_sums(keep, send, order, sizes):
     for axis, bit in order:
-        if total is not None:
-            half = total.shape[0] // 2
-            keep, send = total[:half], total[half:]
-        total = keep + lax.ppermute(send, axis, [(i, i ^ bit) for i in range(sizes[axis])])
-    return total[0]
+        keep = keep + lax.ppermute(send, axis, [(i, i ^ bit) for i in range(sizes[axis])])
+        if keep.shape[0] > 1:
+            half = keep.shape[0] // 2
+            keep, send = keep[:half], keep[half:]
+    return keep, send
 
 
 def output_kernel(rows, w_out, out):
@@ -503,6 +535,7 @@
     air_rows = air_state.reshape(cells, feats)
     cot_rows = cotangent.reshape(cells, feats)
     both = ("grp", "tile")
+    stay = lambda x: pltpu.with_memory_space_constraint(x, pltpu.HBM)
 
     def state(space, rows):
         return [
@@ -516,11 +549,16 @@
     strips = pl.pallas_call(
         functools.partial(pack_kernel, n, levels),
         out_shape=[shape((2 * n, feats), F32)] * 2,
-        in_specs=[SMEM, VMEM],
+        in_specs=[SMEM, HBM],
         out_specs=[VMEM] * 2,
+        scratch_shapes=[
+            pltpu.VMEM((4, n, feats), F32),
+            pltpu.VMEM((n, 16, feats), F32),
+            pltpu.SemaphoreType.DMA((2,)),
+        ],
         compiler_params=params(8),
         name="pack_strips",
-    )(orientation, air_rows)
+    )(orientation, stay(air_state))
     from_left = lax.ppermute(strips[1], "grp", shift_perm(groups, 1))
     from_right = lax.ppermute(strips[0], "grp", shift_perm(groups, -1))
 
@@ -580,12 +618,11 @@
         out_specs=[HBM] * 4 + [VMEM, HBM],
         input_output_aliases={10: 4},
         scratch_shapes=[*state(pltpu.VMEM, rim), pltpu.SemaphoreType.DMA((2, 3, 4))]
-        + [pltpu.VMEM((6, wide, feats), F32)] * 3
-        + [pltpu.VMEM((6, slim, feats), F32)] * 3
-        + [pltpu.VMEM((5, wide, period * LANES), F32), pltpu.VMEM((4, wide, period * LANES), F32)]
-        + [pltpu.VMEM((5, slim, period * LANES), F32), pltpu.VMEM((4, slim, period * LANES), F32)]
+        + [pltpu.VMEM((2, 3, 6, wide, feats), F32), pltpu.VMEM((2, 3, 6, slim, feats), F32)]
+        + [pltpu.VMEM((2, rows, wide, period * LANES), F32) for rows in (5, 4)]
+        + [pltpu.VMEM((2, rows, slim, period * LANES), F32) for rows in (5, 4)]
         + [pltpu.VMEM((rim, feats), F32), pltpu.VMEM((rim, units), F32)],
-        compiler_params=params(16),
+        compiler_params=params(26),
         cost_estimate=pl.CostEstimate(
             flops=10 * rim * feats * units, bytes_accessed=20 << 20, transcendentals=3 * rim * units
         ),
@@ -597,7 +634,6 @@
     ).reshape(cells, units)
 
     me = jnp.stack([lax.axis_index("grp"), lax.axis_index("tile")]).astype(jnp.int32)
-    stay = lambda x: pltpu.with_memory_space_constraint(x, pltpu.HBM)
     saved = lambda rows: state(pltpu.VMEM, rows)[:3]
     halves = lambda rows, columns: [shape((count // 2, rows // count * (columns // COL), COL), F32)] * 2
     orders = [exchange_order(groups, tiles, tile_first) for tile_first in (False, True)]
@@ -639,8 +675,12 @@
 
     flat = lambda part, rows: part.reshape(-1, rows, COL).transpose(1, 0, 2).reshape(-1)
     sizes = {"grp": groups, "tile": tiles}
-    summed_in = flat(sum_over_devices(*pieces_in, orders[0], sizes), feats // count)
-    summed_out = flat(sum_over_devices(*pieces_out, orders[1], sizes), units // count)
+    far = [pair for pair in orders[0] if pair[0] == "tile" and pair[1] > 1]
+    near = len(orders[0]) - len(far)
+    sums = [exchange_sums(*pieces, order[:near], sizes) for pieces, order in zip((pieces_in, pieces_out), orders)]
+    split = sums[0][0].shape[1]
+    keep, _ = exchange_sums(*(jnp.concatenate(pair, axis=1) for pair in zip(*sums)), far, sizes)
+    summed_in, summed_out = flat(keep[0, :split], feats // count), flat(keep[0, split:], units // count)
 
     block = cells // 4
     tendency = pl.pallas_call(

time: 109 us -> 116 us (1.064)
  waiting for transfers between devices: 18.2 us -> 25.6 us
  starting transfers between devices: 32.4 us -> 27.4 us
  local copies, waits for them, and re-layouts: 3.38 us -> 5.61 us
  Pallas kernels: 53.1 us -> 54.3 us
    ppermute x10 -> x8, waiting for transfers between devices: 18.2 us -> 25.6 us  [exchange_sums(): lax.ppermute(send, axis, [(i, i ^ bit) for i in range(sizes[axis])])]
    ppermute x10 -> x8, starting transfers between devices: 21 us -> 16.1 us  [exchange_sums(): lax.ppermute(send, axis, [(i, i ^ bit) for i in range(sizes[axis])])]
    unnamed x15 -> x23, local copies, waits for them, and re-layouts: 2.55 us -> 4.77 us
    pallas_call x1, Pallas kernels: 0.76 us -> 2.29 us  [per_device(): pl.pallas_call(functools.partial(pack_kernel, n, levels), out_shape=[shap...]
  transfers between devices with their start and end apart: 15 -> 13, of which waited for: 7 -> 6; matrix products, arithmetic and copies ran while one was open for 2% -> 2% of each run, Pallas kernels for 37% -> 34%
where the time goes in v5:
time: 116 us; the launch traced here: 115 us
  Pallas kernels  54.3 us (47%)
  starting transfers between devices  27.4 us (24%)
  waiting for transfers between devices  25.6 us (22%)
  local copies, waits for them, and re-layouts  5.61 us (5%)
  between operations  1.68 us (1%)
    ppermute x8, waiting for transfers between devices, exchange_sums(): lax.ppermute(send, axis, [(i, i ^ bit) for i in range(sizes[axis])])  25.6 us
    ppermute x8, starting transfers between devices, exchange_sums(): lax.ppermute(send, axis, [(i, i ^ bit) for i in range(sizes[axis])])  16.1 us
    pallas_call x1, Pallas kernels, per_device(): pl.pallas_call(functools.partial(backward_kernel, n, (groups, tiles), ord...  15.8 us
    pallas_call x1, Pallas kernels, per_device(): pl.pallas_call(functools.partial(inner_network_kernel, n), out_shape=[*st...  9.9 us
    pallas_call x1, Pallas kernels, per_device(): pl.pallas_call(functools.partial(inner_transport_kernel, n, levels), out_...  8.58 us
    pallas_call x1, Pallas kernels, per_device(): pl.pallas_call(functools.partial(rim_kernel, n, levels), out_shape=[*stat...  7.81 us
    pallas_call x1, Pallas kernels, per_device(): pl.pallas_call(functools.partial(output_gradient_kernel, (groups, tiles),...  4.95 us
    unnamed x23, local copies, waits for them, and re-layouts  4.77 us
  transfers between devices with their start and end apart: 13, of which 6 were waited for; matrix products, arithmetic and copies ran while one was open for 2% of the time, Pallas kernels for 34%

profile of v5, /device:TPU:0, one launch (start us, length us, event | category | flops | bytes accessed | tf_op | source)
XLA Modules:
  0.0 115.2 jit_solution(8435485984707759446)
XLA Ops:
  0.6 0.0 copy-start
  1.4 2.3 %pack_strips.1 = (f32[64,768]{1,0:T(8,128)S(1)}, f32[64,768]{1,0:T(8,128)S(1)}) custom-call(s32[1,1]{1,0:T(1,128)S(6)} %copy.19.turn, f32[32,32,768]{2,1,0:T(8,128)} %air.1), custom_call_target="tpu_custom_call" | custom-call | tf_op jit(solution)/shard_map/pack_strips/pallas_call | solution.py:549
  3.7 0.2 collective-permute-start
  3.9 2.0 %collective-permute-start.1 = (f32[64,768]{1,0:T(8,128)S(1)}, f32[64,768]{1,0:T(8,128)S(1)}, u32[]{:S(2)}, u32[]{:S(2)}) collective-permute-start(f32[64,768]{1,0:T(8,128)S(1)} %get-tuple-element.28), channel_id=1, source_target_pairs={{0,24},{8,0},{16,8},{24,16},{1,25},{9,1},{17,9},{25,17},{2,26},{10... | collective-permute-start | bytes 589832 | tf_op jit(solution)/shard_map/ppermute | solution.py:563
  5.9 0.0 copy-done
  5.9 0.0 copy-start.1
  5.9 0.0 copy-start.5
  5.9 0.0 copy-start.9
  5.9 0.0 copy-start.10
  5.9 8.6 %inner_transport.1 = (f32[32,32,768]{2,1,0:T(8,128)S(1)}, f32[512,768]{1,0:T(8,128)S(1)}, f32[8,128]{1,0:T(8,128)S(1)}) custom-call(s32[1,1]{1,0:T(1,128)S(6)} %copy.19.turn, f32[1024,768]{1,0:T(8,128)S(1)} %bitcast.16), custom_call_target="tpu_custom_call" | custom-call | flops 47185920 | bytes 16777216 | tf_op jit(solution)/shard_map/inner_transport/pallas_call | solution.py:565
  14.5 0.0 copy-start.3
  14.5 0.0 collective-permute-done.h1
  14.5 0.0 collective-permute-done.1.h3
  14.5 1.5 %pack_strips_corners.1 = (f32[72,768]{1,0:T(8,128)}, f32[72,768]{1,0:T(8,128)}) custom-call(s32[1,1]{1,0:T(1,128)S(6)} %copy.19.turn, f32[1024,768]{1,0:T(8,128)S(1)} %bitcast.17, f32[64,768]{1,0:T(8,128)S(1)} %collective-permute-done.h1, f32[64,768]{1,0:T(8,128)S(1)} %collective-permute-done.1.h3, f32[8,128]{1,0:T(8,128)S(1)} %get-tuple-element.29.order), custom_call_target="tpu_custom_call" | custom-call | tf_op jit(solution)/shard_map/pack_strips_corners/pallas_call | solution.py:584
  16.0 2.6 %collective-permute-start.2 = (f32[72,768]{1,0:T(8,128)}, f32[72,768]{1,0:T(8,128)S(1)}, u32[]{:S(2)}, u32[]{:S(2)}) collective-permute-start(f32[72,768]{1,0:T(8,128)} %get-tuple-element.30), channel_id=1, source_target_pairs={{0,1},{1,2},{2,3},{3,4},{4,5},{5,6},{6,7},{7,0},{8,9},{9,10},{10,1... | collective-permute-start | bytes 663560 | tf_op jit(solution)/shard_map/ppermute | solution.py:592
  18.6 2.7 %collective-permute-start.3 = (f32[72,768]{1,0:T(8,128)}, f32[72,768]{1,0:T(8,128)}, u32[]{:S(2)}, u32[]{:S(2)}) collective-permute-start(f32[72,768]{1,0:T(8,128)} %get-tuple-element.31), channel_id=1, source_target_pairs={{0,7},{1,0},{2,1},{3,2},{4,3},{5,4},{6,5},{7,6},{8,15},{9,8},{10,9... | collective-permute-start | bytes 663560 | tf_op jit(solution)/shard_map/ppermute | solution.py:593
  21.3 0.0 copy-done.3
  21.3 0.0 copy-done.1
  21.3 0.0 copy-done.5
  21.3 0.0 copy-done.9
  21.3 0.0 copy-done.10
  21.3 9.9 %inner_network.1 = (bf16[3,896,768]{2,1,0:T(8,128)(2,1)}, f32[896,128]{1,0:T(8,128)}, f32[3,896,512]{2,1,0:T(8,128)}, bf16[3,896,512]{2,1,0:T(8,128)(2,1)}, f32[...) custom-call(s32[32,32]{1,0:T(8,128)S(1)} %copy-done.9, s32[1,1]{1,0:T(1,128)S(6)} %copy.19.turn, ...), custom_call_target="tpu_custom_call" | custom-call | flops 3523215360 | bytes 16777216 | tf_op jit(solution)/shard_map/inner_network/pallas_call | solution.py:595
  31.3 0.0 copy-start.7
  31.3 0.6 copy-done.7
  31.9 0.1 pad_add_fusion.me
  32.0 0.0 collective-permute-done.2.h0
  32.0 0.0 collective-permute-done.3.h2
  32.0 0.0 copy-start.4
  32.0 1.4 %copy-done.4 = f32[512,768]{1,0:T(8,128)S(1)} copy-done((f32[512,768]{1,0:T(8,128)S(1)}, f32[512,768]{1,0:T(8,128)}, u32[]{:S(2)}) %copy-start.4) | copy-done | bytes 1572888
  33.4 0.0 copy-start.6
  33.4 1.1 copy-done.6
  34.5 0.0 copy-start.8
  34.5 0.9 copy-done.8
  35.4 7.8 %rim_columns.1 = (bf16[3,256,768]{2,1,0:T(8,128)(2,1)}, f32[256,128]{1,0:T(8,128)}, f32[3,256,512]{2,1,0:T(8,128)}, bf16[3,256,512]{2,1,0:T(8,128)(2,1)}, f32[1024,512]{1,0:T(8,128)S(1)}, /*index=5*/f32[1024,512]{1,0:T(8,128)}) custom-call(s32[1,1]{1,0:T(1,128)S(6)} %copy.19.turn, s32[32,32]{1,0:T(8,128)S(1)} %copy-done.9, ...), custom_call_target="tpu_custom_call", output_to_operand_aliasing={{4}: (10, {})} | custom-call | flops 1006632960 | bytes 20971520 | tf_op jit(solution)/shard_map/rim_columns/pallas_call | solution.py:614
  43.3 3.9 %all-to-all-start = ((f32[32,32,512]{2,1,0:T(8,128)}), f32[32,32,512]{2,1,0:T(8,128)S(1)}, u32[]{:S(2)}, u32[]{:S(2)}) async-start(f32[32,32,512]{2,1,0:T(8,128)} %bitcast.19), calls=%async_computation | async-start | bytes 4194304 | tf_op jit(solution)/shard_map/all_to_all | solution.py:632
  47.2 15.8 %columns_backward.1 = (f32[16,48,256]{2,1,0:T(8,128)S(1)}, f32[16,48,256]{2,1,0:T(8,128)S(1)}, bf16[3,1152,768]{2,1,0:T(8,128)(2,1)S(1)}, bf16[3,1152,512]{2,1,0:T(8,128)(2,1)S(1)}) custom-call(s32[2]{0:T(128)S(1)} %pad_add_fusion.me, s32[1,1]{1,0:T(1,128)S(6)} %copy.19.turn, f32[1024,768]{1,0:T(8,128)} %bitcast.25, bf16[768,512]{1,0:T(8,128)(2,1)} %in_weights.1, ...), custom_call_target="tpu_custom_call" | custom-call | flops 6442450944 | bytes 20971520 | tf_op jit(solution)/shard_map/columns_backward/pallas_call | solution.py:640
  63.0 0.1 collective-permute-start.4
  63.1 4.9 %output_gradient.1 = (f32[16,48,256]{2,1,0:T(8,128)S(1)}, f32[16,48,256]{2,1,0:T(8,128)S(1)}) custom-call(s32[2]{0:T(128)S(1)} %pad_add_fusion.me, bf16[3,1152,768]{2,1,0:T(8,128)(2,1)S(1)} %get-tuple-element.47.err_out, bf16[3,1152,512]{2,1,0:T(8,128)(2,1)S(1)} %get-tuple-element.48.h), custom_call_target="tpu_custom_call" | custom-call | flops 2415919104 | bytes 8388608 | tf_op jit(solution)/shard_map/output_gradient/pallas_call | solution.py:665
  68.0 0.5 collective-permute-start.7
  68.5 0.0 collective-permute-done.4
  68.6 0.1 add.24
  68.7 1.6 %collective-permute-start.5 = (f32[8,48,256]{2,1,0:T(8,128)S(1)}, f32[8,48,256]{2,1,0:T(8,128)S(1)}, u32[]{:S(2)}, u32[]{:S(2)}) collective-permute-start(f32[8,48,256]{2,1,0:T(8,128)S(1)} %slice.65), channel_id=1, source_target_pairs={{0,16},{8,24},{16,0},{24,8},{1,17},{9,25},{17,1},{25,9},{2,18},{10... | collective-permute-start | bytes 1179656 | tf_op jit(solution)/shard_map/ppermute | solution.py:502
  70.3 0.1 collective-permute-done.7
  70.5 0.1 add.27
  70.6 1.6 %collective-permute-start.8 = (f32[8,48,256]{2,1,0:T(8,128)S(1)}, f32[8,48,256]{2,1,0:T(8,128)S(1)}, u32[]{:S(2)}, u32[]{:S(2)}) collective-permute-start(f32[8,48,256]{2,1,0:T(8,128)S(1)} %slice.70), channel_id=1, source_target_pairs={{0,1},{1,0},{2,3},{3,2},{4,5},{5,4},{6,7},{7,6},{8,9},{9,8},{10,11... | collective-permute-start | bytes 1179656 | tf_op jit(solution)/shard_map/ppermute | solution.py:502
  72.2 11.2 %collective-permute-done.5 = f32[8,48,256]{2,1,0:T(8,128)S(1)} collective-permute-done((f32[8,48,256]{2,1,0:T(8,128)S(1)}, f32[8,48,256]{2,1,0:T(8,128)S(1)}, u32[]{:S(2)}, u32[]{:S(2)}) %collective-permute-start.5) | collective-permute-done | bytes 393248 | tf_op jit(solution)/shard_map/ppermute | solution.py:502
  83.4 0.1 slice_add_fusion.1
  83.5 0.0 copy-start.2
  83.5 1.7 %collective-permute-start.6 = (f32[4,48,256]{2,1,0:T(8,128)S(1)}, f32[4,48,256]{2,1,0:T(8,128)S(1)}, u32[]{:S(2)}, u32[]{:S(2)}) collective-permute-start(f32[4,48,256]{2,1,0:T(8,128)S(1)} %slice.67), channel_id=1, source_target_pairs={{0,1},{1,0},{2,3},{3,2},{4,5},{5,4},{6,7},{7,6},{8,9},{9,8},{10,11... | collective-permute-start | bytes 589832 | tf_op jit(solution)/shard_map/ppermute | solution.py:502
  85.2 0.0 collective-permute-done.8
  85.2 0.1 slice_add_fusion
  85.2 1.5 %collective-permute-start.9 = (f32[4,48,256]{2,1,0:T(8,128)S(1)}, f32[4,48,256]{2,1,0:T(8,128)S(1)}, u32[]{:S(2)}, u32[]{:S(2)}) collective-permute-start(f32[4,48,256]{2,1,0:T(8,128)S(1)} %slice.72), channel_id=1, source_target_pairs={{0,16},{8,24},{16,0},{24,8},{1,17},{9,25},{17,1},{25,9},{2,18},{10... | collective-permute-start | bytes 589832 | tf_op jit(solution)/shard_map/ppermute | solution.py:502
  86.8 3.3 %collective-permute-done.6 = f32[4,48,256]{2,1,0:T(8,128)S(1)} collective-permute-done((f32[4,48,256]{2,1,0:T(8,128)S(1)}, f32[4,48,256]{2,1,0:T(8,128)S(1)}, u32[]{:S(2)}, u32[]{:S(2)}) %collective-permute-start.6) | collective-permute-done | bytes 196640 | tf_op jit(solution)/shard_map/ppermute | solution.py:502
  90.2 1.8 %collective-permute-done.9 = f32[4,48,256]{2,1,0:T(8,128)S(1)} collective-permute-done((f32[4,48,256]{2,1,0:T(8,128)S(1)}, f32[4,48,256]{2,1,0:T(8,128)S(1)}, u32[]{:S(2)}, u32[]{:S(2)}) %collective-permute-start.9) | collective-permute-done | bytes 196640 | tf_op jit(solution)/shard_map/ppermute | solution.py:502
  92.1 8.3 %collective-permute-start.10 = (f32[2,96,256]{2,1,0:T(8,128)S(1)}, f32[2,96,256]{2,1,0:T(8,128)S(1)}, u32[]{:S(2)}, u32[]{:S(2)}) collective-permute-start(f32[2,96,256]{2,1,0:T(8,128)S(1)} %pad_maximum_fusion), channel_id=1, source_target_pairs={{0,2},{1,3},{2,0},{3,1},{4,6},{5,7},{6,4},{7,5},{8,10},{9,11},{10,... | collective-permute-start | bytes 589832 | tf_op jit(solution)/shard_map/ppermute | solution.py:502
  100.4 4.2 %collective-permute-done.10 = f32[2,96,256]{2,1,0:T(8,128)S(1)} collective-permute-done((f32[2,96,256]{2,1,0:T(8,128)S(1)}, f32[2,96,256]{2,1,0:T(8,128)S(1)}, u32[]{:S(2)}, u32[]{:S(2)}) %collective-permute-start.10) | collective-permute-done | bytes 196640 | tf_op jit(solution)/shard_map/ppermute | solution.py:502
  104.7 0.7 collective-permute-start.11
  105.4 4.9 %collective-permute-done.11 = f32[1,96,256]{2,1,0:T(8,128)S(1)} collective-permute-done((f32[1,96,256]{2,1,0:T(8,128)S(1)}, f32[1,96,256]{2,1,0:T(8,128)S(1)}, u32[]{:S(2)}, u32[]{:S(2)}) %collective-permute-start.11) | collective-permute-done | bytes 98336 | tf_op jit(solution)/shard_map/ppermute | solution.py:502
  110.3 0.6 copy.13
  111.0 0.6 reshape.29
  111.7 0.0 all-to-all-done
  111.7 0.0 copy-done.2
  111.7 3.5 %tendency_rows.1 = f32[1024,768]{1,0:T(8,128)} custom-call(f32[1024,512]{1,0:T(8,128)S(1)} %bitcast.18, bf16[512,768]{1,0:T(8,128)(2,1)S(1)} %copy-done.2), custom_call_target="tpu_custom_call" | custom-call | flops 1610612736 | bytes 6291456 | tf_op jit(solution)/shard_map/tendency_rows/pallas_call | solution.py:686
  (15 shorter events, 0.3 us)
Async XLA Ops:
  0.6 5.3 %copy-start = (f32[32,32,768]{2,1,0:T(8,128)S(1)}, f32[32,32,768]{2,1,0:T(8,128)}, u32[]{:S(2)}) copy-start(f32[32,32,768]{2,1,0:T(8,128)} %air.1) | copy-start | bytes 9437188
  3.7 10.8 %collective-permute-start = (f32[64,768]{1,0:T(8,128)S(1)}, f32[64,768]{1,0:T(8,128)S(1)}, u32[]{:S(2)}, u32[]{:S(2)}) collective-permute-start(f32[64,768]{1,0:T(8,128)S(1)} %get-tuple-element.27), channel_id=1, source_target_pairs={{0,8},{8,16},{16,24},{24,0},{1,9},{9,17},{17,25},{25,1},{2,10},{10... | collective-permute-start | bytes 589832 | tf_op jit(solution)/shard_map/ppermute | solution.py:562
  3.9 10.6 %collective-permute-start.1 = (f32[64,768]{1,0:T(8,128)S(1)}, f32[64,768]{1,0:T(8,128)S(1)}, u32[]{:S(2)}, u32[]{:S(2)}) collective-permute-start(f32[64,768]{1,0:T(8,128)S(1)} %get-tuple-element.28), channel_id=1, source_target_pairs={{0,24},{8,0},{16,8},{24,16},{1,25},{9,1},{17,9},{25,17},{2,26},{10... | collective-permute-start | bytes 589832 | tf_op jit(solution)/shard_map/ppermute | solution.py:563
  5.9 15.4 %copy-start.1 = (bf16[512,768]{1,0:T(8,128)(2,1)S(1)}, bf16[512,768]{1,0:T(8,128)(2,1)}, u32[]{:S(2)}) copy-start(bf16[512,768]{1,0:T(8,128)(2,1)} %out_weights.1) | copy-start | bytes 2359300
  5.9 15.4 %copy-start.5 = (bf16[768,512]{1,0:T(8,128)(2,1)S(1)}, bf16[768,512]{1,0:T(8,128)(2,1)}, u32[]{:S(2)}) copy-start(bf16[768,512]{1,0:T(8,128)(2,1)} %in_weights.1) | copy-start | bytes 2359300
  5.9 15.4 %copy-start.9 = (s32[32,32]{1,0:T(8,128)S(1)}, s32[32,32]{1,0:T(8,128)}, u32[]{:S(2)}) copy-start(s32[32,32]{1,0:T(8,128)} %dest.3) | copy-start | bytes 12292
  5.9 15.4 %copy-start.10 = (s32[32,32]{1,0:T(8,128)S(1)}, s32[32,32]{1,0:T(8,128)}, u32[]{:S(2)}) copy-start(s32[32,32]{1,0:T(8,128)} %cost.1) | copy-start | bytes 12292
  14.5 6.8 %copy-start.3 = (f32[512,768]{1,0:T(8,128)}, f32[512,768]{1,0:T(8,128)S(1)}, u32[]{:S(2)}) copy-start(f32[512,768]{1,0:T(8,128)S(1)} %get-tuple-element.32.own) | copy-start | bytes 4718596
  16.0 16.0 %collective-permute-start.2 = (f32[72,768]{1,0:T(8,128)}, f32[72,768]{1,0:T(8,128)S(1)}, u32[]{:S(2)}, u32[]{:S(2)}) collective-permute-start(f32[72,768]{1,0:T(8,128)} %get-tuple-element.30), channel_id=1, source_target_pairs={{0,1},{1,2},{2,3},{3,4},{4,5},{5,6},{6,7},{7,0},{8,9},{9,10},{10,1... | collective-permute-start | bytes 663560 | tf_op jit(solution)/shard_map/ppermute | solution.py:592
  18.6 13.4 %collective-permute-start.3 = (f32[72,768]{1,0:T(8,128)}, f32[72,768]{1,0:T(8,128)}, u32[]{:S(2)}, u32[]{:S(2)}) collective-permute-start(f32[72,768]{1,0:T(8,128)} %get-tuple-element.31), channel_id=1, source_target_pairs={{0,7},{1,0},{2,1},{3,2},{4,3},{5,4},{6,5},{7,6},{8,15},{9,8},{10,9... | collective-permute-start | bytes 663560 | tf_op jit(solution)/shard_map/ppermute | solution.py:593
  31.3 0.7 copy-start.7
  32.0 1.4 %copy-start.4 = (f32[512,768]{1,0:T(8,128)S(1)}, f32[512,768]{1,0:T(8,128)}, u32[]{:S(2)}) copy-start(f32[512,768]{1,0:T(8,128)} %copy-done.3) | copy-start | bytes 4718596
  33.4 1.1 copy-start.6
  34.5 0.9 copy-start.8
  43.3 68.4 %all-to-all-start = ((f32[32,32,512]{2,1,0:T(8,128)}), f32[32,32,512]{2,1,0:T(8,128)S(1)}, u32[]{:S(2)}, u32[]{:S(2)}) async-start(f32[32,32,512]{2,1,0:T(8,128)} %bitcast.19), calls=%async_computation | async-start | bytes 4194304 | tf_op jit(solution)/shard_map/all_to_all | solution.py:632
  63.0 5.6 %collective-permute-start.4 = (f32[16,48,256]{2,1,0:T(8,128)S(1)}, f32[16,48,256]{2,1,0:T(8,128)S(1)}, u32[]{:S(2)}, u32[]{:S(2)}) collective-permute-start(f32[16,48,256]{2,1,0:T(8,128)S(1)} %get-tuple-element.46), channel_id=1, source_target_pairs={{0,8},{8,0},{16,24},{24,16},{1,9},{9,1},{17,25},{25,17},{2,10},{10... | collective-permute-start | bytes 2359304 | tf_op jit(solution)/shard_map/ppermute | solution.py:502
  68.0 2.4 %collective-permute-start.7 = (f32[16,48,256]{2,1,0:T(8,128)S(1)}, f32[16,48,256]{2,1,0:T(8,128)S(1)}, u32[]{:S(2)}, u32[]{:S(2)}) collective-permute-start(f32[16,48,256]{2,1,0:T(8,128)S(1)} %get-tuple-element.50), channel_id=1, source_target_pairs={{0,8},{8,0},{16,24},{24,16},{1,9},{9,1},{17,25},{25,17},{2,10},{10... | collective-permute-start | bytes 2359304 | tf_op jit(solution)/shard_map/ppermute | solution.py:502
  68.7 14.7 %collective-permute-start.5 = (f32[8,48,256]{2,1,0:T(8,128)S(1)}, f32[8,48,256]{2,1,0:T(8,128)S(1)}, u32[]{:S(2)}, u32[]{:S(2)}) collective-permute-start(f32[8,48,256]{2,1,0:T(8,128)S(1)} %slice.65), channel_id=1, source_target_pairs={{0,16},{8,24},{16,0},{24,8},{1,17},{9,25},{17,1},{25,9},{2,18},{10... | collective-permute-start | bytes 1179656 | tf_op jit(solution)/shard_map/ppermute | solution.py:502
  70.6 14.6 %collective-permute-start.8 = (f32[8,48,256]{2,1,0:T(8,128)S(1)}, f32[8,48,256]{2,1,0:T(8,128)S(1)}, u32[]{:S(2)}, u32[]{:S(2)}) collective-permute-start(f32[8,48,256]{2,1,0:T(8,128)S(1)} %slice.70), channel_id=1, source_target_pairs={{0,1},{1,0},{2,3},{3,2},{4,5},{5,4},{6,7},{7,6},{8,9},{9,8},{10,11... | collective-permute-start | bytes 1179656 | tf_op jit(solution)/shard_map/ppermute | solution.py:502
  83.5 28.2 %copy-start.2 = (bf16[512,768]{1,0:T(8,128)(2,1)S(1)}, bf16[512,768]{1,0:T(8,128)(2,1)}, u32[]{:S(2)}) copy-start(bf16[512,768]{1,0:T(8,128)(2,1)} %out_weights.1) | copy-start | bytes 2359300
  83.5 6.6 %collective-permute-start.6 = (f32[4,48,256]{2,1,0:T(8,128)S(1)}, f32[4,48,256]{2,1,0:T(8,128)S(1)}, u32[]{:S(2)}, u32[]{:S(2)}) collective-permute-start(f32[4,48,256]{2,1,0:T(8,128)S(1)} %slice.67), channel_id=1, source_target_pairs={{0,1},{1,0},{2,3},{3,2},{4,5},{5,4},{6,7},{7,6},{8,9},{9,8},{10,11... | collective-permute-start | bytes 589832 | tf_op jit(solution)/shard_map/ppermute | solution.py:502
  85.2 6.7 %collective-permute-start.9 = (f32[4,48,256]{2,1,0:T(8,128)S(1)}, f32[4,48,256]{2,1,0:T(8,128)S(1)}, u32[]{:S(2)}, u32[]{:S(2)}) collective-permute-start(f32[4,48,256]{2,1,0:T(8,128)S(1)} %slice.72), channel_id=1, source_target_pairs={{0,16},{8,24},{16,0},{24,8},{1,17},{9,25},{17,1},{25,9},{2,18},{10... | collective-permute-start | bytes 589832 | tf_op jit(solution)/shard_map/ppermute | solution.py:502
  92.1 12.6 %collective-permute-start.10 = (f32[2,96,256]{2,1,0:T(8,128)S(1)}, f32[2,96,256]{2,1,0:T(8,128)S(1)}, u32[]{:S(2)}, u32[]{:S(2)}) collective-permute-start(f32[2,96,256]{2,1,0:T(8,128)S(1)} %pad_maximum_fusion), channel_id=1, source_target_pairs={{0,2},{1,3},{2,0},{3,1},{4,6},{5,7},{6,4},{7,5},{8,10},{9,11},{10,... | collective-permute-start | bytes 589832 | tf_op jit(solution)/shard_map/ppermute | solution.py:502
  104.7 5.6 %collective-permute-start.11 = (f32[1,96,256]{2,1,0:T(8,128)S(1)}, f32[1,96,256]{2,1,0:T(8,128)S(1)}, u32[]{:S(2)}, u32[]{:S(2)}) collective-permute-start(f32[1,96,256]{2,1,0:T(8,128)S(1)} %slice.77), channel_id=1, source_target_pairs={{0,4},{1,5},{2,6},{3,7},{4,0},{5,1},{6,2},{7,3},{8,12},{9,13},{10,... | collective-permute-start | bytes 294920 | tf_op jit(solution)/shard_map/ppermute | solution.py:502

commit v6 on v4

--- a/solution.py
+++ b/solution.py
@@ -11,7 +11,6 @@
 COURANT = 0.1
 EPS = 1e-06
 LANES = 128
-COL = 256
 F32 = jnp.float32
 BF16 = jnp.bfloat16
 SIDE_WINDS = (((0, 1.0), (1, 1.0)), ((1, 1.0), (0, -1.0)), ((0, -1.0), (1, -1.0)), ((1, -1.0), (0, 1.0)))
@@ -120,7 +119,10 @@
                     q[i], before[i] = ahead, flux
         return carry
 
-    lax.fori_loop(0, (hi - lo) // block, body, 0)
+    if hi - lo == block:
+        body(0, 0)
+    else:
+        lax.fori_loop(0, (hi - lo) // block, body, 0)
 
 
 def network_forward(x, mask, w_in, w_out, state, hsum, rows, kept):
@@ -270,20 +272,20 @@
 def rim_kernel(n, levels, turn, dest, h0, h1, h2, h3, own, mask_rim, w_in, w_out, before,
                n_o, s_o, g_o, h_o, outgoing, sent,
                normed, scale, slope, hidden, sems,
-               wide, wide_one, wide_two, slim, slim_one, slim_two, lead_wide, sub_wide, lead_slim, sub_slim, x_rim, hsum):
+               cells_wide, cells_slim, lead_wide, sub_wide, lead_slim, sub_slim, x_rim, hsum):
     del before
     state, out = (normed, scale, slope, hidden), (n_o, s_o, g_o, h_o)
     o = turn[0, 0]
     halo = (h0, h1, h2, h3)
+    wide = [lead_wide, sub_wide] + [cells_wide.at[step] for step in range(3)]
+    slim = [lead_slim, sub_slim] + [cells_slim.at[step] for step in range(3)]
     for k in range(4):
-        ends = k % 2 == 0
-        src, one, two = (wide, wide_one, wide_two) if ends else (slim, slim_one, slim_two)
-        lead, sub = (lead_wide, sub_wide) if ends else (lead_slim, sub_slim)
+        lead, sub, src, one, two = slim if k % 2 else wide
         for depth in range(6):
             d = depth - 2
             row = halo[k][(1 - depth) * n : (2 - depth) * n, :] if d < 0 else own[(k * 4 + d) * n : (k * 4 + d + 1) * n, :]
             src[depth, 0:n, :] = row
-            if ends:
+            if k % 2 == 0:
                 src[depth, n + 2 : n + 8, :] = row[0:6, :]
                 src[depth, n + 8 : n + 14, :] = row[n - 6 : n, :]
                 for e in range(2):
@@ -302,7 +304,7 @@
         for d in range(2):
             at = (k * 2 + d) * n
             x_rim[at : at + n, :] = two[2 + d, 0:n, :]
-            if ends:
+            if k % 2 == 0:
                 x_rim[at : at + 2, :] = two[2 + d, n + 2 : n + 4, :]
                 x_rim[at + n - 2 : at + n, :] = two[2 + d, n + 12 : n + 14, :]
     turn_winds(x_rim, (0, 8 * n), (4 - o) % 4, levels)
@@ -313,10 +315,11 @@
             copy.start()
             copies.append(copy)
 
-    rows = slice(0, 8 * n)
-    run_together(
-        [network_forward(lambda: x_rim[...], lambda: mask_rim[...], w_in, w_out, state, hsum, rows, kept)], 0
-    )
+    halves = ((slice(0, 4 * n), lambda use: None), (slice(4 * n, 8 * n), kept))
+    run_together([
+        network_forward(lambda r=r: x_rim[r, :], lambda r=r: mask_rim[r, :], w_in, w_out, state, hsum, r, done)
+        for r, done in halves
+    ], 0)
     for k in range(4):
         (bi, di, mi), (bj, dj, mj) = side_cells((k - o + 4) % 4, n)
         skip = 2 * (k % 2)
@@ -382,8 +385,10 @@
                 at = at * 2 + (away[axis] // bit) % 2
 
             def store(ref, p=p, at=at):
-                for c in range(grad.shape[1] // COL):
-                    ref[at, c * rows : (c + 1) * rows, :] = grad[p * rows : (p + 1) * rows, c * COL : (c + 1) * COL]
+                chunks = grad.shape[1] // LANES
+                for c in range(chunks):
+                    part = grad[p * rows : (p + 1) * rows, c * LANES : (c + 1) * LANES]
+                    ref[at, pl.ds(c, rows, stride=chunks), :] = part
 
             pl.when(away["grp"] % 2 == 0)(functools.partial(store, keep))
             pl.when(away["grp"] % 2 == 1)(functools.partial(store, send))
@@ -430,6 +435,7 @@
 
     start_next()
     start_next()
+    start_next()
     steps = []
     for part, start, size in parts:
         at = slice(edge + start, edge + start + size)
@@ -464,14 +470,12 @@
     store_pieces(grid_shape, me, order, grad_out, keep, send)
 
 
-def sum_over_devices(keep, send, order, sizes):
-    total = None
+def exchange_sums(keep, send, order, sizes):
     for axis, bit in order:
-        if total is not None:
-            half = total.shape[0] // 2
-            keep, send = total[:half], total[half:]
-        total = keep + lax.ppermute(send, axis, [(i, i ^ bit) for i in range(sizes[axis])])
-    return total[0]
+        keep = keep + lax.ppermute(send, axis, [(i, i ^ bit) for i in range(sizes[axis])])
+        half = keep.shape[0] // 2
+        keep, send = keep[:half], keep[half:]
+    return keep, send
 
 
 def output_kernel(rows, w_out, out):
@@ -503,6 +507,7 @@
     air_rows = air_state.reshape(cells, feats)
     cot_rows = cotangent.reshape(cells, feats)
     both = ("grp", "tile")
+    stay = lambda x: pltpu.with_memory_space_constraint(x, pltpu.HBM)
 
     def state(space, rows):
         return [
@@ -580,10 +585,9 @@
         out_specs=[HBM] * 4 + [VMEM, HBM],
         input_output_aliases={10: 4},
         scratch_shapes=[*state(pltpu.VMEM, rim), pltpu.SemaphoreType.DMA((2, 3, 4))]
-        + [pltpu.VMEM((6, wide, feats), F32)] * 3
-        + [pltpu.VMEM((6, slim, feats), F32)] * 3
-        + [pltpu.VMEM((5, wide, period * LANES), F32), pltpu.VMEM((4, wide, period * LANES), F32)]
-        + [pltpu.VMEM((5, slim, period * LANES), F32), pltpu.VMEM((4, slim, period * LANES), F32)]
+        + [pltpu.VMEM((3, 6, wide, feats), F32), pltpu.VMEM((3, 6, slim, feats), F32)]
+        + [pltpu.VMEM((rows, wide, period * LANES), F32) for rows in (5, 4)]
+        + [pltpu.VMEM((rows, slim, period * LANES), F32) for rows in (5, 4)]
         + [pltpu.VMEM((rim, feats), F32), pltpu.VMEM((rim, units), F32)],
         compiler_params=params(16),
         cost_estimate=pl.CostEstimate(
@@ -597,14 +601,13 @@
     ).reshape(cells, units)
 
     me = jnp.stack([lax.axis_index("grp"), lax.axis_index("tile")]).astype(jnp.int32)
-    stay = lambda x: pltpu.with_memory_space_constraint(x, pltpu.HBM)
     saved = lambda rows: state(pltpu.VMEM, rows)[:3]
-    halves = lambda rows, columns: [shape((count // 2, rows // count * (columns // COL), COL), F32)] * 2
+    halves = [shape((count // 2, feats * units // count // LANES, LANES), F32)] * 2
     orders = [exchange_order(groups, tiles, tile_first) for tile_first in (False, True)]
     *pieces_in, err_out, hidden = pl.pallas_call(
         functools.partial(backward_kernel, n, (groups, tiles), orders[0]),
         out_shape=[
-            *halves(feats, units),
+            *halves,
             pltpu.VMEM((3, inner + rim, feats), BF16),
             pltpu.VMEM((3, inner + rim, units), BF16),
         ],
@@ -628,7 +631,7 @@
     )(me, orientation, *map(stay, (cot_rows, weight_in, weight_out, *saved_inner, *saved_rim)))
     pieces_out = pl.pallas_call(
         functools.partial(output_gradient_kernel, (groups, tiles), orders[1]),
-        out_shape=halves(units, feats),
+        out_shape=halves,
         in_specs=[SMEM, VMEM, VMEM],
         out_specs=[VMEM] * 2,
         scratch_shapes=[pltpu.VMEM((units, feats), F32)],
@@ -637,10 +640,13 @@
         name="output_gradient",
     )(me, err_out, hidden)
 
-    flat = lambda part, rows: part.reshape(-1, rows, COL).transpose(1, 0, 2).reshape(-1)
     sizes = {"grp": groups, "tile": tiles}
-    summed_in = flat(sum_over_devices(*pieces_in, orders[0], sizes), feats // count)
-    summed_out = flat(sum_over_devices(*pieces_out, orders[1], sizes), units // count)
+    far = [pair for pair in orders[0] if pair[0] == "tile" and pair[1] > 1]
+    near = len(orders[0]) - len(far)
+    sums = [exchange_sums(*pieces, order[:near], sizes) for pieces, order in zip((pieces_in, pieces_out), orders)]
+    split = sums[0][0].shape[1]
+    keep, send = (jnp.concatenate(pair, axis=1) for pair in zip(*sums))
+    keep, send = exchange_sums(keep, send, far[:-1], sizes)
 
     block = cells // 4
     tendency = pl.pallas_call(
@@ -653,6 +659,11 @@
         cost_estimate=pl.CostEstimate(flops=4 * cells * feats * units, bytes_accessed=6 << 20, transcendentals=0),
         name="tendency_rows",
     )(arrived, weight_out)
+    (axis, bit), = far[-1:]
+    arriving = lax.ppermute(send, axis, [(i, i ^ bit) for i in range(sizes[axis])])
+    keep, tendency = lax.optimization_barrier((keep, tendency))
+    keep = keep + arriving
+    summed_in, summed_out = keep[0, :split].reshape(-1), keep[0, split:].reshape(-1)
     return (tendency, summed_in, summed_out)
 
 

time: 109 us -> 108 us (level); the launches traced: 109 us -> 107 us
  starting transfers between devices: 32.4 us -> 27.5 us
  waiting for transfers between devices: 18.2 us -> 22.1 us
    ppermute x10 -> x8, starting transfers between devices: 21 us -> 16.1 us  [the longest x7 15.5 us: exchange_sums(): lax.ppermute(send, axis, [(i, i ^ bit) for i in range(sizes[axis])])]
    ppermute x10 -> x8, waiting for transfers between devices: 18.2 us -> 22.1 us  [the longest x7 20.7 us: exchange_sums(): lax.ppermute(send, axis, [(i, i ^ bit) for i in range(sizes[axis])])]
    unnamed x15 -> x14, local copies, waits for them, and re-layouts: 2.55 us -> 1.91 us
  transfers between devices with their start and end apart: 15 -> 13, of which waited for: 7 -> 6; matrix products, arithmetic and copies ran while one was open for 2% -> 1% of each run, Pallas kernels for 37% -> 40%
where the time goes in v6:
time: 108 us; the launch traced here: 107 us
  Pallas kernels  52.6 us (49%)
  starting transfers between devices  27.5 us (25%)
  waiting for transfers between devices  22.1 us (20%)
  local copies, waits for them, and re-layouts  2.68 us (2%)
  between operations  1.5 us (1%)
    ppermute x7, waiting for transfers between devices, exchange_sums(): lax.ppermute(send, axis, [(i, i ^ bit) for i in range(sizes[axis])])  20.7 us
    pallas_call x1, Pallas kernels, per_device(): pl.pallas_call(functools.partial(backward_kernel, n, (groups, tiles), ord...  15.8 us
    ppermute x7, starting transfers between devices, exchange_sums(): lax.ppermute(send, axis, [(i, i ^ bit) for i in range(sizes[axis])])  15.5 us
    pallas_call x1, Pallas kernels, per_device(): pl.pallas_call(functools.partial(inner_network_kernel, n), out_shape=[*st...  9.91 us
    pallas_call x1, Pallas kernels, per_device(): pl.pallas_call(functools.partial(inner_transport_kernel, n, levels), out_...  8.54 us
    pallas_call x1, Pallas kernels, per_device(): pl.pallas_call(functools.partial(rim_kernel, n, levels), out_shape=[*stat...  7.68 us
    pallas_call x1, Pallas kernels, per_device(): pl.pallas_call(functools.partial(output_gradient_kernel, (groups, tiles),...  4.95 us
    pallas_call x1, Pallas kernels, per_device(): pl.pallas_call(output_kernel, out_shape=shape((cells, feats), F32), grid=...  3.54 us
  transfers between devices with their start and end apart: 13, of which 6 were waited for; matrix products, arithmetic and copies ran while one was open for 1% of the time, Pallas kernels for 40%

profile of v6, /device:TPU:0, one launch (start us, length us, event | category | flops | bytes accessed | tf_op | source)
XLA Modules:
  0.0 106.9 jit_solution(5323889954774527589)
XLA Ops:
  1.3 0.0 copy-start
  1.3 1.9 %copy-done = f32[32,32,768]{2,1,0:T(8,128)S(1)} copy-done((f32[32,32,768]{2,1,0:T(8,128)S(1)}, f32[32,32,768]{2,1,0:T(8,128)}, u32[]{:S(2)}) %copy-start) | copy-done | bytes 3145752
  3.2 0.0 copy-start.1
  3.2 1.4 %pack_strips.1 = (f32[64,768]{1,0:T(8,128)}, f32[64,768]{1,0:T(8,128)}) custom-call(s32[1,1]{1,0:T(1,128)S(6)} %copy.12.turn, f32[1024,768]{1,0:T(8,128)S(1)} %bitcast.10), custom_call_target="tpu_custom_call" | custom-call | tf_op jit(solution)/shard_map/pack_strips/pallas_call | solution.py:521
  4.6 0.5 collective-permute-start
  5.1 1.9 %collective-permute-start.1 = (f32[64,768]{1,0:T(8,128)}, f32[64,768]{1,0:T(8,128)S(1)}, u32[]{:S(2)}, u32[]{:S(2)}) collective-permute-start(f32[64,768]{1,0:T(8,128)} %get-tuple-element.35), channel_id=1, source_target_pairs={{0,24},{8,0},{16,8},{24,16},{1,25},{9,1},{17,9},{25,17},{2,26},{10... | collective-permute-start | bytes 589832 | tf_op jit(solution)/shard_map/ppermute | solution.py:530
  7.0 0.0 copy-done.1
  7.0 0.0 copy-start.2
  7.0 0.0 copy-start.4
  7.0 0.0 copy-start.5
  7.0 0.0 copy-start.6
  7.0 8.5 %inner_transport.1 = (f32[32,32,768]{2,1,0:T(8,128)S(1)}, f32[512,768]{1,0:T(8,128)S(1)}, f32[8,128]{1,0:T(8,128)S(1)}) custom-call(s32[1,1]{1,0:T(1,128)S(6)} %copy.12.turn, f32[1024,768]{1,0:T(8,128)S(1)} %bitcast.11), custom_call_target="tpu_custom_call" | custom-call | flops 47185920 | bytes 16777216 | tf_op jit(solution)/shard_map/inner_transport/pallas_call | solution.py:532
  15.6 0.0 collective-permute-done.h1
  15.6 0.0 collective-permute-done.1.h3
  15.6 0.8 pack_strips_corners.1
  16.4 2.4 %collective-permute-start.2 = (f32[72,768]{1,0:T(8,128)S(1)}, f32[72,768]{1,0:T(8,128)S(1)}, u32[]{:S(2)}, u32[]{:S(2)}) collective-permute-start(f32[72,768]{1,0:T(8,128)S(1)} %get-tuple-element.37), channel_id=1, source_target_pairs={{0,1},{1,2},{2,3},{3,4},{4,5},{5,6},{6,7},{7,0},{8,9},{9,10},{10,1... | collective-permute-start | bytes 663560 | tf_op jit(solution)/shard_map/ppermute | solution.py:559
  18.8 3.3 %collective-permute-start.3 = (f32[72,768]{1,0:T(8,128)S(1)}, f32[72,768]{1,0:T(8,128)S(1)}, u32[]{:S(2)}, u32[]{:S(2)}) collective-permute-start(f32[72,768]{1,0:T(8,128)S(1)} %get-tuple-element.38), channel_id=1, source_target_pairs={{0,7},{1,0},{2,1},{3,2},{4,3},{5,4},{6,5},{7,6},{8,15},{9,8},{10,9... | collective-permute-start | bytes 663560 | tf_op jit(solution)/shard_map/ppermute | solution.py:560
  22.1 0.0 copy-done.2
  22.1 0.0 copy-done.4
  22.1 0.0 copy-done.5
  22.1 0.0 copy-done.6
  22.1 9.9 %inner_network.1 = (bf16[3,896,768]{2,1,0:T(8,128)(2,1)}, f32[896,128]{1,0:T(8,128)}, f32[3,896,512]{2,1,0:T(8,128)}, bf16[3,896,512]{2,1,0:T(8,128)(2,1)}, f32[...) custom-call(s32[32,32]{1,0:T(8,128)S(1)} %copy-done.5, s32[1,1]{1,0:T(1,128)S(6)} %copy.12.turn, ...), custom_call_target="tpu_custom_call" | custom-call | flops 3523215360 | bytes 16777216 | tf_op jit(solution)/shard_map/inner_network/pallas_call | solution.py:562
  32.0 0.0 collective-permute-done.2.h0
  32.0 0.0 collective-permute-done.3.h2
  32.0 7.7 %rim_columns.1 = (bf16[3,256,768]{2,1,0:T(8,128)(2,1)}, f32[256,128]{1,0:T(8,128)}, f32[3,256,512]{2,1,0:T(8,128)}, bf16[3,256,512]{2,1,0:T(8,128)(2,1)}, f32[1024,512]{1,0:T(8,128)S(1)}, /*index=5*/f32[1024,512]{1,0:T(8,128)}) custom-call(s32[1,1]{1,0:T(1,128)S(6)} %copy.12.turn, s32[32,32]{1,0:T(8,128)S(1)} %copy-done.5, ...), custom_call_target="tpu_custom_call", output_to_operand_aliasing={{4}: (10, {})} | custom-call | flops 1006632960 | bytes 20971520 | tf_op jit(solution)/shard_map/rim_columns/pallas_call | solution.py:581
  39.7 3.3 %all-to-all-start = ((f32[32,32,512]{2,1,0:T(8,128)}), f32[32,32,512]{2,1,0:T(8,128)S(1)}, u32[]{:S(2)}, u32[]{:S(2)}) async-start(f32[32,32,512]{2,1,0:T(8,128)} %bitcast.14), calls=%async_computation | async-start | bytes 4194304 | tf_op jit(solution)/shard_map/all_to_all | solution.py:599
  43.0 0.1 pad_add_fusion.me
  43.1 15.8 %columns_backward.1 = (f32[16,96,128]{2,1,0:T(8,128)S(1)}, f32[16,96,128]{2,1,0:T(8,128)S(1)}, bf16[3,1152,768]{2,1,0:T(8,128)(2,1)S(1)}, bf16[3,1152,512]{2,1,0:T(8,128)(2,1)S(1)}) custom-call(s32[2]{0:T(128)S(1)} %pad_add_fusion.me, s32[1,1]{1,0:T(1,128)S(6)} %copy.12.turn, f32[1024,768]{1,0:T(8,128)} %bitcast.15, bf16[768,512]{1,0:T(8,128)(2,1)} %in_weights.1, ...), custom_call_target="tpu_custom_call" | custom-call | flops 6442450944 | bytes 20971520 | tf_op jit(solution)/shard_map/columns_backward/pallas_call | solution.py:607
  58.9 0.1 collective-permute-start.4
  59.0 4.9 %output_gradient.1 = (f32[16,96,128]{2,1,0:T(8,128)S(1)}, f32[16,96,128]{2,1,0:T(8,128)S(1)}) custom-call(s32[2]{0:T(128)S(1)} %pad_add_fusion.me, bf16[3,1152,768]{2,1,0:T(8,128)(2,1)S(1)} %get-tuple-element.48.err_out, bf16[3,1152,512]{2,1,0:T(8,128)(2,1)S(1)} %get-tuple-element.49.h), custom_call_target="tpu_custom_call" | custom-call | flops 2415919104 | bytes 8388608 | tf_op jit(solution)/shard_map/output_gradient/pallas_call | solution.py:632
  63.9 0.5 collective-permute-start.7
  64.5 0.0 collective-permute-done.4
  64.5 0.1 add.24
  64.6 1.6 %collective-permute-start.5 = (f32[8,96,128]{2,1,0:T(8,128)S(1)}, f32[8,96,128]{2,1,0:T(8,128)S(1)}, u32[]{:S(2)}, u32[]{:S(2)}) collective-permute-start(f32[8,96,128]{2,1,0:T(8,128)S(1)} %slice.65), channel_id=1, source_target_pairs={{0,16},{8,24},{16,0},{24,8},{1,17},{9,25},{17,1},{25,9},{2,18},{10... | collective-permute-start | bytes 1179656 | tf_op jit(solution)/shard_map/ppermute | solution.py:475
  66.2 0.1 collective-permute-done.7
  66.4 0.1 add.27
  66.5 0.0 copy-start.3
  66.5 1.6 %collective-permute-start.8 = (f32[8,96,128]{2,1,0:T(8,128)S(1)}, f32[8,96,128]{2,1,0:T(8,128)S(1)}, u32[]{:S(2)}, u32[]{:S(2)}) collective-permute-start(f32[8,96,128]{2,1,0:T(8,128)S(1)} %slice.70), channel_id=1, source_target_pairs={{0,1},{1,0},{2,3},{3,2},{4,5},{5,4},{6,7},{7,6},{8,9},{9,8},{10,11... | collective-permute-start | bytes 1179656 | tf_op jit(solution)/shard_map/ppermute | solution.py:475
  68.2 11.1 %collective-permute-done.5 = f32[8,96,128]{2,1,0:T(8,128)S(1)} collective-permute-done((f32[8,96,128]{2,1,0:T(8,128)S(1)}, f32[8,96,128]{2,1,0:T(8,128)S(1)}, u32[]{:S(2)}, u32[]{:S(2)}) %collective-permute-start.5) | collective-permute-done | bytes 393248 | tf_op jit(solution)/shard_map/ppermute | solution.py:475
  79.3 0.1 slice_add_fusion.1
  79.4 1.7 %collective-permute-start.6 = (f32[4,96,128]{2,1,0:T(8,128)S(1)}, f32[4,96,128]{2,1,0:T(8,128)S(1)}, u32[]{:S(2)}, u32[]{:S(2)}) collective-permute-start(f32[4,96,128]{2,1,0:T(8,128)S(1)} %slice.67), channel_id=1, source_target_pairs={{0,1},{1,0},{2,3},{3,2},{4,5},{5,4},{6,7},{7,6},{8,9},{9,8},{10,11... | collective-permute-start | bytes 589832 | tf_op jit(solution)/shard_map/ppermute | solution.py:475
  81.1 0.0 collective-permute-done.8
  81.1 1.5 %collective-permute-start.9 = (f32[4,96,128]{2,1,0:T(8,128)S(1)}, f32[4,96,128]{2,1,0:T(8,128)S(1)}, u32[]{:S(2)}, u32[]{:S(2)}) collective-permute-start(f32[4,96,128]{2,1,0:T(8,128)S(1)} %slice.72), channel_id=1, source_target_pairs={{0,16},{8,24},{16,0},{24,8},{1,17},{9,25},{17,1},{25,9},{2,18},{10... | collective-permute-start | bytes 589832 | tf_op jit(solution)/shard_map/ppermute | solution.py:475
  82.7 3.3 %collective-permute-done.6 = f32[4,96,128]{2,1,0:T(8,128)S(1)} collective-permute-done((f32[4,96,128]{2,1,0:T(8,128)S(1)}, f32[4,96,128]{2,1,0:T(8,128)S(1)}, u32[]{:S(2)}, u32[]{:S(2)}) %collective-permute-start.6) | collective-permute-done | bytes 196640 | tf_op jit(solution)/shard_map/ppermute | solution.py:475
  86.0 1.8 %collective-permute-done.9 = f32[4,96,128]{2,1,0:T(8,128)S(1)} collective-permute-done((f32[4,96,128]{2,1,0:T(8,128)S(1)}, f32[4,96,128]{2,1,0:T(8,128)S(1)}, u32[]{:S(2)}, u32[]{:S(2)}) %collective-permute-start.9) | collective-permute-done | bytes 196640 | tf_op jit(solution)/shard_map/ppermute | solution.py:475
  87.9 8.4 %collective-permute-start.10 = (f32[2,192,128]{2,1,0:T(8,128)S(1)}, f32[2,192,128]{2,1,0:T(8,128)S(1)}, u32[]{:S(2)}, u32[]{:S(2)}) collective-permute-start(f32[2,192,128]{2,1,0:T(8,128)S(1)} %pad_maximum_fusion), channel_id=1, source_target_pairs={{0,2},{1,3},{2,0},{3,1},{4,6},{5,7},{6,4},{7,5},{8,10},{9,11},{10,... | collective-permute-start | bytes 589832 | tf_op jit(solution)/shard_map/ppermute | solution.py:475
  96.3 4.2 %collective-permute-done.10 = f32[2,192,128]{2,1,0:T(8,128)S(1)} collective-permute-done((f32[2,192,128]{2,1,0:T(8,128)S(1)}, f32[2,192,128]{2,1,0:T(8,128)S(1)}, u32[]{:S(2)}, u32[]{:S(2)}) %collective-permute-start.10) | collective-permute-done | bytes 196640 | tf_op jit(solution)/shard_map/ppermute | solution.py:475
  100.6 0.6 collective-permute-start.11
  101.2 0.0 all-to-all-done
  101.2 0.0 copy-done.3
  101.3 3.5 %tendency_rows.1 = f32[1024,768]{1,0:T(8,128)} custom-call(f32[1024,512]{1,0:T(8,128)S(1)} %bitcast.13, bf16[512,768]{1,0:T(8,128)(2,1)S(1)} %copy-done.3), custom_call_target="tpu_custom_call" | custom-call | flops 1610612736 | bytes 6291456 | tf_op jit(solution)/shard_map/tendency_rows/pallas_call | solution.py:652
  104.8 1.4 %collective-permute-done.11 = f32[1,192,128]{2,1,0:T(8,128)S(1)} collective-permute-done((f32[1,192,128]{2,1,0:T(8,128)S(1)}, f32[1,192,128]{2,1,0:T(8,128)S(1)}, u32[]{:S(2)}, u32[]{:S(2)}) %collective-permute-start.11) | collective-permute-done | bytes 98336 | tf_op jit(solution)/shard_map/ppermute | solution.py:663
  106.2 0.6 slice_bitcast_fusion
  (13 shorter events, 0.3 us)
Async XLA Ops:
  1.3 1.9 %copy-start = (f32[32,32,768]{2,1,0:T(8,128)S(1)}, f32[32,32,768]{2,1,0:T(8,128)}, u32[]{:S(2)}) copy-start(f32[32,32,768]{2,1,0:T(8,128)} %param.7) | copy-start | bytes 9437188
  3.2 3.8 %copy-start.1 = (f32[32,32,768]{2,1,0:T(8,128)S(1)}, f32[32,32,768]{2,1,0:T(8,128)}, u32[]{:S(2)}) copy-start(f32[32,32,768]{2,1,0:T(8,128)} %param.7) | copy-start | bytes 9437188
  4.6 11.0 %collective-permute-start = (f32[64,768]{1,0:T(8,128)}, f32[64,768]{1,0:T(8,128)S(1)}, u32[]{:S(2)}, u32[]{:S(2)}) collective-permute-start(f32[64,768]{1,0:T(8,128)} %get-tuple-element.34), channel_id=1, source_target_pairs={{0,8},{8,16},{16,24},{24,0},{1,9},{9,17},{17,25},{25,1},{2,10},{10... | collective-permute-start | bytes 589832 | tf_op jit(solution)/shard_map/ppermute | solution.py:529
  5.1 10.5 %collective-permute-start.1 = (f32[64,768]{1,0:T(8,128)}, f32[64,768]{1,0:T(8,128)S(1)}, u32[]{:S(2)}, u32[]{:S(2)}) collective-permute-start(f32[64,768]{1,0:T(8,128)} %get-tuple-element.35), channel_id=1, source_target_pairs={{0,24},{8,0},{16,8},{24,16},{1,25},{9,1},{17,9},{25,17},{2,26},{10... | collective-permute-start | bytes 589832 | tf_op jit(solution)/shard_map/ppermute | solution.py:530
  7.0 15.1 %copy-start.2 = (bf16[512,768]{1,0:T(8,128)(2,1)S(1)}, bf16[512,768]{1,0:T(8,128)(2,1)}, u32[]{:S(2)}) copy-start(bf16[512,768]{1,0:T(8,128)(2,1)} %w_out.5) | copy-start | bytes 2359300
  7.0 15.1 %copy-start.4 = (bf16[768,512]{1,0:T(8,128)(2,1)S(1)}, bf16[768,512]{1,0:T(8,128)(2,1)}, u32[]{:S(2)}) copy-start(bf16[768,512]{1,0:T(8,128)(2,1)} %in_weights.1) | copy-start | bytes 2359300
  7.0 15.1 %copy-start.5 = (s32[32,32]{1,0:T(8,128)S(1)}, s32[32,32]{1,0:T(8,128)}, u32[]{:S(2)}) copy-start(s32[32,32]{1,0:T(8,128)} %dest.3) | copy-start | bytes 12292
  7.0 15.1 %copy-start.6 = (s32[32,32]{1,0:T(8,128)S(1)}, s32[32,32]{1,0:T(8,128)}, u32[]{:S(2)}) copy-start(s32[32,32]{1,0:T(8,128)} %cost.1) | copy-start | bytes 12292
  16.4 15.6 %collective-permute-start.2 = (f32[72,768]{1,0:T(8,128)S(1)}, f32[72,768]{1,0:T(8,128)S(1)}, u32[]{:S(2)}, u32[]{:S(2)}) collective-permute-start(f32[72,768]{1,0:T(8,128)S(1)} %get-tuple-element.37), channel_id=1, source_target_pairs={{0,1},{1,2},{2,3},{3,4},{4,5},{5,6},{6,7},{7,0},{8,9},{9,10},{10,1... | collective-permute-start | bytes 663560 | tf_op jit(solution)/shard_map/ppermute | solution.py:559
  18.8 13.2 %collective-permute-start.3 = (f32[72,768]{1,0:T(8,128)S(1)}, f32[72,768]{1,0:T(8,128)S(1)}, u32[]{:S(2)}, u32[]{:S(2)}) collective-permute-start(f32[72,768]{1,0:T(8,128)S(1)} %get-tuple-element.38), channel_id=1, source_target_pairs={{0,7},{1,0},{2,1},{3,2},{4,3},{5,4},{6,5},{7,6},{8,15},{9,8},{10,9... | collective-permute-start | bytes 663560 | tf_op jit(solution)/shard_map/ppermute | solution.py:560
  39.7 61.6 %all-to-all-start = ((f32[32,32,512]{2,1,0:T(8,128)}), f32[32,32,512]{2,1,0:T(8,128)S(1)}, u32[]{:S(2)}, u32[]{:S(2)}) async-start(f32[32,32,512]{2,1,0:T(8,128)} %bitcast.14), calls=%async_computation | async-start | bytes 4194304 | tf_op jit(solution)/shard_map/all_to_all | solution.py:599
  58.9 5.6 %collective-permute-start.4 = (f32[16,96,128]{2,1,0:T(8,128)S(1)}, f32[16,96,128]{2,1,0:T(8,128)S(1)}, u32[]{:S(2)}, u32[]{:S(2)}) collective-permute-start(f32[16,96,128]{2,1,0:T(8,128)S(1)} %get-tuple-element.47), channel_id=1, source_target_pairs={{0,8},{8,0},{16,24},{24,16},{1,9},{9,1},{17,25},{25,17},{2,10},{10... | collective-permute-start | bytes 2359304 | tf_op jit(solution)/shard_map/ppermute | solution.py:475
  63.9 2.4 %collective-permute-start.7 = (f32[16,96,128]{2,1,0:T(8,128)S(1)}, f32[16,96,128]{2,1,0:T(8,128)S(1)}, u32[]{:S(2)}, u32[]{:S(2)}) collective-permute-start(f32[16,96,128]{2,1,0:T(8,128)S(1)} %get-tuple-element.51), channel_id=1, source_target_pairs={{0,8},{8,0},{16,24},{24,16},{1,9},{9,1},{17,25},{25,17},{2,10},{10... | collective-permute-start | bytes 2359304 | tf_op jit(solution)/shard_map/ppermute | solution.py:475
  64.6 14.7 %collective-permute-start.5 = (f32[8,96,128]{2,1,0:T(8,128)S(1)}, f32[8,96,128]{2,1,0:T(8,128)S(1)}, u32[]{:S(2)}, u32[]{:S(2)}) collective-permute-start(f32[8,96,128]{2,1,0:T(8,128)S(1)} %slice.65), channel_id=1, source_target_pairs={{0,16},{8,24},{16,0},{24,8},{1,17},{9,25},{17,1},{25,9},{2,18},{10... | collective-permute-start | bytes 1179656 | tf_op jit(solution)/shard_map/ppermute | solution.py:475
  66.5 34.8 %copy-start.3 = (bf16[512,768]{1,0:T(8,128)(2,1)S(1)}, bf16[512,768]{1,0:T(8,128)(2,1)}, u32[]{:S(2)}) copy-start(bf16[512,768]{1,0:T(8,128)(2,1)} %w_out.5) | copy-start | bytes 2359300
  66.5 14.5 %collective-permute-start.8 = (f32[8,96,128]{2,1,0:T(8,128)S(1)}, f32[8,96,128]{2,1,0:T(8,128)S(1)}, u32[]{:S(2)}, u32[]{:S(2)}) collective-permute-start(f32[8,96,128]{2,1,0:T(8,128)S(1)} %slice.70), channel_id=1, source_target_pairs={{0,1},{1,0},{2,3},{3,2},{4,5},{5,4},{6,7},{7,6},{8,9},{9,8},{10,11... | collective-permute-start | bytes 1179656 | tf_op jit(solution)/shard_map/ppermute | solution.py:475
  79.4 6.6 %collective-permute-start.6 = (f32[4,96,128]{2,1,0:T(8,128)S(1)}, f32[4,96,128]{2,1,0:T(8,128)S(1)}, u32[]{:S(2)}, u32[]{:S(2)}) collective-permute-start(f32[4,96,128]{2,1,0:T(8,128)S(1)} %slice.67), channel_id=1, source_target_pairs={{0,1},{1,0},{2,3},{3,2},{4,5},{5,4},{6,7},{7,6},{8,9},{9,8},{10,11... | collective-permute-start | bytes 589832 | tf_op jit(solution)/shard_map/ppermute | solution.py:475
  81.1 6.7 %collective-permute-start.9 = (f32[4,96,128]{2,1,0:T(8,128)S(1)}, f32[4,96,128]{2,1,0:T(8,128)S(1)}, u32[]{:S(2)}, u32[]{:S(2)}) collective-permute-start(f32[4,96,128]{2,1,0:T(8,128)S(1)} %slice.72), channel_id=1, source_target_pairs={{0,16},{8,24},{16,0},{24,8},{1,17},{9,25},{17,1},{25,9},{2,18},{10... | collective-permute-start | bytes 589832 | tf_op jit(solution)/shard_map/ppermute | solution.py:475
  87.9 12.7 %collective-permute-start.10 = (f32[2,192,128]{2,1,0:T(8,128)S(1)}, f32[2,192,128]{2,1,0:T(8,128)S(1)}, u32[]{:S(2)}, u32[]{:S(2)}) collective-permute-start(f32[2,192,128]{2,1,0:T(8,128)S(1)} %pad_maximum_fusion), channel_id=1, source_target_pairs={{0,2},{1,3},{2,0},{3,1},{4,6},{5,7},{6,4},{7,5},{8,10},{9,11},{10,... | collective-permute-start | bytes 589832 | tf_op jit(solution)/shard_map/ppermute | solution.py:475
  100.6 5.6 %collective-permute-start.11 = (f32[1,192,128]{2,1,0:T(8,128)S(1)}, f32[1,192,128]{2,1,0:T(8,128)S(1)}, u32[]{:S(2)}, u32[]{:S(2)}) collective-permute-start(f32[1,192,128]{2,1,0:T(8,128)S(1)} %get-tuple-element.55), channel_id=1, source_target_pairs={{0,4},{1,5},{2,6},{3,7},{4,0},{5,1},{6,2},{7,3},{8,12},{9,13},{10,... | collective-permute-start | bytes 294920 | tf_op jit(solution)/shard_map/ppermute | solution.py:663

commit v7 on v6

--- a/solution.py
+++ b/solution.py
@@ -227,6 +227,7 @@
 
 PARTS = 2
 LAG = 0
+INNER_LAG = 3
 
 
 def inner_parts(n):
@@ -245,6 +246,15 @@
         for d in range(2):
             copy_rows(mask_rim, (k * 2 + d) * n, mask, base + cd * d, cm, n)
     copies = []
+
+    def part_steps(network, start, size):
+        yield from network
+        for i in range(start // n, (start + size) // n):
+            if i % 2 == 0:
+                yield
+            for j in range(2, n - 2):
+                outgoing[pl.ds(dest[2 + i, j], 1), :] = hsum[i * n + j : i * n + j + 1, :]
+
     steps = []
     for part, start, size in inner_parts(n):
         rows = slice(start, start + size)
@@ -256,15 +266,8 @@
                 copy.start()
                 copies.append(copy)
 
-        steps.append(network_forward(x, m, w_in, w_out, state, hsum, rows, kept))
-    run_together(steps, LAG)
-
-    def place(i, carry):
-        for j in range(2, n - 2):
-            outgoing[pl.ds(dest[i, j], 1), :] = hsum[pl.ds((i - 2) * n + j, 1), :]
-        return carry
-
-    lax.fori_loop(2, n - 2, place, 0)
+        steps.append(part_steps(network_forward(x, m, w_in, w_out, state, hsum, rows, kept), start, size))
+    run_together(steps, INNER_LAG)
     for copy in copies:
         copy.wait()
 

time: 108 us -> 107 us (level)
  transfers between devices with their start and end apart: 13 -> 13, of which waited for: 6 -> 6; matrix products, arithmetic and copies ran while one was open for 1% -> 1% of each run, Pallas kernels for 40% -> 39%
where the time goes in v7:
time: 107 us; the launch traced here: 106 us
  Pallas kernels  51.6 us (48%)
  starting transfers between devices  27.6 us (26%)
  waiting for transfers between devices  22.1 us (21%)
  local copies, waits for them, and re-layouts  2.68 us (3%)
  between operations  1.5 us (1%)
    ppermute x7, waiting for transfers between devices, exchange_sums(): lax.ppermute(send, axis, [(i, i ^ bit) for i in range(sizes[axis])])  20.7 us
    pallas_call x1, Pallas kernels, per_device(): pl.pallas_call(functools.partial(backward_kernel, n, (groups, tiles), ord...  15.8 us
    ppermute x7, starting transfers between devices, exchange_sums(): lax.ppermute(send, axis, [(i, i ^ bit) for i in range(sizes[axis])])  15.5 us
    pallas_call x1, Pallas kernels, per_device(): pl.pallas_call(functools.partial(inner_network_kernel, n), out_shape=[*st...  8.86 us
    pallas_call x1, Pallas kernels, per_device(): pl.pallas_call(functools.partial(inner_transport_kernel, n, levels), out_...  8.54 us
    pallas_call x1, Pallas kernels, per_device(): pl.pallas_call(functools.partial(rim_kernel, n, levels), out_shape=[*stat...  7.68 us
    pallas_call x1, Pallas kernels, per_device(): pl.pallas_call(functools.partial(output_gradient_kernel, (groups, tiles),...  4.95 us
    pallas_call x1, Pallas kernels, per_device(): pl.pallas_call(output_kernel, out_shape=shape((cells, feats), F32), grid=...  3.55 us
  transfers between devices with their start and end apart: 13, of which 6 were waited for; matrix products, arithmetic and copies ran while one was open for 1% of the time, Pallas kernels for 39%

profile of v7, /device:TPU:0, one launch (start us, length us, event | category | flops | bytes accessed | tf_op | source)
XLA Modules:
  0.0 105.9 jit_solution(1343057893621633197)
XLA Ops:
  1.3 0.0 copy-start
  1.3 1.9 %copy-done = f32[32,32,768]{2,1,0:T(8,128)S(1)} copy-done((f32[32,32,768]{2,1,0:T(8,128)S(1)}, f32[32,32,768]{2,1,0:T(8,128)}, u32[]{:S(2)}) %copy-start) | copy-done | bytes 3145752
  3.2 0.0 copy-start.1
  3.2 1.4 %pack_strips.1 = (f32[64,768]{1,0:T(8,128)}, f32[64,768]{1,0:T(8,128)}) custom-call(s32[1,1]{1,0:T(1,128)S(6)} %copy.12.turn, f32[1024,768]{1,0:T(8,128)S(1)} %bitcast.10), custom_call_target="tpu_custom_call" | custom-call | tf_op jit(solution)/shard_map/pack_strips/pallas_call | solution.py:524
  4.6 0.5 collective-permute-start
  5.1 1.9 %collective-permute-start.1 = (f32[64,768]{1,0:T(8,128)}, f32[64,768]{1,0:T(8,128)S(1)}, u32[]{:S(2)}, u32[]{:S(2)}) collective-permute-start(f32[64,768]{1,0:T(8,128)} %get-tuple-element.35), channel_id=1, source_target_pairs={{0,24},{8,0},{16,8},{24,16},{1,25},{9,1},{17,9},{25,17},{2,26},{10... | collective-permute-start | bytes 589832 | tf_op jit(solution)/shard_map/ppermute | solution.py:533
  7.0 0.0 copy-done.1
  7.0 0.0 copy-start.2
  7.0 0.0 copy-start.4
  7.0 0.0 copy-start.5
  7.0 0.0 copy-start.6
  7.0 8.5 %inner_transport.1 = (f32[32,32,768]{2,1,0:T(8,128)S(1)}, f32[512,768]{1,0:T(8,128)S(1)}, f32[8,128]{1,0:T(8,128)S(1)}) custom-call(s32[1,1]{1,0:T(1,128)S(6)} %copy.12.turn, f32[1024,768]{1,0:T(8,128)S(1)} %bitcast.11), custom_call_target="tpu_custom_call" | custom-call | flops 47185920 | bytes 16777216 | tf_op jit(solution)/shard_map/inner_transport/pallas_call | solution.py:535
  15.6 0.0 collective-permute-done.h1
  15.6 0.0 collective-permute-done.1.h3
  15.6 0.8 pack_strips_corners.1
  16.4 2.4 %collective-permute-start.2 = (f32[72,768]{1,0:T(8,128)S(1)}, f32[72,768]{1,0:T(8,128)S(1)}, u32[]{:S(2)}, u32[]{:S(2)}) collective-permute-start(f32[72,768]{1,0:T(8,128)S(1)} %get-tuple-element.37), channel_id=1, source_target_pairs={{0,1},{1,2},{2,3},{3,4},{4,5},{5,6},{6,7},{7,0},{8,9},{9,10},{10,1... | collective-permute-start | bytes 663560 | tf_op jit(solution)/shard_map/ppermute | solution.py:562
  18.8 3.3 %collective-permute-start.3 = (f32[72,768]{1,0:T(8,128)S(1)}, f32[72,768]{1,0:T(8,128)S(1)}, u32[]{:S(2)}, u32[]{:S(2)}) collective-permute-start(f32[72,768]{1,0:T(8,128)S(1)} %get-tuple-element.38), channel_id=1, source_target_pairs={{0,7},{1,0},{2,1},{3,2},{4,3},{5,4},{6,5},{7,6},{8,15},{9,8},{10,9... | collective-permute-start | bytes 663560 | tf_op jit(solution)/shard_map/ppermute | solution.py:563
  22.1 0.0 copy-done.2
  22.1 0.0 copy-done.4
  22.1 0.0 copy-done.5
  22.1 0.0 copy-done.6
  22.1 8.9 %inner_network.1 = (bf16[3,896,768]{2,1,0:T(8,128)(2,1)}, f32[896,128]{1,0:T(8,128)}, f32[3,896,512]{2,1,0:T(8,128)}, bf16[3,896,512]{2,1,0:T(8,128)(2,1)}, f32[...) custom-call(s32[32,32]{1,0:T(8,128)S(1)} %copy-done.5, s32[1,1]{1,0:T(1,128)S(6)} %copy.12.turn, ...), custom_call_target="tpu_custom_call" | custom-call | flops 3523215360 | bytes 16777216 | tf_op jit(solution)/shard_map/inner_network/pallas_call | solution.py:565
  30.9 0.0 collective-permute-done.2.h0
  30.9 0.0 collective-permute-done.3.h2
  31.0 7.7 %rim_columns.1 = (bf16[3,256,768]{2,1,0:T(8,128)(2,1)}, f32[256,128]{1,0:T(8,128)}, f32[3,256,512]{2,1,0:T(8,128)}, bf16[3,256,512]{2,1,0:T(8,128)(2,1)}, f32[1024,512]{1,0:T(8,128)S(1)}, /*index=5*/f32[1024,512]{1,0:T(8,128)}) custom-call(s32[1,1]{1,0:T(1,128)S(6)} %copy.12.turn, s32[32,32]{1,0:T(8,128)S(1)} %copy-done.5, ...), custom_call_target="tpu_custom_call", output_to_operand_aliasing={{4}: (10, {})} | custom-call | flops 1006632960 | bytes 20971520 | tf_op jit(solution)/shard_map/rim_columns/pallas_call | solution.py:584
  38.6 3.4 %all-to-all-start = ((f32[32,32,512]{2,1,0:T(8,128)}), f32[32,32,512]{2,1,0:T(8,128)S(1)}, u32[]{:S(2)}, u32[]{:S(2)}) async-start(f32[32,32,512]{2,1,0:T(8,128)} %bitcast.14), calls=%async_computation | async-start | bytes 4194304 | tf_op jit(solution)/shard_map/all_to_all | solution.py:602
  42.0 0.1 pad_add_fusion.me
  42.1 15.8 %columns_backward.1 = (f32[16,96,128]{2,1,0:T(8,128)S(1)}, f32[16,96,128]{2,1,0:T(8,128)S(1)}, bf16[3,1152,768]{2,1,0:T(8,128)(2,1)S(1)}, bf16[3,1152,512]{2,1,0:T(8,128)(2,1)S(1)}) custom-call(s32[2]{0:T(128)S(1)} %pad_add_fusion.me, s32[1,1]{1,0:T(1,128)S(6)} %copy.12.turn, f32[1024,768]{1,0:T(8,128)} %bitcast.15, bf16[768,512]{1,0:T(8,128)(2,1)} %in_weights.1, ...), custom_call_target="tpu_custom_call" | custom-call | flops 6442450944 | bytes 20971520 | tf_op jit(solution)/shard_map/columns_backward/pallas_call | solution.py:610
  57.9 0.1 collective-permute-start.4
  58.0 4.9 %output_gradient.1 = (f32[16,96,128]{2,1,0:T(8,128)S(1)}, f32[16,96,128]{2,1,0:T(8,128)S(1)}) custom-call(s32[2]{0:T(128)S(1)} %pad_add_fusion.me, bf16[3,1152,768]{2,1,0:T(8,128)(2,1)S(1)} %get-tuple-element.48.err_out, bf16[3,1152,512]{2,1,0:T(8,128)(2,1)S(1)} %get-tuple-element.49.h), custom_call_target="tpu_custom_call" | custom-call | flops 2415919104 | bytes 8388608 | tf_op jit(solution)/shard_map/output_gradient/pallas_call | solution.py:635
  63.0 0.5 collective-permute-start.7
  63.5 0.0 collective-permute-done.4
  63.5 0.1 add.24
  63.6 1.6 %collective-permute-start.5 = (f32[8,96,128]{2,1,0:T(8,128)S(1)}, f32[8,96,128]{2,1,0:T(8,128)S(1)}, u32[]{:S(2)}, u32[]{:S(2)}) collective-permute-start(f32[8,96,128]{2,1,0:T(8,128)S(1)} %slice.65), channel_id=1, source_target_pairs={{0,16},{8,24},{16,0},{24,8},{1,17},{9,25},{17,1},{25,9},{2,18},{10... | collective-permute-start | bytes 1179656 | tf_op jit(solution)/shard_map/ppermute | solution.py:478
  65.3 0.1 collective-permute-done.7
  65.4 0.1 add.27
  65.5 0.0 copy-start.3
  65.5 1.6 %collective-permute-start.8 = (f32[8,96,128]{2,1,0:T(8,128)S(1)}, f32[8,96,128]{2,1,0:T(8,128)S(1)}, u32[]{:S(2)}, u32[]{:S(2)}) collective-permute-start(f32[8,96,128]{2,1,0:T(8,128)S(1)} %slice.70), channel_id=1, source_target_pairs={{0,1},{1,0},{2,3},{3,2},{4,5},{5,4},{6,7},{7,6},{8,9},{9,8},{10,11... | collective-permute-start | bytes 1179656 | tf_op jit(solution)/shard_map/ppermute | solution.py:478
  67.2 11.1 %collective-permute-done.5 = f32[8,96,128]{2,1,0:T(8,128)S(1)} collective-permute-done((f32[8,96,128]{2,1,0:T(8,128)S(1)}, f32[8,96,128]{2,1,0:T(8,128)S(1)}, u32[]{:S(2)}, u32[]{:S(2)}) %collective-permute-start.5) | collective-permute-done | bytes 393248 | tf_op jit(solution)/shard_map/ppermute | solution.py:478
  78.3 0.1 slice_add_fusion.1
  78.4 1.7 %collective-permute-start.6 = (f32[4,96,128]{2,1,0:T(8,128)S(1)}, f32[4,96,128]{2,1,0:T(8,128)S(1)}, u32[]{:S(2)}, u32[]{:S(2)}) collective-permute-start(f32[4,96,128]{2,1,0:T(8,128)S(1)} %slice.67), channel_id=1, source_target_pairs={{0,1},{1,0},{2,3},{3,2},{4,5},{5,4},{6,7},{7,6},{8,9},{9,8},{10,11... | collective-permute-start | bytes 589832 | tf_op jit(solution)/shard_map/ppermute | solution.py:478
  80.1 0.0 collective-permute-done.8
  80.2 1.5 %collective-permute-start.9 = (f32[4,96,128]{2,1,0:T(8,128)S(1)}, f32[4,96,128]{2,1,0:T(8,128)S(1)}, u32[]{:S(2)}, u32[]{:S(2)}) collective-permute-start(f32[4,96,128]{2,1,0:T(8,128)S(1)} %slice.72), channel_id=1, source_target_pairs={{0,16},{8,24},{16,0},{24,8},{1,17},{9,25},{17,1},{25,9},{2,18},{10... | collective-permute-start | bytes 589832 | tf_op jit(solution)/shard_map/ppermute | solution.py:478
  81.7 3.3 %collective-permute-done.6 = f32[4,96,128]{2,1,0:T(8,128)S(1)} collective-permute-done((f32[4,96,128]{2,1,0:T(8,128)S(1)}, f32[4,96,128]{2,1,0:T(8,128)S(1)}, u32[]{:S(2)}, u32[]{:S(2)}) %collective-permute-start.6) | collective-permute-done | bytes 196640 | tf_op jit(solution)/shard_map/ppermute | solution.py:478
  85.1 1.9 %collective-permute-done.9 = f32[4,96,128]{2,1,0:T(8,128)S(1)} collective-permute-done((f32[4,96,128]{2,1,0:T(8,128)S(1)}, f32[4,96,128]{2,1,0:T(8,128)S(1)}, u32[]{:S(2)}, u32[]{:S(2)}) %collective-permute-start.9) | collective-permute-done | bytes 196640 | tf_op jit(solution)/shard_map/ppermute | solution.py:478
  87.0 8.4 %collective-permute-start.10 = (f32[2,192,128]{2,1,0:T(8,128)S(1)}, f32[2,192,128]{2,1,0:T(8,128)S(1)}, u32[]{:S(2)}, u32[]{:S(2)}) collective-permute-start(f32[2,192,128]{2,1,0:T(8,128)S(1)} %pad_maximum_fusion), channel_id=1, source_target_pairs={{0,2},{1,3},{2,0},{3,1},{4,6},{5,7},{6,4},{7,5},{8,10},{9,11},{10,... | collective-permute-start | bytes 589832 | tf_op jit(solution)/shard_map/ppermute | solution.py:478
  95.4 4.2 %collective-permute-done.10 = f32[2,192,128]{2,1,0:T(8,128)S(1)} collective-permute-done((f32[2,192,128]{2,1,0:T(8,128)S(1)}, f32[2,192,128]{2,1,0:T(8,128)S(1)}, u32[]{:S(2)}, u32[]{:S(2)}) %collective-permute-start.10) | collective-permute-done | bytes 196640 | tf_op jit(solution)/shard_map/ppermute | solution.py:478
  99.7 0.6 collective-permute-start.11
  100.3 0.0 all-to-all-done
  100.3 0.0 copy-done.3
  100.3 3.6 %tendency_rows.1 = f32[1024,768]{1,0:T(8,128)} custom-call(f32[1024,512]{1,0:T(8,128)S(1)} %bitcast.13, bf16[512,768]{1,0:T(8,128)(2,1)S(1)} %copy-done.3), custom_call_target="tpu_custom_call" | custom-call | flops 1610612736 | bytes 6291456 | tf_op jit(solution)/shard_map/tendency_rows/pallas_call | solution.py:655
  103.9 1.4 %collective-permute-done.11 = f32[1,192,128]{2,1,0:T(8,128)S(1)} collective-permute-done((f32[1,192,128]{2,1,0:T(8,128)S(1)}, f32[1,192,128]{2,1,0:T(8,128)S(1)}, u32[]{:S(2)}, u32[]{:S(2)}) %collective-permute-start.11) | collective-permute-done | bytes 98336 | tf_op jit(solution)/shard_map/ppermute | solution.py:666
  105.3 0.6 slice_bitcast_fusion
  (13 shorter events, 0.3 us)
Async XLA Ops:
  1.3 1.9 %copy-start = (f32[32,32,768]{2,1,0:T(8,128)S(1)}, f32[32,32,768]{2,1,0:T(8,128)}, u32[]{:S(2)}) copy-start(f32[32,32,768]{2,1,0:T(8,128)} %param.7) | copy-start | bytes 9437188
  3.2 3.8 %copy-start.1 = (f32[32,32,768]{2,1,0:T(8,128)S(1)}, f32[32,32,768]{2,1,0:T(8,128)}, u32[]{:S(2)}) copy-start(f32[32,32,768]{2,1,0:T(8,128)} %param.7) | copy-start | bytes 9437188
  4.6 11.0 %collective-permute-start = (f32[64,768]{1,0:T(8,128)}, f32[64,768]{1,0:T(8,128)S(1)}, u32[]{:S(2)}, u32[]{:S(2)}) collective-permute-start(f32[64,768]{1,0:T(8,128)} %get-tuple-element.34), channel_id=1, source_target_pairs={{0,8},{8,16},{16,24},{24,0},{1,9},{9,17},{17,25},{25,1},{2,10},{10... | collective-permute-start | bytes 589832 | tf_op jit(solution)/shard_map/ppermute | solution.py:532
  5.1 10.5 %collective-permute-start.1 = (f32[64,768]{1,0:T(8,128)}, f32[64,768]{1,0:T(8,128)S(1)}, u32[]{:S(2)}, u32[]{:S(2)}) collective-permute-start(f32[64,768]{1,0:T(8,128)} %get-tuple-element.35), channel_id=1, source_target_pairs={{0,24},{8,0},{16,8},{24,16},{1,25},{9,1},{17,9},{25,17},{2,26},{10... | collective-permute-start | bytes 589832 | tf_op jit(solution)/shard_map/ppermute | solution.py:533
  7.0 15.1 %copy-start.2 = (bf16[512,768]{1,0:T(8,128)(2,1)S(1)}, bf16[512,768]{1,0:T(8,128)(2,1)}, u32[]{:S(2)}) copy-start(bf16[512,768]{1,0:T(8,128)(2,1)} %w_out.5) | copy-start | bytes 2359300
  7.0 15.1 %copy-start.4 = (bf16[768,512]{1,0:T(8,128)(2,1)S(1)}, bf16[768,512]{1,0:T(8,128)(2,1)}, u32[]{:S(2)}) copy-start(bf16[768,512]{1,0:T(8,128)(2,1)} %in_weights.1) | copy-start | bytes 2359300
  7.0 15.1 %copy-start.5 = (s32[32,32]{1,0:T(8,128)S(1)}, s32[32,32]{1,0:T(8,128)}, u32[]{:S(2)}) copy-start(s32[32,32]{1,0:T(8,128)} %dest.3) | copy-start | bytes 12292
  7.0 15.1 %copy-start.6 = (s32[32,32]{1,0:T(8,128)S(1)}, s32[32,32]{1,0:T(8,128)}, u32[]{:S(2)}) copy-start(s32[32,32]{1,0:T(8,128)} %cost.1) | copy-start | bytes 12292
  16.4 14.6 %collective-permute-start.2 = (f32[72,768]{1,0:T(8,128)S(1)}, f32[72,768]{1,0:T(8,128)S(1)}, u32[]{:S(2)}, u32[]{:S(2)}) collective-permute-start(f32[72,768]{1,0:T(8,128)S(1)} %get-tuple-element.37), channel_id=1, source_target_pairs={{0,1},{1,2},{2,3},{3,4},{4,5},{5,6},{6,7},{7,0},{8,9},{9,10},{10,1... | collective-permute-start | bytes 663560 | tf_op jit(solution)/shard_map/ppermute | solution.py:562
  18.8 12.2 %collective-permute-start.3 = (f32[72,768]{1,0:T(8,128)S(1)}, f32[72,768]{1,0:T(8,128)S(1)}, u32[]{:S(2)}, u32[]{:S(2)}) collective-permute-start(f32[72,768]{1,0:T(8,128)S(1)} %get-tuple-element.38), channel_id=1, source_target_pairs={{0,7},{1,0},{2,1},{3,2},{4,3},{5,4},{6,5},{7,6},{8,15},{9,8},{10,9... | collective-permute-start | bytes 663560 | tf_op jit(solution)/shard_map/ppermute | solution.py:563
  38.6 61.7 %all-to-all-start = ((f32[32,32,512]{2,1,0:T(8,128)}), f32[32,32,512]{2,1,0:T(8,128)S(1)}, u32[]{:S(2)}, u32[]{:S(2)}) async-start(f32[32,32,512]{2,1,0:T(8,128)} %bitcast.14), calls=%async_computation | async-start | bytes 4194304 | tf_op jit(solution)/shard_map/all_to_all | solution.py:602
  57.9 5.6 %collective-permute-start.4 = (f32[16,96,128]{2,1,0:T(8,128)S(1)}, f32[16,96,128]{2,1,0:T(8,128)S(1)}, u32[]{:S(2)}, u32[]{:S(2)}) collective-permute-start(f32[16,96,128]{2,1,0:T(8,128)S(1)} %get-tuple-element.47), channel_id=1, source_target_pairs={{0,8},{8,0},{16,24},{24,16},{1,9},{9,1},{17,25},{25,17},{2,10},{10... | collective-permute-start | bytes 2359304 | tf_op jit(solution)/shard_map/ppermute | solution.py:478
  63.0 2.4 %collective-permute-start.7 = (f32[16,96,128]{2,1,0:T(8,128)S(1)}, f32[16,96,128]{2,1,0:T(8,128)S(1)}, u32[]{:S(2)}, u32[]{:S(2)}) collective-permute-start(f32[16,96,128]{2,1,0:T(8,128)S(1)} %get-tuple-element.51), channel_id=1, source_target_pairs={{0,8},{8,0},{16,24},{24,16},{1,9},{9,1},{17,25},{25,17},{2,10},{10... | collective-permute-start | bytes 2359304 | tf_op jit(solution)/shard_map/ppermute | solution.py:478
  63.6 14.7 %collective-permute-start.5 = (f32[8,96,128]{2,1,0:T(8,128)S(1)}, f32[8,96,128]{2,1,0:T(8,128)S(1)}, u32[]{:S(2)}, u32[]{:S(2)}) collective-permute-start(f32[8,96,128]{2,1,0:T(8,128)S(1)} %slice.65), channel_id=1, source_target_pairs={{0,16},{8,24},{16,0},{24,8},{1,17},{9,25},{17,1},{25,9},{2,18},{10... | collective-permute-start | bytes 1179656 | tf_op jit(solution)/shard_map/ppermute | solution.py:478
  65.5 34.8 %copy-start.3 = (bf16[512,768]{1,0:T(8,128)(2,1)S(1)}, bf16[512,768]{1,0:T(8,128)(2,1)}, u32[]{:S(2)}) copy-start(bf16[512,768]{1,0:T(8,128)(2,1)} %w_out.5) | copy-start | bytes 2359300
  65.5 14.6 %collective-permute-start.8 = (f32[8,96,128]{2,1,0:T(8,128)S(1)}, f32[8,96,128]{2,1,0:T(8,128)S(1)}, u32[]{:S(2)}, u32[]{:S(2)}) collective-permute-start(f32[8,96,128]{2,1,0:T(8,128)S(1)} %slice.70), channel_id=1, source_target_pairs={{0,1},{1,0},{2,3},{3,2},{4,5},{5,4},{6,7},{7,6},{8,9},{9,8},{10,11... | collective-permute-start | bytes 1179656 | tf_op jit(solution)/shard_map/ppermute | solution.py:478
  78.4 6.6 %collective-permute-start.6 = (f32[4,96,128]{2,1,0:T(8,128)S(1)}, f32[4,96,128]{2,1,0:T(8,128)S(1)}, u32[]{:S(2)}, u32[]{:S(2)}) collective-permute-start(f32[4,96,128]{2,1,0:T(8,128)S(1)} %slice.67), channel_id=1, source_target_pairs={{0,1},{1,0},{2,3},{3,2},{4,5},{5,4},{6,7},{7,6},{8,9},{9,8},{10,11... | collective-permute-start | bytes 589832 | tf_op jit(solution)/shard_map/ppermute | solution.py:478
  80.2 6.7 %collective-permute-start.9 = (f32[4,96,128]{2,1,0:T(8,128)S(1)}, f32[4,96,128]{2,1,0:T(8,128)S(1)}, u32[]{:S(2)}, u32[]{:S(2)}) collective-permute-start(f32[4,96,128]{2,1,0:T(8,128)S(1)} %slice.72), channel_id=1, source_target_pairs={{0,16},{8,24},{16,0},{24,8},{1,17},{9,25},{17,1},{25,9},{2,18},{10... | collective-permute-start | bytes 589832 | tf_op jit(solution)/shard_map/ppermute | solution.py:478
  87.0 12.6 %collective-permute-start.10 = (f32[2,192,128]{2,1,0:T(8,128)S(1)}, f32[2,192,128]{2,1,0:T(8,128)S(1)}, u32[]{:S(2)}, u32[]{:S(2)}) collective-permute-start(f32[2,192,128]{2,1,0:T(8,128)S(1)} %pad_maximum_fusion), channel_id=1, source_target_pairs={{0,2},{1,3},{2,0},{3,1},{4,6},{5,7},{6,4},{7,5},{8,10},{9,11},{10,... | collective-permute-start | bytes 589832 | tf_op jit(solution)/shard_map/ppermute | solution.py:478
  99.7 5.6 %collective-permute-start.11 = (f32[1,192,128]{2,1,0:T(8,128)S(1)}, f32[1,192,128]{2,1,0:T(8,128)S(1)}, u32[]{:S(2)}, u32[]{:S(2)}) collective-permute-start(f32[1,192,128]{2,1,0:T(8,128)S(1)} %get-tuple-element.55), channel_id=1, source_target_pairs={{0,4},{1,5},{2,6},{3,7},{4,0},{5,1},{6,2},{7,3},{8,12},{9,13},{10,... | collective-permute-start | bytes 294920 | tf_op jit(solution)/shard_map/ppermute | solution.py:666

commit v8 on v7

--- a/solution.py
+++ b/solution.py
@@ -52,7 +52,7 @@
         dst[pl.ds(dst_base + s, 1), :] = src[pl.ds(cell + s * step, 1), :]
         return carry
 
-    lax.fori_loop(0, count, body, 0, unroll=8)
+    lax.fori_loop(0, count, body, 0, unroll=count)
 
 
 def wind_row(src, a, which, levels):

time: 107 us -> 102 us (0.953); the launches traced: 106 us -> 102 us
  Pallas kernels: 51.6 us -> 47.4 us
  starting transfers between devices: 27.6 us -> 29.9 us
  waiting for transfers between devices: 22.1 us -> 20.3 us
    ppermute x1, starting transfers between devices: 0.63 us -> 3.42 us  [per_device(): lax.ppermute(send, axis, [(i, i ^ bit) for i in range(sizes[axis])])]
    pallas_call x1, Pallas kernels: 8.54 us -> 7.02 us  [per_device(): pl.pallas_call(functools.partial(inner_transport_kernel, n, levels), out_...]
    ppermute x1, waiting for transfers between devices: 1.39 us -> 0.01 us  [per_device(): lax.ppermute(send, axis, [(i, i ^ bit) for i in range(sizes[axis])])]
    pallas_call x1, Pallas kernels: 15.8 us -> 14.5 us  [per_device(): pl.pallas_call(functools.partial(backward_kernel, n, (groups, tiles), ord...]
  transfers between devices with their start and end apart: 13 -> 13, of which waited for: 6 -> 5; matrix products, arithmetic and copies ran while one was open for 1% -> 1% of each run, Pallas kernels for 39% -> 37%
where the time goes in v8:
time: 102 us
  Pallas kernels  47.4 us (46%)
  starting transfers between devices  29.9 us (29%)
  waiting for transfers between devices  20.3 us (20%)
  local copies, waits for them, and re-layouts  2.68 us (3%)
  between operations  1.5 us (1%)
    ppermute x7, waiting for transfers between devices, exchange_sums(): lax.ppermute(send, axis, [(i, i ^ bit) for i in range(sizes[axis])])  20.3 us
    ppermute x7, starting transfers between devices, exchange_sums(): lax.ppermute(send, axis, [(i, i ^ bit) for i in range(sizes[axis])])  14.6 us
    pallas_call x1, Pallas kernels, per_device(): pl.pallas_call(functools.partial(backward_kernel, n, (groups, tiles), ord...  14.5 us
    pallas_call x1, Pallas kernels, per_device(): pl.pallas_call(functools.partial(inner_network_kernel, n), out_shape=[*st...  8.46 us
    pallas_call x1, Pallas kernels, per_device(): pl.pallas_call(functools.partial(rim_kernel, n, levels), out_shape=[*stat...  7.68 us
    pallas_call x1, Pallas kernels, per_device(): pl.pallas_call(functools.partial(inner_transport_kernel, n, levels), out_...  7.02 us
    pallas_call x1, Pallas kernels, per_device(): pl.pallas_call(functools.partial(output_gradient_kernel, (groups, tiles),...  4.68 us
    all_to_all x1, starting transfers between devices, per_device(): lax.all_to_all(outgoing.reshape(count, cells // count, units), both, spli...  3.86 us
  transfers between devices with their start and end apart: 13, of which 5 were waited for; matrix products, arithmetic and copies ran while one was open for 1% of the time, Pallas kernels for 37%

profile of v8, /device:TPU:0, one launch (start us, length us, event | category | flops | bytes accessed | tf_op | source)
XLA Modules:
  0.0 102.2 jit_solution(8072305433882799993)
XLA Ops:
  1.3 0.0 copy-start
  1.3 1.9 %copy-done = f32[32,32,768]{2,1,0:T(8,128)S(1)} copy-done((f32[32,32,768]{2,1,0:T(8,128)S(1)}, f32[32,32,768]{2,1,0:T(8,128)}, u32[]{:S(2)}) %copy-start) | copy-done | bytes 3145752
  3.2 0.0 copy-start.1
  3.2 1.1 %pack_strips.1 = (f32[64,768]{1,0:T(8,128)}, f32[64,768]{1,0:T(8,128)}) custom-call(s32[1,1]{1,0:T(1,128)S(6)} %copy.12.turn, f32[1024,768]{1,0:T(8,128)S(1)} %bitcast.10), custom_call_target="tpu_custom_call" | custom-call | tf_op jit(solution)/shard_map/pack_strips/pallas_call | solution.py:524
  4.2 0.5 collective-permute-start
  4.7 1.9 %collective-permute-start.1 = (f32[64,768]{1,0:T(8,128)}, f32[64,768]{1,0:T(8,128)S(1)}, u32[]{:S(2)}, u32[]{:S(2)}) collective-permute-start(f32[64,768]{1,0:T(8,128)} %get-tuple-element.35), channel_id=1, source_target_pairs={{0,24},{8,0},{16,8},{24,16},{1,25},{9,1},{17,9},{25,17},{2,26},{10... | collective-permute-start | bytes 589832 | tf_op jit(solution)/shard_map/ppermute | solution.py:533
  6.6 0.0 copy-done.1
  6.6 0.0 copy-start.2
  6.6 0.0 copy-start.4
  6.6 0.0 copy-start.5
  6.6 0.0 copy-start.6
  6.7 7.0 %inner_transport.1 = (f32[32,32,768]{2,1,0:T(8,128)S(1)}, f32[512,768]{1,0:T(8,128)S(1)}, f32[8,128]{1,0:T(8,128)S(1)}) custom-call(s32[1,1]{1,0:T(1,128)S(6)} %copy.12.turn, f32[1024,768]{1,0:T(8,128)S(1)} %bitcast.11), custom_call_target="tpu_custom_call" | custom-call | flops 47185920 | bytes 16777216 | tf_op jit(solution)/shard_map/inner_transport/pallas_call | solution.py:535
  13.7 0.0 collective-permute-done.h1
  13.7 0.0 collective-permute-done.1.h3
  13.7 0.4 pack_strips_corners.1
  14.1 2.4 %collective-permute-start.2 = (f32[72,768]{1,0:T(8,128)S(1)}, f32[72,768]{1,0:T(8,128)S(1)}, u32[]{:S(2)}, u32[]{:S(2)}) collective-permute-start(f32[72,768]{1,0:T(8,128)S(1)} %get-tuple-element.37), channel_id=1, source_target_pairs={{0,1},{1,2},{2,3},{3,4},{4,5},{5,6},{6,7},{7,0},{8,9},{9,10},{10,1... | collective-permute-start | bytes 663560 | tf_op jit(solution)/shard_map/ppermute | solution.py:562
  16.5 3.3 %collective-permute-start.3 = (f32[72,768]{1,0:T(8,128)S(1)}, f32[72,768]{1,0:T(8,128)S(1)}, u32[]{:S(2)}, u32[]{:S(2)}) collective-permute-start(f32[72,768]{1,0:T(8,128)S(1)} %get-tuple-element.38), channel_id=1, source_target_pairs={{0,7},{1,0},{2,1},{3,2},{4,3},{5,4},{6,5},{7,6},{8,15},{9,8},{10,9... | collective-permute-start | bytes 663560 | tf_op jit(solution)/shard_map/ppermute | solution.py:563
  19.8 0.0 copy-done.2
  19.8 0.0 copy-done.4
  19.8 0.0 copy-done.5
  19.8 0.0 copy-done.6
  19.8 8.5 %inner_network.1 = (bf16[3,896,768]{2,1,0:T(8,128)(2,1)}, f32[896,128]{1,0:T(8,128)}, f32[3,896,512]{2,1,0:T(8,128)}, bf16[3,896,512]{2,1,0:T(8,128)(2,1)}, f32[...) custom-call(s32[32,32]{1,0:T(8,128)S(1)} %copy-done.5, s32[1,1]{1,0:T(1,128)S(6)} %copy.12.turn, ...), custom_call_target="tpu_custom_call" | custom-call | flops 3523215360 | bytes 16777216 | tf_op jit(solution)/shard_map/inner_network/pallas_call | solution.py:565
  28.3 0.0 collective-permute-done.2.h0
  28.3 0.0 collective-permute-done.3.h2
  28.3 7.7 %rim_columns.1 = (bf16[3,256,768]{2,1,0:T(8,128)(2,1)}, f32[256,128]{1,0:T(8,128)}, f32[3,256,512]{2,1,0:T(8,128)}, bf16[3,256,512]{2,1,0:T(8,128)(2,1)}, f32[1024,512]{1,0:T(8,128)S(1)}, /*index=5*/f32[1024,512]{1,0:T(8,128)}) custom-call(s32[1,1]{1,0:T(1,128)S(6)} %copy.12.turn, s32[32,32]{1,0:T(8,128)S(1)} %copy-done.5, ...), custom_call_target="tpu_custom_call", output_to_operand_aliasing={{4}: (10, {})} | custom-call | flops 1006632960 | bytes 20971520 | tf_op jit(solution)/shard_map/rim_columns/pallas_call | solution.py:584
  36.0 3.9 %all-to-all-start = ((f32[32,32,512]{2,1,0:T(8,128)}), f32[32,32,512]{2,1,0:T(8,128)S(1)}, u32[]{:S(2)}, u32[]{:S(2)}) async-start(f32[32,32,512]{2,1,0:T(8,128)} %bitcast.14), calls=%async_computation | async-start | bytes 4194304 | tf_op jit(solution)/shard_map/all_to_all | solution.py:602
  39.9 0.1 pad_add_fusion.me
  39.9 14.5 %columns_backward.1 = (f32[16,96,128]{2,1,0:T(8,128)S(1)}, f32[16,96,128]{2,1,0:T(8,128)S(1)}, bf16[3,1152,768]{2,1,0:T(8,128)(2,1)S(1)}, bf16[3,1152,512]{2,1,0:T(8,128)(2,1)S(1)}) custom-call(s32[2]{0:T(128)S(1)} %pad_add_fusion.me, s32[1,1]{1,0:T(1,128)S(6)} %copy.12.turn, f32[1024,768]{1,0:T(8,128)} %bitcast.15, bf16[768,512]{1,0:T(8,128)(2,1)} %in_weights.1, ...), custom_call_target="tpu_custom_call" | custom-call | flops 6442450944 | bytes 20971520 | tf_op jit(solution)/shard_map/columns_backward/pallas_call | solution.py:610
  54.4 0.1 collective-permute-start.4
  54.5 4.7 %output_gradient.1 = (f32[16,96,128]{2,1,0:T(8,128)S(1)}, f32[16,96,128]{2,1,0:T(8,128)S(1)}) custom-call(s32[2]{0:T(128)S(1)} %pad_add_fusion.me, bf16[3,1152,768]{2,1,0:T(8,128)(2,1)S(1)} %get-tuple-element.48.err_out, bf16[3,1152,512]{2,1,0:T(8,128)(2,1)S(1)} %get-tuple-element.49.h), custom_call_target="tpu_custom_call" | custom-call | flops 2415919104 | bytes 8388608 | tf_op jit(solution)/shard_map/output_gradient/pallas_call | solution.py:635
  59.2 0.5 collective-permute-start.7
  59.8 0.0 collective-permute-done.4
  59.8 0.1 add.24
  59.9 1.6 %collective-permute-start.5 = (f32[8,96,128]{2,1,0:T(8,128)S(1)}, f32[8,96,128]{2,1,0:T(8,128)S(1)}, u32[]{:S(2)}, u32[]{:S(2)}) collective-permute-start(f32[8,96,128]{2,1,0:T(8,128)S(1)} %slice.65), channel_id=1, source_target_pairs={{0,16},{8,24},{16,0},{24,8},{1,17},{9,25},{17,1},{25,9},{2,18},{10... | collective-permute-start | bytes 1179656 | tf_op jit(solution)/shard_map/ppermute | solution.py:478
  61.5 0.1 collective-permute-done.7
  61.7 0.1 add.27
  61.8 0.0 copy-start.3
  61.8 1.7 %collective-permute-start.8 = (f32[8,96,128]{2,1,0:T(8,128)S(1)}, f32[8,96,128]{2,1,0:T(8,128)S(1)}, u32[]{:S(2)}, u32[]{:S(2)}) collective-permute-start(f32[8,96,128]{2,1,0:T(8,128)S(1)} %slice.70), channel_id=1, source_target_pairs={{0,1},{1,0},{2,3},{3,2},{4,5},{5,4},{6,7},{7,6},{8,9},{9,8},{10,11... | collective-permute-start | bytes 1179656 | tf_op jit(solution)/shard_map/ppermute | solution.py:478
  63.5 11.7 %collective-permute-done.5 = f32[8,96,128]{2,1,0:T(8,128)S(1)} collective-permute-done((f32[8,96,128]{2,1,0:T(8,128)S(1)}, f32[8,96,128]{2,1,0:T(8,128)S(1)}, u32[]{:S(2)}, u32[]{:S(2)}) %collective-permute-start.5) | collective-permute-done | bytes 393248 | tf_op jit(solution)/shard_map/ppermute | solution.py:478
  75.1 0.1 slice_add_fusion.1
  75.2 1.1 %collective-permute-start.6 = (f32[4,96,128]{2,1,0:T(8,128)S(1)}, f32[4,96,128]{2,1,0:T(8,128)S(1)}, u32[]{:S(2)}, u32[]{:S(2)}) collective-permute-start(f32[4,96,128]{2,1,0:T(8,128)S(1)} %slice.67), channel_id=1, source_target_pairs={{0,1},{1,0},{2,3},{3,2},{4,5},{5,4},{6,7},{7,6},{8,9},{9,8},{10,11... | collective-permute-start | bytes 589832 | tf_op jit(solution)/shard_map/ppermute | solution.py:478
  76.3 0.0 collective-permute-done.8
  76.4 1.6 %collective-permute-start.9 = (f32[4,96,128]{2,1,0:T(8,128)S(1)}, f32[4,96,128]{2,1,0:T(8,128)S(1)}, u32[]{:S(2)}, u32[]{:S(2)}) collective-permute-start(f32[4,96,128]{2,1,0:T(8,128)S(1)} %slice.72), channel_id=1, source_target_pairs={{0,16},{8,24},{16,0},{24,8},{1,17},{9,25},{17,1},{25,9},{2,18},{10... | collective-permute-start | bytes 589832 | tf_op jit(solution)/shard_map/ppermute | solution.py:478
  78.0 3.7 %collective-permute-done.6 = f32[4,96,128]{2,1,0:T(8,128)S(1)} collective-permute-done((f32[4,96,128]{2,1,0:T(8,128)S(1)}, f32[4,96,128]{2,1,0:T(8,128)S(1)}, u32[]{:S(2)}, u32[]{:S(2)}) %collective-permute-start.6) | collective-permute-done | bytes 196640 | tf_op jit(solution)/shard_map/ppermute | solution.py:478
  81.7 1.1 %collective-permute-done.9 = f32[4,96,128]{2,1,0:T(8,128)S(1)} collective-permute-done((f32[4,96,128]{2,1,0:T(8,128)S(1)}, f32[4,96,128]{2,1,0:T(8,128)S(1)}, u32[]{:S(2)}, u32[]{:S(2)}) %collective-permute-start.9) | collective-permute-done | bytes 196640 | tf_op jit(solution)/shard_map/ppermute | solution.py:478
  82.9 8.0 %collective-permute-start.10 = (f32[2,192,128]{2,1,0:T(8,128)S(1)}, f32[2,192,128]{2,1,0:T(8,128)S(1)}, u32[]{:S(2)}, u32[]{:S(2)}) collective-permute-start(f32[2,192,128]{2,1,0:T(8,128)S(1)} %pad_maximum_fusion), channel_id=1, source_target_pairs={{0,2},{1,3},{2,0},{3,1},{4,6},{5,7},{6,4},{7,5},{8,10},{9,11},{10,... | collective-permute-start | bytes 589832 | tf_op jit(solution)/shard_map/ppermute | solution.py:478
  90.9 3.6 %collective-permute-done.10 = f32[2,192,128]{2,1,0:T(8,128)S(1)} collective-permute-done((f32[2,192,128]{2,1,0:T(8,128)S(1)}, f32[2,192,128]{2,1,0:T(8,128)S(1)}, u32[]{:S(2)}, u32[]{:S(2)}) %collective-permute-start.10) | collective-permute-done | bytes 196640 | tf_op jit(solution)/shard_map/ppermute | solution.py:478
  94.6 3.4 %collective-permute-start.11 = (f32[1,192,128]{2,1,0:T(8,128)S(1)}, f32[1,192,128]{2,1,0:T(8,128)S(1)}, u32[]{:S(2)}, u32[]{:S(2)}) collective-permute-start(f32[1,192,128]{2,1,0:T(8,128)S(1)} %get-tuple-element.55), channel_id=1, source_target_pairs={{0,4},{1,5},{2,6},{3,7},{4,0},{5,1},{6,2},{7,3},{8,12},{9,13},{10,... | collective-permute-start | bytes 294920 | tf_op jit(solution)/shard_map/ppermute | solution.py:666
  98.0 0.0 all-to-all-done
  98.0 0.0 copy-done.3
  98.0 3.5 %tendency_rows.1 = f32[1024,768]{1,0:T(8,128)} custom-call(f32[1024,512]{1,0:T(8,128)S(1)} %bitcast.13, bf16[512,768]{1,0:T(8,128)(2,1)S(1)} %copy-done.3), custom_call_target="tpu_custom_call" | custom-call | flops 1610612736 | bytes 6291456 | tf_op jit(solution)/shard_map/tendency_rows/pallas_call | solution.py:655
  101.5 0.0 collective-permute-done.11
  101.6 0.6 slice_bitcast_fusion
  (13 shorter events, 0.3 us)
Async XLA Ops:
  1.3 1.9 %copy-start = (f32[32,32,768]{2,1,0:T(8,128)S(1)}, f32[32,32,768]{2,1,0:T(8,128)}, u32[]{:S(2)}) copy-start(f32[32,32,768]{2,1,0:T(8,128)} %param.7) | copy-start | bytes 9437188
  3.2 3.5 %copy-start.1 = (f32[32,32,768]{2,1,0:T(8,128)S(1)}, f32[32,32,768]{2,1,0:T(8,128)}, u32[]{:S(2)}) copy-start(f32[32,32,768]{2,1,0:T(8,128)} %param.7) | copy-start | bytes 9437188
  4.2 9.4 %collective-permute-start = (f32[64,768]{1,0:T(8,128)}, f32[64,768]{1,0:T(8,128)S(1)}, u32[]{:S(2)}, u32[]{:S(2)}) collective-permute-start(f32[64,768]{1,0:T(8,128)} %get-tuple-element.34), channel_id=1, source_target_pairs={{0,8},{8,16},{16,24},{24,0},{1,9},{9,17},{17,25},{25,1},{2,10},{10... | collective-permute-start | bytes 589832 | tf_op jit(solution)/shard_map/ppermute | solution.py:532
  4.7 9.0 %collective-permute-start.1 = (f32[64,768]{1,0:T(8,128)}, f32[64,768]{1,0:T(8,128)S(1)}, u32[]{:S(2)}, u32[]{:S(2)}) collective-permute-start(f32[64,768]{1,0:T(8,128)} %get-tuple-element.35), channel_id=1, source_target_pairs={{0,24},{8,0},{16,8},{24,16},{1,25},{9,1},{17,9},{25,17},{2,26},{10... | collective-permute-start | bytes 589832 | tf_op jit(solution)/shard_map/ppermute | solution.py:533
  6.6 13.2 %copy-start.2 = (bf16[512,768]{1,0:T(8,128)(2,1)S(1)}, bf16[512,768]{1,0:T(8,128)(2,1)}, u32[]{:S(2)}) copy-start(bf16[512,768]{1,0:T(8,128)(2,1)} %w_out.5) | copy-start | bytes 2359300
  6.6 13.2 %copy-start.4 = (bf16[768,512]{1,0:T(8,128)(2,1)S(1)}, bf16[768,512]{1,0:T(8,128)(2,1)}, u32[]{:S(2)}) copy-start(bf16[768,512]{1,0:T(8,128)(2,1)} %in_weights.1) | copy-start | bytes 2359300
  6.6 13.2 %copy-start.5 = (s32[32,32]{1,0:T(8,128)S(1)}, s32[32,32]{1,0:T(8,128)}, u32[]{:S(2)}) copy-start(s32[32,32]{1,0:T(8,128)} %dest.3) | copy-start | bytes 12292
  6.6 13.2 %copy-start.6 = (s32[32,32]{1,0:T(8,128)S(1)}, s32[32,32]{1,0:T(8,128)}, u32[]{:S(2)}) copy-start(s32[32,32]{1,0:T(8,128)} %cost.1) | copy-start | bytes 12292
  14.1 14.2 %collective-permute-start.2 = (f32[72,768]{1,0:T(8,128)S(1)}, f32[72,768]{1,0:T(8,128)S(1)}, u32[]{:S(2)}, u32[]{:S(2)}) collective-permute-start(f32[72,768]{1,0:T(8,128)S(1)} %get-tuple-element.37), channel_id=1, source_target_pairs={{0,1},{1,2},{2,3},{3,4},{4,5},{5,6},{6,7},{7,0},{8,9},{9,10},{10,1... | collective-permute-start | bytes 663560 | tf_op jit(solution)/shard_map/ppermute | solution.py:562
  16.5 11.8 %collective-permute-start.3 = (f32[72,768]{1,0:T(8,128)S(1)}, f32[72,768]{1,0:T(8,128)S(1)}, u32[]{:S(2)}, u32[]{:S(2)}) collective-permute-start(f32[72,768]{1,0:T(8,128)S(1)} %get-tuple-element.38), channel_id=1, source_target_pairs={{0,7},{1,0},{2,1},{3,2},{4,3},{5,4},{6,5},{7,6},{8,15},{9,8},{10,9... | collective-permute-start | bytes 663560 | tf_op jit(solution)/shard_map/ppermute | solution.py:563
  36.0 62.0 %all-to-all-start = ((f32[32,32,512]{2,1,0:T(8,128)}), f32[32,32,512]{2,1,0:T(8,128)S(1)}, u32[]{:S(2)}, u32[]{:S(2)}) async-start(f32[32,32,512]{2,1,0:T(8,128)} %bitcast.14), calls=%async_computation | async-start | bytes 4194304 | tf_op jit(solution)/shard_map/all_to_all | solution.py:602
  54.4 5.3 %collective-permute-start.4 = (f32[16,96,128]{2,1,0:T(8,128)S(1)}, f32[16,96,128]{2,1,0:T(8,128)S(1)}, u32[]{:S(2)}, u32[]{:S(2)}) collective-permute-start(f32[16,96,128]{2,1,0:T(8,128)S(1)} %get-tuple-element.47), channel_id=1, source_target_pairs={{0,8},{8,0},{16,24},{24,16},{1,9},{9,1},{17,25},{25,17},{2,10},{10... | collective-permute-start | bytes 2359304 | tf_op jit(solution)/shard_map/ppermute | solution.py:478
  59.2 2.5 %collective-permute-start.7 = (f32[16,96,128]{2,1,0:T(8,128)S(1)}, f32[16,96,128]{2,1,0:T(8,128)S(1)}, u32[]{:S(2)}, u32[]{:S(2)}) collective-permute-start(f32[16,96,128]{2,1,0:T(8,128)S(1)} %get-tuple-element.51), channel_id=1, source_target_pairs={{0,8},{8,0},{16,24},{24,16},{1,9},{9,1},{17,25},{25,17},{2,10},{10... | collective-permute-start | bytes 2359304 | tf_op jit(solution)/shard_map/ppermute | solution.py:478
  59.9 15.2 %collective-permute-start.5 = (f32[8,96,128]{2,1,0:T(8,128)S(1)}, f32[8,96,128]{2,1,0:T(8,128)S(1)}, u32[]{:S(2)}, u32[]{:S(2)}) collective-permute-start(f32[8,96,128]{2,1,0:T(8,128)S(1)} %slice.65), channel_id=1, source_target_pairs={{0,16},{8,24},{16,0},{24,8},{1,17},{9,25},{17,1},{25,9},{2,18},{10... | collective-permute-start | bytes 1179656 | tf_op jit(solution)/shard_map/ppermute | solution.py:478
  61.8 36.2 %copy-start.3 = (bf16[512,768]{1,0:T(8,128)(2,1)S(1)}, bf16[512,768]{1,0:T(8,128)(2,1)}, u32[]{:S(2)}) copy-start(bf16[512,768]{1,0:T(8,128)(2,1)} %w_out.5) | copy-start | bytes 2359300
  61.8 14.5 %collective-permute-start.8 = (f32[8,96,128]{2,1,0:T(8,128)S(1)}, f32[8,96,128]{2,1,0:T(8,128)S(1)}, u32[]{:S(2)}, u32[]{:S(2)}) collective-permute-start(f32[8,96,128]{2,1,0:T(8,128)S(1)} %slice.70), channel_id=1, source_target_pairs={{0,1},{1,0},{2,3},{3,2},{4,5},{5,4},{6,7},{7,6},{8,9},{9,8},{10,11... | collective-permute-start | bytes 1179656 | tf_op jit(solution)/shard_map/ppermute | solution.py:478
  75.2 6.4 %collective-permute-start.6 = (f32[4,96,128]{2,1,0:T(8,128)S(1)}, f32[4,96,128]{2,1,0:T(8,128)S(1)}, u32[]{:S(2)}, u32[]{:S(2)}) collective-permute-start(f32[4,96,128]{2,1,0:T(8,128)S(1)} %slice.67), channel_id=1, source_target_pairs={{0,1},{1,0},{2,3},{3,2},{4,5},{5,4},{6,7},{7,6},{8,9},{9,8},{10,11... | collective-permute-start | bytes 589832 | tf_op jit(solution)/shard_map/ppermute | solution.py:478
  76.4 6.4 %collective-permute-start.9 = (f32[4,96,128]{2,1,0:T(8,128)S(1)}, f32[4,96,128]{2,1,0:T(8,128)S(1)}, u32[]{:S(2)}, u32[]{:S(2)}) collective-permute-start(f32[4,96,128]{2,1,0:T(8,128)S(1)} %slice.72), channel_id=1, source_target_pairs={{0,16},{8,24},{16,0},{24,8},{1,17},{9,25},{17,1},{25,9},{2,18},{10... | collective-permute-start | bytes 589832 | tf_op jit(solution)/shard_map/ppermute | solution.py:478
  82.9 11.6 %collective-permute-start.10 = (f32[2,192,128]{2,1,0:T(8,128)S(1)}, f32[2,192,128]{2,1,0:T(8,128)S(1)}, u32[]{:S(2)}, u32[]{:S(2)}) collective-permute-start(f32[2,192,128]{2,1,0:T(8,128)S(1)} %pad_maximum_fusion), channel_id=1, source_target_pairs={{0,2},{1,3},{2,0},{3,1},{4,6},{5,7},{6,4},{7,5},{8,10},{9,11},{10,... | collective-permute-start | bytes 589832 | tf_op jit(solution)/shard_map/ppermute | solution.py:478
  94.6 7.0 %collective-permute-start.11 = (f32[1,192,128]{2,1,0:T(8,128)S(1)}, f32[1,192,128]{2,1,0:T(8,128)S(1)}, u32[]{:S(2)}, u32[]{:S(2)}) collective-permute-start(f32[1,192,128]{2,1,0:T(8,128)S(1)} %get-tuple-element.55), channel_id=1, source_target_pairs={{0,4},{1,5},{2,6},{3,7},{4,0},{5,1},{6,2},{7,3},{8,12},{9,13},{10,... | collective-permute-start | bytes 294920 | tf_op jit(solution)/shard_map/ppermute | solution.py:666
